TPU v7x, 512 devices: a whole 4x8x8 slice. The times are simulated.
512 devices in a mesh: chan: 64 (over y_hi, z, x), hour: 8 (over y_lo, core).
Axes of the slice: x: 4, y: 8 (y_hi: 2, y_lo: 4; y = y_hi * 4 + y_lo), z: 8, core: 2. Of those that a mesh axis runs over, the one named last changes fastest.
Arguments:
- raw: float32 [8, 1536, 1024], P('hour', 'chan'), may hold values from -700 to 700
Outputs:
- stack: float32 [1024, 63, 1024], P('chan', None, 'hour')
All inputs are finite; a program needn't handle non-finite values.
Results may differ from a plain program's by a relative error of at most 0.00011.
Values sent between devices are 32-bit elements; how exact they have to be, the bound alone decides.
No kernel may reach another device: no remote copies, remote signals or barrier semaphores. Data moves between devices by JAX's collectives and lax.ppermute only.
A program may use at most 64 MiB of HBM per device.

v0:
```python
import jax
import jax.numpy as jnp
from jax import lax
from jax.sharding import PartitionSpec as P

MAXLAG = 31
HALF = 64
LAGS = 63


epsilon = 1e-06


def normalize(block):
    length = block.shape[-1]
    demeaned = block - jnp.mean(block, axis=-1, keepdims=True)
    magnitude = jnp.abs(demeaned)
    index = jnp.arange(length, dtype=jnp.int32)
    band = (jnp.abs(index[:, None] - index[None, :]) <= HALF).astype(jnp.float32)
    count = jnp.sum(band, axis=0)
    flat = magnitude.reshape(-1, length)
    running = jnp.dot(flat, band, precision=lax.Precision.HIGHEST).reshape(magnitude.shape) / count
    return demeaned / (running + epsilon)


def expand(normed):
    length = normed.shape[-1]
    widths = [(0, 0)] * (normed.ndim - 1) + [(MAXLAG, MAXLAG)]
    padded = jnp.pad(normed, widths)
    return jnp.stack(
        [padded[..., 2 * MAXLAG - j : 2 * MAXLAG - j + length] for j in range(LAGS)], axis=-2
    )


def local(raw):
    turned = lax.all_to_all(raw, "chan", split_axis=2, concat_axis=1, tiled=True)
    normed = normalize(jnp.transpose(turned, (0, 2, 1)))
    length = normed.shape[-1]
    expanded = expand(normed)
    table = jnp.einsum(
        "hpjt,hqt->pjq",
        expanded,
        lax.all_gather(normed, "chan", axis=1, tiled=True),
        precision=lax.Precision.HIGHEST,
    )
    summed = lax.psum_scatter(table, "hour", scatter_dimension=2, tiled=True)
    return summed * (1.0 / length)


def solution(mesh):
    in_specs = (P("hour", "chan", None),)
    out_specs = P("chan", None, "hour")
    return jax.shard_map(local, mesh=mesh, in_specs=in_specs, out_specs=out_specs, check_vma=False)
```

profile of v0, /device:TPU:1, one launch (start us, length us, event | category | flops | bytes accessed | tf_op | source)
XLA Modules:
  0.0 298.1 jit_solution(807043971135981947)
XLA Ops:
  6.5 1.1 copy.18
  8.2 2.0 reduce.6
  10.2 1.0 reshape.29
  11.2 19.6 %all-to-all-start = ((f32[64,1,384]{2,1,0:T(1,128)}), f32[64,1,384]{2,1,0:T(1,128)S(1)}, u32[]{:S(2)}, u32[]{:S(2)}) async-start(f32[64,1,384]{2,1,0:T(1,128)} %reshape.29), calls=%async_computation | async-start | bytes 196608 | tf_op jit(solution)/shard_map/all_to_all | solution.py:36
  31.2 13.1 %all-to-all-done = f32[64,1,384]{2,1,0:T(1,128)S(1)} async-done(((f32[64,1,384]{2,1,0:T(1,128)}), f32[64,1,384]{2,1,0:T(1,128)S(1)}, u32[]{:S(2)}, u32[]{:S(2)}) %all-to-all-start) | async-done | bytes 98336 | tf_op jit(solution)/shard_map/all_to_all | solution.py:36
  44.4 0.9 reduce.7
  45.3 0.9 reshape.30
  46.2 1.8 bitcast_reduce_fusion
  49.7 1.1 fusion.8
  51.9 1.6 constant_dynamic-update-slice_fusion.61
  53.5 1.6 constant_dynamic-update-slice_fusion.60
  55.2 1.6 constant_dynamic-update-slice_fusion.59
  56.8 1.6 constant_dynamic-update-slice_fusion.58
  58.4 1.6 constant_dynamic-update-slice_fusion.57
  60.0 1.6 constant_dynamic-update-slice_fusion.56
  61.6 1.6 constant_dynamic-update-slice_fusion.55
  63.3 1.6 constant_dynamic-update-slice_fusion.54
  64.9 1.6 constant_dynamic-update-slice_fusion.53
  66.5 1.6 constant_dynamic-update-slice_fusion.52
  68.1 1.6 constant_dynamic-update-slice_fusion.51
  69.7 1.6 constant_dynamic-update-slice_fusion.50
  71.4 1.6 constant_dynamic-update-slice_fusion.49
  73.0 1.6 constant_dynamic-update-slice_fusion.48
  74.6 1.6 constant_dynamic-update-slice_fusion.47
  76.2 1.6 constant_dynamic-update-slice_fusion.46
  77.8 1.6 constant_dynamic-update-slice_fusion.45
  79.5 1.6 constant_dynamic-update-slice_fusion.44
  81.1 1.6 constant_dynamic-update-slice_fusion.43
  82.7 1.6 constant_dynamic-update-slice_fusion.42
  84.3 1.6 constant_dynamic-update-slice_fusion.41
  86.0 1.6 constant_dynamic-update-slice_fusion.40
  87.6 1.6 constant_dynamic-update-slice_fusion.39
  89.2 1.6 constant_dynamic-update-slice_fusion.38
  90.8 1.6 constant_dynamic-update-slice_fusion.37
  92.5 1.6 constant_dynamic-update-slice_fusion.36
  94.1 1.6 constant_dynamic-update-slice_fusion.35
  95.7 1.6 constant_dynamic-update-slice_fusion.34
  97.3 1.6 constant_dynamic-update-slice_fusion.33
  98.9 1.6 constant_dynamic-update-slice_fusion.32
  100.6 1.5 constant_dynamic-update-slice_fusion.31
  102.1 1.6 constant_dynamic-update-slice_fusion.30
  103.7 0.7 constant_dynamic-update-slice_fusion.29
  105.2 0.7 constant_dynamic-update-slice_fusion.27
  105.9 0.7 constant_dynamic-update-slice_fusion.26
  106.7 0.7 constant_dynamic-update-slice_fusion.25
  108.1 0.7 constant_dynamic-update-slice_fusion.23
  108.8 0.7 constant_dynamic-update-slice_fusion.22
  109.6 0.7 constant_dynamic-update-slice_fusion.21
  111.0 0.7 constant_dynamic-update-slice_fusion.19
  111.8 0.7 constant_dynamic-update-slice_fusion.18
  112.5 0.7 constant_dynamic-update-slice_fusion.17
  113.2 0.7 constant_dynamic-update-slice_fusion.16
  113.9 0.7 constant_dynamic-update-slice_fusion.15
  115.4 0.7 constant_dynamic-update-slice_fusion.13
  117.6 0.7 constant_dynamic-update-slice_fusion.10
  119.0 0.7 constant_dynamic-update-slice_fusion.8
  119.8 0.7 constant_dynamic-update-slice_fusion.7
  121.2 0.7 constant_dynamic-update-slice_fusion.5
  123.4 0.7 constant_dynamic-update-slice_fusion.2
  124.1 0.7 constant_dynamic-update-slice_fusion.1
  125.6 85.0 %all-gather.2.cloned.1.call-done = f32[1,1024,1536]{2,1,0:T(8,128)} async-done(((f32[1,16,1536]{2,1,0:T(8,128)}), f32[1,1024,1536]{2,1,0:T(8,128)}) %all-gather.2.cloned.1.call-update) | async-done | bytes 6291472 | tf_op jit(solution)/shard_map/all_gather | solution.py:43
  210.5 24.3 %fusion.1 = f32[16,63,1024]{2,0,1:T(8,128)} fusion(f32[1,1024,1536]{2,1,0:T(8,128)} %all-gather.2.cloned.1.call-done, f32[1,16,63,1536]{3,1,2,0:T(8,128)} %constant_dynamic-update-slice_fusion), kind=kOutput, calls=%fused_computation.3 | convolution fusion | flops 19025362944 | bytes 16613376 | tf_op jit(solution)/shard_map/hpjt,hqt->pjq/dot_general | solution.py:40
  234.8 54.5 %reduce-scatter.2.cloned.1.call-done = f32[16,63,128]{2,0,1:T(8,128)} async-done(((f32[16,63,1024]{2,0,1:T(8,128)}), f32[16,63,128]{2,0,1:T(8,128)}) %reduce-scatter.2.cloned.1.call-update) | async-done | bytes 516112 | tf_op jit(solution)/shard_map/reduce_scatter | solution.py:46
  289.4 1.9 broadcast_multiply_fusion
  (28 shorter events, 11.7 us)
Async XLA Ops:
  11.2 33.1 %all-to-all-start = ((f32[64,1,384]{2,1,0:T(1,128)}), f32[64,1,384]{2,1,0:T(1,128)S(1)}, u32[]{:S(2)}, u32[]{:S(2)}) async-start(f32[64,1,384]{2,1,0:T(1,128)} %reshape.29), calls=%async_computation | async-start | bytes 196608 | tf_op jit(solution)/shard_map/all_to_all | solution.py:36
  30.8 179.7 %all-gather.2.cloned.1.call-start = ((), (), s32[]{:S(2)}) async-start(), calls=%async_computation.2 | async-start | bytes 6389760 | tf_op jit(solution)/shard_map/all_gather | solution.py:43
  50.9 0.7 copy-start
  51.7 52.1 %copy-start.1 = (f32[1,16,1536]{2,1,0:T(8,128)S(1)}, f32[1,16,1536]{2,1,0:T(8,128)}, u32[]{:S(2)}) copy-start(f32[1,16,1536]{2,1,0:T(8,128)} %copy-done) | copy-start | bytes 294916
  51.7 237.7 %reduce-scatter.2.cloned.1.call-start = ((), (), s32[]{:S(2)}) async-start(), calls=%async_computation.3 | async-start | bytes 4644864 | tf_op jit(solution)/shard_map/reduce_scatter | solution.py:46
Sparse Core Ops, SparseCore 0:
  51.8 158.7 all-gather.1
  235.0 54.3 reduce-scatter.1
where the time goes:
time: 301 us; the launch traced here: 298 us
  waiting for transfers between devices  153 us (51%)
  local copies, waits for them, and re-layouts  79.7 us (26%)
  matrix products  25.4 us (8%)
  starting transfers between devices  19.9 us (7%)
  between operations  13.5 us (4%)
  other arithmetic  6.95 us (2%)
    all_gather x1, waiting for transfers between devices, local(): lax.all_gather(normed, 'chan', axis=1, tiled=True)  85 us
    unnamed x70, local copies, waits for them, and re-layouts  77.2 us
    reduce_scatter x1, waiting for transfers between devices, local(): summed = lax.psum_scatter(table, 'hour', scatter_dimension=2, tiled=True)  54.5 us
    dot_general x1, matrix products, local(): jnp.einsum('hpjt,hqt->pjq', expanded, lax.all_gather(normed, 'chan', axis...  24.3 us
    all_to_all x1, starting transfers between devices, local(): lax.all_to_all(raw, 'chan', split_axis=2, concat_axis=1, tiled=True)  19.6 us
    all_to_all x1, waiting for transfers between devices, local(): lax.all_to_all(raw, 'chan', split_axis=2, concat_axis=1, tiled=True)  13.1 us
  transfers between devices with their start and end apart: 3, of which 3 were waited for; matrix products, arithmetic and copies ran while one was open for 25% of the time, Pallas kernels for 0%

commit v1 on v0

v1 whole, which is shorter than its diff:
```python
import jax
import jax.numpy as jnp
from jax import lax
from jax.experimental import pallas as pl
from jax.experimental.pallas import tpu as pltpu
from jax.sharding import Mesh, PartitionSpec as P

C = 1024
MAXLAG = 31
HALF = 64
LAGS = 63
SAMPLES = 1536
epsilon = 1e-06

TAU = 24
ROW = SAMPLES + 32
K = 6400
FRONT = 40
QFRONT = FRONT - 24
SEQ = K + 128
CHUNK = 1280
ROT = (4, 8, 36, 40)
VMEM = pl.BlockSpec(memory_space=pltpu.VMEM)
SMEM = pl.BlockSpec(memory_space=pltpu.SMEM)
BIG = 56 * 1024 * 1024


def lanes(shape):
    return lax.broadcasted_iota(jnp.int32, shape, len(shape) - 1)


def prepack(raw, out):
    lane = lanes((TAU, 128))
    for low in range(4):
        a = raw[:, 256 * low : 256 * low + 128]
        b = raw[:, 256 * low + 128 : 256 * low + 256]
        first = jnp.where(
            lane < 32, a, jnp.where(lane < 64, pltpu.roll(b, 32, 1), jnp.where(lane < 96, pltpu.roll(a, 32, 1), pltpu.roll(b, 64, 1)))
        )
        second = jnp.where(
            lane < 32, pltpu.roll(a, 64, 1), jnp.where(lane < 64, pltpu.roll(b, 96, 1), jnp.where(lane < 96, pltpu.roll(a, 96, 1), b))
        )
        for high in range(2):
            out[4 * high + low, :, 512:640] = first
            out[4 * high + low, :, 640:768] = second
            out[4 * high + low, :, 0:512] = raw[:, 512 * high : 512 * high + 512]


def repack(got, p_out, q_out):
    low = lanes((TAU, 128)) < 64
    for high in range(2):
        for pair in range(2):
            one, two = 4 * high + 2 * pair, 4 * high + 2 * pair + 1
            for v in range(6):
                a = got[one, :, 128 * v : 128 * v + 128]
                b = got[two, :, 128 * v : 128 * v + 128]
                even = jnp.where(low, a, pltpu.roll(b, 64, 1))
                odd = jnp.where(low, pltpu.roll(a, 64, 1), b)
                if v < 4:
                    p_out[2 * v, high, pair] = even
                    p_out[2 * v + 1, high, pair] = odd
                else:
                    q_out[2 * (v - 4), high, pair] = even
                    q_out[2 * (v - 4) + 1, high, pair] = odd


def split(x):
    hi = x.astype(jnp.bfloat16)
    return hi, (x - hi.astype(jnp.float32)).astype(jnp.bfloat16)


def normalize(rec, mag):
    row = lax.broadcasted_iota(jnp.int32, (128, 256), 0)
    col = lanes((128, 256))
    band = jnp.where((col >= row) & (col <= row + 2 * HALF), 1.0, 0.0).astype(jnp.bfloat16)
    zero = jnp.zeros((HALF, 256), jnp.bfloat16)
    mag[0:HALF, :] = zero
    mag[HALF + SAMPLES : 2 * HALF + SAMPLES, :] = zero
    for pair in range(2):
        mean = jnp.sum(rec[pair], axis=0, keepdims=True) * (1.0 / SAMPLES)
        for i in range(12):
            d = rec[pair, 128 * i : 128 * i + 128, :] - mean
            rec[pair, 128 * i : 128 * i + 128, :] = d
            hi, lo = split(jnp.abs(d))
            mag[HALF + 128 * i : HALF + 128 * i + 128, 0:128] = hi
            mag[HALF + 128 * i : HALF + 128 * i + 128, 128:256] = lo
        for i in range(12):
            both = jnp.dot(band, mag[128 * i : 128 * i + 256, :], preferred_element_type=jnp.float32)
            t = lax.broadcasted_iota(jnp.int32, (128, 128), 0) + 128 * i
            count = (jnp.minimum(t, HALF) + jnp.minimum(SAMPLES - 1 - t, HALF) + 1).astype(jnp.float32)
            running = (both[:, 0:128] + both[:, 128:256]) / count
            rec[pair, 128 * i : 128 * i + 128, :] = rec[pair, 128 * i : 128 * i + 128, :] / (running + epsilon)


def p_kernel(me, p0, p1, p2, p3, hi_out, lo_out, rec, mag, seq, turned):
    for d, ref in enumerate((p0, p1, p2, p3)):
        x = lax.rem(me[0] + 4 - d, 4)
        for high in range(2):
            for z in range(8):
                at = pl.multiple_of(((high * 8 + z) * 4) * TAU + x * TAU, 8)
                for pair in range(2):
                    rec[pair, pl.ds(at, TAU), :] = ref[z, high, pair]
    normalize(rec, mag)
    seq[...] = jnp.zeros_like(seq)
    for pair in range(2):
        for i in range(12):
            x = rec[pair, 128 * i : 128 * i + 128, :]
            r = pltpu.roll(x, 64, 1)
            at = FRONT + 2 * pair * ROW + 128 * i
            seq[at : at + 128, 0:64] = x[:, 0:64]
            seq[at - 16 : at + 112, 64:128] = r[:, 64:128]
            at += ROW
            seq[at : at + 128, 0:64] = r[:, 0:64]
            seq[at - 16 : at + 112, 64:128] = x[:, 64:128]
    for i in range(SEQ // 128):
        turned[:, 128 * i : 128 * i + 128] = seq[128 * i : 128 * i + 128, :].T
    for n, rot in enumerate(ROT):
        for m in range(8):
            x = turned[16 * m : 16 * m + 16, :]
            if rot:
                x = pltpu.roll(x, SEQ - rot, 1)
            hi, lo = split(x[:, 0:K])
            hi_out[128 * n + 16 * m : 128 * n + 16 * m + 16, :] = hi
            lo_out[128 * n + 16 * m : 128 * n + 16 * m + 16, :] = lo


def main_kernel(me, q_in, lhs_hi, lhs_lo, out, rec, mag, seq, rhs_hi, rhs_lo, acc):
    for d in range(4):
        x = lax.rem(me[0] + 4 - d, 4)
        for high in range(2):
            for z in range(8):
                at = pl.multiple_of(((high * 8 + z) * 4) * TAU + x * TAU, 8)
                for pair in range(2):
                    rec[pair, pl.ds(at, TAU), :] = q_in[z, d, high, pair]
    normalize(rec, mag)
    seq[...] = jnp.zeros_like(seq)
    for pair in range(2):
        for i in range(12):
            x = rec[pair, 128 * i : 128 * i + 128, :]
            r32, r64, r96 = (pltpu.roll(x, n, 1) for n in (32, 64, 96))
            at = QFRONT + 2 * pair * ROW + 128 * i
            for e, parts in enumerate(((x, r32, r32, r64), (r64, r96, r96, x))):
                for n, part in enumerate(parts):
                    to = at + e * ROW - 8 * (n % 2)
                    seq[to : to + 128, 32 * n : 32 * n + 32] = part[:, 32 * n : 32 * n + 32]
    for k in range(K // CHUNK):
        for s in range(4):
            for m in range(CHUNK // 128):
                at = CHUNK * k + 128 * m
                hi, lo = split(seq[at + s : at + s + 128, :])
                rhs_hi[at : at + 128, 128 * s : 128 * s + 128] = hi
                rhs_lo[at : at + 128, 128 * s : 128 * s + 128] = lo
        span = slice(CHUNK * k, CHUNK * k + CHUNK)
        part = jnp.dot(lhs_hi[:, span], rhs_hi[span, :], preferred_element_type=jnp.float32)
        part += jnp.dot(lhs_hi[:, span], rhs_lo[span, :], preferred_element_type=jnp.float32)
        part += jnp.dot(lhs_lo[:, span], rhs_hi[span, :], preferred_element_type=jnp.float32)
        if k == 0:
            acc[...] = part
        else:
            acc[...] += part
    low = lanes((16, 128)) < 64
    for g in range(8):
        for x in range(4):
            at = 64 * g + 16 * x
            for s2 in range(2):
                a = acc[at : at + 16, 256 * s2 : 256 * s2 + 128]
                b = acc[at : at + 16, 256 * s2 + 128 : 256 * s2 + 256]
                out[0, x, g, s2] = jnp.where(low, a, pltpu.roll(b, 64, 1))
                out[1, x, g, s2] = jnp.where(low, pltpu.roll(a, 64, 1), b)


def final_kernel(got, out):
    lane = lanes((16, 128))
    for g in range(8):
        r, j = g // 2, g % 2
        r0, r1 = r % 2, r // 2
        for s2 in range(2):
            parts = [got[x, g, s2] for x in range(4)]
            for sb in range(2):
                for i in range(2):
                    mu = 2 * s2 + sb + 4 * (1 - r0) + 8 * i + 16 * (1 - j) + 32 * (1 - r1)
                    if mu == 0:
                        continue
                    n = 2 * sb + i
                    moved = [pltpu.roll(parts[x], (32 * (x - n)) % 128, 1) if x != n else parts[x] for x in range(4)]
                    value = jnp.where(lane < 32, moved[0], jnp.where(lane < 64, moved[1], jnp.where(lane < 96, moved[2], moved[3])))
                    out[:, mu - 1, :] = value * (1.0 / SAMPLES)


def sds(*shape, dtype=jnp.float32):
    return jax.ShapeDtypeStruct(shape, dtype)


def around(v, d):
    return lax.ppermute(v, "x", [(i, (i + d) % 4) for i in range(4)])


def local(raw):
    x = lax.axis_index("x")
    me = x.reshape(1).astype(jnp.int32)
    sent = pl.pallas_call(prepack, out_shape=sds(8, TAU, 768), in_specs=[VMEM], out_specs=VMEM, name="prepack")(raw[0])
    got = lax.all_to_all(sent, ("yh", "yl"), 0, 0, tiled=True)
    p_send, q_send = pl.pallas_call(
        repack, out_shape=(sds(8, 2, 2, TAU, 128), sds(4, 2, 2, TAU, 128)), in_specs=[VMEM], out_specs=(VMEM, VMEM), name="repack"
    )(got)
    p_mine = lax.all_to_all(p_send, "z", 0, 0, tiled=True)
    picked = [lax.dynamic_index_in_dim(q_send, lax.rem(x + d, 4), 0, keepdims=False) for d in range(4)]
    q_mine = jnp.stack([picked[0]] + [around(picked[d], d) for d in (1, 2, 3)])
    q_all = lax.all_to_all(jnp.broadcast_to(q_mine[None], (8,) + q_mine.shape), "z", 0, 0, tiled=True)
    p_all = [p_mine] + [around(p_mine, d) for d in (1, 2, 3)]
    lhs_hi, lhs_lo = pl.pallas_call(
        p_kernel,
        out_shape=(sds(512, K, dtype=jnp.bfloat16), sds(512, K, dtype=jnp.bfloat16)),
        in_specs=[SMEM] + [VMEM] * 4,
        out_specs=(VMEM, VMEM),
        scratch_shapes=[
            pltpu.VMEM((2, SAMPLES, 128), jnp.float32),
            pltpu.VMEM((SAMPLES + 2 * HALF, 256), jnp.bfloat16),
            pltpu.VMEM((SEQ, 128), jnp.float32),
            pltpu.VMEM((128, SEQ), jnp.float32),
        ],
        compiler_params=pltpu.CompilerParams(vmem_limit_bytes=BIG),
        cost_estimate=pl.CostEstimate(flops=10**9, bytes_accessed=20 * 10**6, transcendentals=0),
        name="p_side",
    )(me, *p_all)
    part = pl.pallas_call(
        main_kernel,
        out_shape=sds(2, 4, 8, 2, 16, 128),
        in_specs=[SMEM] + [VMEM] * 3,
        out_specs=VMEM,
        scratch_shapes=[
            pltpu.VMEM((2, SAMPLES, 128), jnp.float32),
            pltpu.VMEM((SAMPLES + 2 * HALF, 256), jnp.bfloat16),
            pltpu.VMEM((SEQ, 128), jnp.float32),
            pltpu.VMEM((K, 512), jnp.bfloat16),
            pltpu.VMEM((K, 512), jnp.bfloat16),
            pltpu.VMEM((512, 512), jnp.float32),
        ],
        compiler_params=pltpu.CompilerParams(vmem_limit_bytes=BIG),
        cost_estimate=pl.CostEstimate(flops=10**10, bytes_accessed=20 * 10**6, transcendentals=0),
        name="correlate",
    )(me, q_all, lhs_hi, lhs_lo)
    both = lax.all_to_all(part, "core", 0, 0, tiled=True)
    summed = both[0] + both[1]
    mine = lax.all_to_all(summed, "x", 0, 0, tiled=True)
    return pl.pallas_call(final_kernel, out_shape=sds(16, LAGS, 128), in_specs=[VMEM], out_specs=VMEM, name="finish")(mine)


def solution(mesh):
    grid = Mesh(mesh.devices.reshape(2, 8, 4, 4, 2), ("yh", "z", "x", "yl", "core"))
    in_specs = (P(("yl", "core"), ("yh", "z", "x"), None),)
    out_specs = P(("yh", "z", "x"), None, ("yl", "core"))
    return jax.shard_map(local, mesh=grid, in_specs=in_specs, out_specs=out_specs, check_vma=False)
```

time: 301 us -> 147 us (0.49)
  waiting for transfers between devices: 153 us -> 20 us
  local copies, waits for them, and re-layouts: 79.7 us -> 6.23 us
  blocking collectives: 0 us -> 43.4 us
  Pallas kernels: 0 us -> 39.2 us
  matrix products: 25.4 us -> 0 us
  starting transfers between devices: 19.9 us -> 36.8 us
  between operations: 13.5 us -> 0.1 us
  other arithmetic: 6.95 us -> 0.09 us
    all_gather x1 -> x0, waiting for transfers between devices: 85 us -> none  [local(): lax.all_gather(normed, 'chan', axis=1, tiled=True)]
    unnamed x70 -> x10, local copies, waits for them, and re-layouts: 77.2 us -> 1.89 us
    reduce_scatter x1 -> x0, waiting for transfers between devices: 54.5 us -> none  [local(): summed = lax.psum_scatter(table, 'hour', scatter_dimension=2, tiled=True)]
    all_to_all x0 -> x3, blocking collectives: none -> 43.4 us  [the longest x1 21.9 us: local(): got = lax.all_to_all(sent, ('yh', 'yl'), 0, 0, tiled=True)]
    pallas_call x0 -> x5, Pallas kernels: none -> 39.2 us  [the longest x1 20.4 us: local(): pl.pallas_call(main_kernel, out_shape=sds(2, 4, 8, 2, 16, 128), in_specs=...]
    dot_general x2 -> x0, matrix products: 25.4 us -> none  [the longest x1 24.3 us: local(): jnp.einsum('hpjt,hqt->pjq', expanded, lax.all_gather(normed, 'chan', axis...]
    ppermute x0 -> x6, waiting for transfers between devices: none -> 17.9 us  [around(): return lax.ppermute(v, 'x', [(i, (i + d) % 4) for i in range(4)])]
    ppermute x0 -> x6, starting transfers between devices: none -> 17.1 us  [around(): return lax.ppermute(v, 'x', [(i, (i + d) % 4) for i in range(4)])]
  transfers between devices with their start and end apart: 3 -> 8, of which waited for: 3 -> 6; matrix products, arithmetic and copies ran while one was open for 25% -> 1% of each run, Pallas kernels for 0% -> 8%
where the time goes in v1:
time: 147 us; the launch traced here: 146 us
  blocking collectives  43.4 us (30%)
  Pallas kernels  39.2 us (27%)
  starting transfers between devices  36.8 us (25%)
  waiting for transfers between devices  20 us (14%)
  local copies, waits for them, and re-layouts  6.23 us (4%)
    all_to_all x1, blocking collectives, local(): got = lax.all_to_all(sent, ('yh', 'yl'), 0, 0, tiled=True)  21.9 us
    pallas_call x1, Pallas kernels, local(): pl.pallas_call(main_kernel, out_shape=sds(2, 4, 8, 2, 16, 128), in_specs=...  20.4 us
    ppermute x6, waiting for transfers between devices, around(): return lax.ppermute(v, 'x', [(i, (i + d) % 4) for i in range(4)])  17.9 us
    ppermute x6, starting transfers between devices, around(): return lax.ppermute(v, 'x', [(i, (i + d) % 4) for i in range(4)])  17.1 us
    all_to_all x1, starting transfers between devices, local(): p_mine = lax.all_to_all(p_send, 'z', 0, 0, tiled=True)  13.3 us
    all_to_all x1, blocking collectives, local(): mine = lax.all_to_all(summed, 'x', 0, 0, tiled=True)  12.3 us
    pallas_call x1, Pallas kernels, local(): pl.pallas_call(p_kernel, out_shape=(sds(512, K, dtype=jnp.bfloat16), sds(...  12.3 us
    all_to_all x1, blocking collectives, local(): both = lax.all_to_all(part, 'core', 0, 0, tiled=True)  9.14 us
  transfers between devices with their start and end apart: 8, of which 6 were waited for; matrix products, arithmetic and copies ran while one was open for 1% of the time, Pallas kernels for 8%

profile of v1, /device:TPU:1, one launch (start us, length us, event | category | flops | bytes accessed | tf_op | source)
XLA Modules:
  0.0 145.8 jit_solution(9348963569585842426)
XLA Ops:
  0.0 1.9 %prepack.1 = f32[8,24,768]{2,1,0:T(8,128)} custom-call(f32[24,1024]{1,0:T(8,128)} %bitcast.13), custom_call_target="tpu_custom_call" | custom-call | tf_op jit(solution)/shard_map/prepack/pallas_call | solution.py:201
  1.9 21.9 %all_to_all.25.got = f32[8,24,768]{2,1,0:T(8,128)} all-to-all(f32[8,24,768]{2,1,0:T(8,128)} %prepack.1), channel_id=1, replica_groups=mesh['yh'=2,'z'=8,'x'=4,'yl'=4,'core'=2] {'yh','yl'}, dimensions={0} | all-to-all | bytes 1179648 | tf_op jit(solution)/shard_map/all_to_all | solution.py:202
  23.8 2.1 %repack.1 = (f32[8,2,2,24,128]{4,3,2,1,0:T(8,128)}, f32[4,2,2,24,128]{4,3,2,1,0:T(8,128)}) custom-call(f32[8,24,768]{2,1,0:T(8,128)} %all_to_all.25.got), custom_call_target="tpu_custom_call" | custom-call | tf_op jit(solution)/shard_map/repack/pallas_call | solution.py:203
  25.9 13.3 %all-to-all-start.2 = ((f32[8,2,2,24,128]{4,3,2,1,0:T(8,128)}), f32[8,2,2,24,128]{4,3,2,1,0:T(8,128)S(1)}, u32[]{:S(2)}, u32[]{:S(2)}) async-start(f32[8,2,2,24,128]{4,3,2,1,0:T(8,128)} %get-tuple-element.10), calls=%async_computation.2 | async-start | bytes 786432 | tf_op jit(solution)/shard_map/all_to_all | solution.py:206
  39.2 0.9 constant_dynamic-slice_fusion
  40.0 4.4 %collective-permute-start.2 = (f32[2,2,24,128]{3,2,1,0:T(8,128)S(1)}, f32[2,2,24,128]{3,2,1,0:T(8,128)S(1)}, u32[]{:S(2)}, u32[]{:S(2)}) collective-permute-start(f32[2,2,24,128]{3,2,1,0:T(8,128)S(1)} %get-tuple-element.14), channel_id=1, source_target_pairs={{0,24},{8,0},{16,8},{24,16},{1,25},{9,1},{17,9},{25,17},{2,26},{10... | collective-permute-start | bytes 147464 | tf_op jit(solution)/shard_map/ppermute | solution.py:195
  44.4 2.4 %collective-permute-start.1 = (f32[2,2,24,128]{3,2,1,0:T(8,128)S(1)}, f32[2,2,24,128]{3,2,1,0:T(8,128)S(1)}, u32[]{:S(2)}, u32[]{:S(2)}) collective-permute-start(f32[2,2,24,128]{3,2,1,0:T(8,128)S(1)} %get-tuple-element.15), channel_id=1, source_target_pairs={{0,16},{8,24},{16,0},{24,8},{1,17},{9,25},{17,1},{25,9},{2,18},{10... | collective-permute-start | bytes 147464 | tf_op jit(solution)/shard_map/ppermute | solution.py:195
  46.9 2.5 %collective-permute-start = (f32[2,2,24,128]{3,2,1,0:T(8,128)S(1)}, f32[2,2,24,128]{3,2,1,0:T(8,128)S(1)}, u32[]{:S(2)}, u32[]{:S(2)}) collective-permute-start(f32[2,2,24,128]{3,2,1,0:T(8,128)S(1)} %get-tuple-element.16), channel_id=1, source_target_pairs={{0,8},{8,16},{16,24},{24,0},{1,9},{9,17},{17,25},{25,1},{2,10},{10... | collective-permute-start | bytes 147464 | tf_op jit(solution)/shard_map/ppermute | solution.py:195
  49.4 0.0 collective-permute-done.2
  49.4 1.4 collective-permute-done.1
  50.8 2.4 %collective-permute-done = f32[2,2,24,128]{3,2,1,0:T(8,128)S(1)} collective-permute-done((f32[2,2,24,128]{3,2,1,0:T(8,128)S(1)}, f32[2,2,24,128]{3,2,1,0:T(8,128)S(1)}, u32[]{:S(2)}, u32[]{:S(2)}) %collective-permute-start) | collective-permute-done | bytes 49184 | tf_op jit(solution)/shard_map/ppermute | solution.py:195
  53.2 0.0 all-to-all-done.2.p0
  53.2 0.0 copy-start.1
  53.3 1.3 broadcast_in_dim.2
  54.6 6.4 %all-to-all-start.1 = ((f32[8,4,2,2,24,128]{5,4,3,2,1,0:T(8,128)}), f32[8,4,2,2,24,128]{5,4,3,2,1,0:T(8,128)S(1)}, u32[]{:S(2)}, u32[]{:S(2)}) async-start(f32[8,4,2,2,24,128]{5,4,3,2,1,0:T(8,128)} %broadcast_in_dim.2), calls=%async_computation.1 | async-start | bytes 3145728 | tf_op jit(solution)/shard_map/all_to_all | solution.py:209
  60.9 2.0 %collective-permute-start.5 = (f32[8,2,2,24,128]{4,3,2,1,0:T(8,128)S(1)}, f32[8,2,2,24,128]{4,3,2,1,0:T(8,128)S(1)}, u32[]{:S(2)}, u32[]{:S(2)}) collective-permute-start(f32[8,2,2,24,128]{4,3,2,1,0:T(8,128)S(1)} %all-to-all-done.2.p0), channel_id=1, source_target_pairs={{0,24},{8,0},{16,8},{24,16},{1,25},{9,1},{17,9},{25,17},{2,26},{10... | collective-permute-start | bytes 1179656 | tf_op jit(solution)/shard_map/ppermute | solution.py:195
  62.9 3.1 %collective-permute-start.4 = (f32[8,2,2,24,128]{4,3,2,1,0:T(8,128)S(1)}, f32[8,2,2,24,128]{4,3,2,1,0:T(8,128)S(1)}, u32[]{:S(2)}, u32[]{:S(2)}) collective-permute-start(f32[8,2,2,24,128]{4,3,2,1,0:T(8,128)S(1)} %all-to-all-done.2.p0), channel_id=1, source_target_pairs={{0,16},{8,24},{16,0},{24,8},{1,17},{9,25},{17,1},{25,9},{2,18},{10... | collective-permute-start | bytes 1179656 | tf_op jit(solution)/shard_map/ppermute | solution.py:195
  66.0 2.8 %collective-permute-start.3 = (f32[8,2,2,24,128]{4,3,2,1,0:T(8,128)S(1)}, f32[8,2,2,24,128]{4,3,2,1,0:T(8,128)S(1)}, u32[]{:S(2)}, u32[]{:S(2)}) collective-permute-start(f32[8,2,2,24,128]{4,3,2,1,0:T(8,128)S(1)} %all-to-all-done.2.p0), channel_id=1, source_target_pairs={{0,8},{8,16},{16,24},{24,0},{1,9},{9,17},{17,25},{25,1},{2,10},{10... | collective-permute-start | bytes 1179656 | tf_op jit(solution)/shard_map/ppermute | solution.py:195
  68.8 1.0 collective-permute-done.5.p3
  69.7 0.0 copy-start.2
  69.7 3.5 %collective-permute-done.4.p2 = f32[8,2,2,24,128]{4,3,2,1,0:T(8,128)S(1)} collective-permute-done((f32[8,2,2,24,128]{4,3,2,1,0:T(8,128)S(1)}, f32[8,2,2,24,128]{4,3,2,1,0:T(8,128)S(1)}, u32[]{:S(2)}, u32[]{:S(2)}) %collective-permute-start.4) | collective-permute-done | bytes 393248 | tf_op jit(solution)/shard_map/ppermute | solution.py:195
  73.2 0.0 copy-start.3
  73.2 9.7 %collective-permute-done.3.p1 = f32[8,2,2,24,128]{4,3,2,1,0:T(8,128)S(1)} collective-permute-done((f32[8,2,2,24,128]{4,3,2,1,0:T(8,128)S(1)}, f32[8,2,2,24,128]{4,3,2,1,0:T(8,128)S(1)}, u32[]{:S(2)}, u32[]{:S(2)}) %collective-permute-start.3) | collective-permute-done | bytes 393248 | tf_op jit(solution)/shard_map/ppermute | solution.py:195
  82.9 0.0 copy-start.4
  82.9 0.0 copy-done.1
  82.9 0.0 copy-done.2
  82.9 0.0 copy-done.3
  82.9 0.7 copy-done.4
  83.6 12.3 %p_side.1 = (bf16[512,6400]{1,0:T(8,128)(2,1)}, bf16[512,6400]{1,0:T(8,128)(2,1)}) custom-call(s32[1]{0:T(128)} %bitcast.me, f32[8,2,2,24,128]{4,3,2,1,0:T(8,128)} %copy-done.1, f32[8,2,2,24,128]{4,3,2,1,0:T(8,128)} %copy-done.4, f32[8,2,2,24,128]{4,3,2,1,0:T(8,128)} %copy-done.3, f32[8,2,2,24,128]{4,3,2,1,0:T(8,128)} %copy-done.2), custom_call_target="tpu_custom_call" | custom-call | flops 1000000000 | bytes 20000000 | tf_op jit(solution)/shard_map/p_side/pallas_call | solution.py:211
  96.0 2.1 %all-to-all-done.1.q_in = f32[8,4,2,2,24,128]{5,4,3,2,1,0:T(8,128)S(1)} async-done(((f32[8,4,2,2,24,128]{5,4,3,2,1,0:T(8,128)}), f32[8,4,2,2,24,128]{5,4,3,2,1,0:T(8,128)S(1)}, u32[]{:S(2)}, u32[]{:S(2)}) %all-to-all-start.1) | async-done | bytes 1572896 | tf_op jit(solution)/shard_map/all_to_all | solution.py:209
  98.1 0.0 copy-start
  98.1 1.1 copy-done
  99.2 20.4 %correlate.1 = f32[2,4,8,2,16,128]{5,4,3,2,1,0:T(8,128)} custom-call(s32[1]{0:T(128)} %bitcast.me, f32[8,4,2,2,24,128]{5,4,3,2,1,0:T(8,128)} %copy-done, bf16[512,6400]{1,0:T(8,128)(2,1)} %get-tuple-element.11.lhs_hi, bf16[512,6400]{1,0:T(8,128)(2,1)} %get-tuple-element.12.lhs_lo), custom_call_target="tpu_custom_call" | custom-call | flops 10000000000 | bytes 20000000 | tf_op jit(solution)/shard_map/correlate/pallas_call | solution.py:226
  119.7 9.1 %all_to_all.26 = f32[2,4,8,2,16,128]{5,4,3,2,1,0:T(8,128)S(1)} all-to-all(f32[2,4,8,2,16,128]{5,4,3,2,1,0:T(8,128)} %correlate.1), channel_id=1, replica_groups=mesh['yh'=2,'z'=8,'x'=4,'yl'=4,'core'=2] {'core'}, dimensions={0} | all-to-all | bytes 2097152 | tf_op jit(solution)/shard_map/all_to_all | solution.py:243
  128.8 0.1 fusion
  128.9 12.3 %all_to_all.27.got = f32[4,8,2,16,128]{4,3,2,1,0:T(8,128)} all-to-all(f32[4,8,2,16,128]{4,3,2,1,0:T(8,128)S(1)} %fusion), channel_id=1, replica_groups=mesh['yh'=2,'z'=8,'x'=4,'yl'=4,'core'=2] {'x'}, dimensions={0} | all-to-all | bytes 1048576 | tf_op jit(solution)/shard_map/all_to_all | solution.py:245
  141.2 2.5 %finish.1 = f32[16,63,128]{2,1,0:T(8,128)} custom-call(f32[4,8,2,16,128]{4,3,2,1,0:T(8,128)} %all_to_all.27.got), custom_call_target="tpu_custom_call" | custom-call | tf_op jit(solution)/shard_map/finish/pallas_call | solution.py:246
  143.7 2.1 %copy.2 = f32[16,63,128]{2,0,1:T(8,128)} copy(f32[16,63,128]{2,1,0:T(8,128)} %finish.1) | data formatting | bytes 1032192 | tf_op jit(solution)/shard_map/finish/pallas_call | solution.py:246
  (1 shorter events, 0.0 us)
Async XLA Ops:
  25.9 27.4 %all-to-all-start.2 = ((f32[8,2,2,24,128]{4,3,2,1,0:T(8,128)}), f32[8,2,2,24,128]{4,3,2,1,0:T(8,128)S(1)}, u32[]{:S(2)}, u32[]{:S(2)}) async-start(f32[8,2,2,24,128]{4,3,2,1,0:T(8,128)} %get-tuple-element.10), calls=%async_computation.2 | async-start | bytes 786432 | tf_op jit(solution)/shard_map/all_to_all | solution.py:206
  40.0 9.4 %collective-permute-start.2 = (f32[2,2,24,128]{3,2,1,0:T(8,128)S(1)}, f32[2,2,24,128]{3,2,1,0:T(8,128)S(1)}, u32[]{:S(2)}, u32[]{:S(2)}) collective-permute-start(f32[2,2,24,128]{3,2,1,0:T(8,128)S(1)} %get-tuple-element.14), channel_id=1, source_target_pairs={{0,24},{8,0},{16,8},{24,16},{1,25},{9,1},{17,9},{25,17},{2,26},{10... | collective-permute-start | bytes 147464 | tf_op jit(solution)/shard_map/ppermute | solution.py:195
  44.4 6.3 %collective-permute-start.1 = (f32[2,2,24,128]{3,2,1,0:T(8,128)S(1)}, f32[2,2,24,128]{3,2,1,0:T(8,128)S(1)}, u32[]{:S(2)}, u32[]{:S(2)}) collective-permute-start(f32[2,2,24,128]{3,2,1,0:T(8,128)S(1)} %get-tuple-element.15), channel_id=1, source_target_pairs={{0,16},{8,24},{16,0},{24,8},{1,17},{9,25},{17,1},{25,9},{2,18},{10... | collective-permute-start | bytes 147464 | tf_op jit(solution)/shard_map/ppermute | solution.py:195
  46.9 6.3 %collective-permute-start = (f32[2,2,24,128]{3,2,1,0:T(8,128)S(1)}, f32[2,2,24,128]{3,2,1,0:T(8,128)S(1)}, u32[]{:S(2)}, u32[]{:S(2)}) collective-permute-start(f32[2,2,24,128]{3,2,1,0:T(8,128)S(1)} %get-tuple-element.16), channel_id=1, source_target_pairs={{0,8},{8,16},{16,24},{24,0},{1,9},{9,17},{17,25},{25,1},{2,10},{10... | collective-permute-start | bytes 147464 | tf_op jit(solution)/shard_map/ppermute | solution.py:195
  53.2 29.7 %copy-start.1 = (f32[8,2,2,24,128]{4,3,2,1,0:T(8,128)}, f32[8,2,2,24,128]{4,3,2,1,0:T(8,128)S(1)}, u32[]{:S(2)}) copy-start(f32[8,2,2,24,128]{4,3,2,1,0:T(8,128)S(1)} %all-to-all-done.2.p0) | copy-start | bytes 1179652
  54.6 43.5 %all-to-all-start.1 = ((f32[8,4,2,2,24,128]{5,4,3,2,1,0:T(8,128)}), f32[8,4,2,2,24,128]{5,4,3,2,1,0:T(8,128)S(1)}, u32[]{:S(2)}, u32[]{:S(2)}) async-start(f32[8,4,2,2,24,128]{5,4,3,2,1,0:T(8,128)} %broadcast_in_dim.2), calls=%async_computation.1 | async-start | bytes 3145728 | tf_op jit(solution)/shard_map/all_to_all | solution.py:209
  60.9 8.8 %collective-permute-start.5 = (f32[8,2,2,24,128]{4,3,2,1,0:T(8,128)S(1)}, f32[8,2,2,24,128]{4,3,2,1,0:T(8,128)S(1)}, u32[]{:S(2)}, u32[]{:S(2)}) collective-permute-start(f32[8,2,2,24,128]{4,3,2,1,0:T(8,128)S(1)} %all-to-all-done.2.p0), channel_id=1, source_target_pairs={{0,24},{8,0},{16,8},{24,16},{1,25},{9,1},{17,9},{25,17},{2,26},{10... | collective-permute-start | bytes 1179656 | tf_op jit(solution)/shard_map/ppermute | solution.py:195
  62.9 10.3 %collective-permute-start.4 = (f32[8,2,2,24,128]{4,3,2,1,0:T(8,128)S(1)}, f32[8,2,2,24,128]{4,3,2,1,0:T(8,128)S(1)}, u32[]{:S(2)}, u32[]{:S(2)}) collective-permute-start(f32[8,2,2,24,128]{4,3,2,1,0:T(8,128)S(1)} %all-to-all-done.2.p0), channel_id=1, source_target_pairs={{0,16},{8,24},{16,0},{24,8},{1,17},{9,25},{17,1},{25,9},{2,18},{10... | collective-permute-start | bytes 1179656 | tf_op jit(solution)/shard_map/ppermute | solution.py:195
  66.0 16.9 %collective-permute-start.3 = (f32[8,2,2,24,128]{4,3,2,1,0:T(8,128)S(1)}, f32[8,2,2,24,128]{4,3,2,1,0:T(8,128)S(1)}, u32[]{:S(2)}, u32[]{:S(2)}) collective-permute-start(f32[8,2,2,24,128]{4,3,2,1,0:T(8,128)S(1)} %all-to-all-done.2.p0), channel_id=1, source_target_pairs={{0,8},{8,16},{16,24},{24,0},{1,9},{9,17},{17,25},{25,1},{2,10},{10... | collective-permute-start | bytes 1179656 | tf_op jit(solution)/shard_map/ppermute | solution.py:195
  69.7 13.2 %copy-start.2 = (f32[8,2,2,24,128]{4,3,2,1,0:T(8,128)}, f32[8,2,2,24,128]{4,3,2,1,0:T(8,128)S(1)}, u32[]{:S(2)}) copy-start(f32[8,2,2,24,128]{4,3,2,1,0:T(8,128)S(1)} %collective-permute-done.5.p3) | copy-start | bytes 1179652
  73.2 9.7 %copy-start.3 = (f32[8,2,2,24,128]{4,3,2,1,0:T(8,128)}, f32[8,2,2,24,128]{4,3,2,1,0:T(8,128)S(1)}, u32[]{:S(2)}) copy-start(f32[8,2,2,24,128]{4,3,2,1,0:T(8,128)S(1)} %collective-permute-done.4.p2) | copy-start | bytes 1179652
  82.9 0.7 copy-start.4
  98.1 1.1 copy-start

commit v2 on v1

v2 whole, which is shorter than its diff:
```python
import functools

import jax
import jax.numpy as jnp
from jax import lax
from jax.experimental import pallas as pl
from jax.experimental.pallas import tpu as pltpu
from jax.sharding import Mesh, PartitionSpec as P

C = 1024
MAXLAG = 31
HALF = 64
LAGS = 63
SAMPLES = 1536
epsilon = 1e-06

TAU = 24
ROW = SAMPLES + 32
K = 3328
FRONT = 40
QFRONT = FRONT - 24
SEQ = K + 128
CHUNKS = (768, 768, 768, 1024)
ROT = (4, 8, 36, 40)
VMEM = pl.BlockSpec(memory_space=pltpu.VMEM)
SMEM = pl.BlockSpec(memory_space=pltpu.SMEM)
BIG = 34 * 1024 * 1024
SMALL = pltpu.CompilerParams(vmem_limit_bytes=8 * 1024 * 1024)


def lanes(shape):
    return lax.broadcasted_iota(jnp.int32, shape, len(shape) - 1)


def prepack(raw, out):
    lane = lanes((TAU, 128))
    for low in range(4):
        a = raw[:, 256 * low : 256 * low + 128]
        b = raw[:, 256 * low + 128 : 256 * low + 256]
        first = jnp.where(
            lane < 32, a, jnp.where(lane < 64, pltpu.roll(b, 32, 1), jnp.where(lane < 96, pltpu.roll(a, 32, 1), pltpu.roll(b, 64, 1)))
        )
        second = jnp.where(
            lane < 32, pltpu.roll(a, 64, 1), jnp.where(lane < 64, pltpu.roll(b, 96, 1), jnp.where(lane < 96, pltpu.roll(a, 96, 1), b))
        )
        for high in range(2):
            out[4 * high + low, :, 512:640] = first
            out[4 * high + low, :, 640:768] = second
            out[4 * high + low, :, 0:512] = raw[:, 512 * high : 512 * high + 512]


def repack(got, p_out, q_out):
    low = lanes((TAU, 128)) < 64
    for high in range(2):
        for pair in range(2):
            one, two = 4 * high + 2 * pair, 4 * high + 2 * pair + 1
            for v in range(6):
                a = got[one, :, 128 * v : 128 * v + 128]
                b = got[two, :, 128 * v : 128 * v + 128]
                even = jnp.where(low, a, pltpu.roll(b, 64, 1))
                odd = jnp.where(low, pltpu.roll(a, 64, 1), b)
                if v < 4:
                    p_out[2 * v, pair, high] = even
                    p_out[2 * v + 1, pair, high] = odd
                else:
                    q_out[pair, 2 * (v - 4), high] = even
                    q_out[pair, 2 * (v - 4) + 1, high] = odd


def split(x):
    hi = x.astype(jnp.bfloat16)
    return hi, (x - hi.astype(jnp.float32)).astype(jnp.bfloat16)


def normalize(rec, mag):
    row = lax.broadcasted_iota(jnp.int32, (128, 256), 0)
    col = lanes((128, 256))
    band = jnp.where((col >= row) & (col <= row + 2 * HALF), 1.0, 0.0).astype(jnp.bfloat16)
    zero = jnp.zeros((HALF, 256), jnp.bfloat16)
    mag[0:HALF, :] = zero
    mag[HALF + SAMPLES : 2 * HALF + SAMPLES, :] = zero
    for pair in range(2):
        mean = jnp.sum(rec[pair], axis=0, keepdims=True) * (1.0 / SAMPLES)
        for i in range(12):
            d = rec[pair, 128 * i : 128 * i + 128, :] - mean
            rec[pair, 128 * i : 128 * i + 128, :] = d
            hi, lo = split(jnp.abs(d))
            mag[HALF + 128 * i : HALF + 128 * i + 128, 0:128] = hi
            mag[HALF + 128 * i : HALF + 128 * i + 128, 128:256] = lo
        for i in range(12):
            both = jnp.dot(band, mag[128 * i : 128 * i + 256, :], preferred_element_type=jnp.float32)
            t = lax.broadcasted_iota(jnp.int32, (128, 128), 0) + 128 * i
            count = (jnp.minimum(t, HALF) + jnp.minimum(SAMPLES - 1 - t, HALF) + 1).astype(jnp.float32)
            running = (both[:, 0:128] + both[:, 128:256]) / count
            rec[pair, 128 * i : 128 * i + 128, :] = rec[pair, 128 * i : 128 * i + 128, :] / (running + epsilon)


def correlate(last, pair, me, p0, p1, p2, p3, q_in, *rest):
    if last:
        before, keep, send, *rest = rest
    else:
        total, *rest = rest
    rec, mag, pseq, qseq, turned, lhs_hi, lhs_lo, rhs_hi, rhs_lo = rest[:9]
    for d, ref in enumerate((p0, p1, p2, p3)):
        x = lax.rem(me[0] + 4 - d, 4)
        for high in range(2):
            for z in range(8):
                at = pl.multiple_of(((high * 8 + z) * 4) * TAU + x * TAU, 8)
                rec[0, pl.ds(at, TAU), :] = ref[z, pair, high]
                rec[1, pl.ds(at, TAU), :] = q_in[z, d, high]
    normalize(rec, mag)
    for seq in (pseq, qseq):
        seq[0:64, :] = jnp.zeros((64, 128), jnp.float32)
        at = QFRONT + SAMPLES - 16
        seq[at : at + 80, :] = jnp.zeros((80, 128), jnp.float32)
        at = QFRONT + ROW + SAMPLES - 16
        seq[at:SEQ, :] = jnp.zeros((SEQ - at, 128), jnp.float32)
    for i in range(12):
        x = rec[0, 128 * i : 128 * i + 128, :]
        r = pltpu.roll(x, 64, 1)
        at = FRONT + 128 * i
        pseq[at : at + 128, 0:64] = x[:, 0:64]
        pseq[at - 16 : at + 112, 64:128] = r[:, 64:128]
        at += ROW
        pseq[at : at + 128, 0:64] = r[:, 0:64]
        pseq[at - 16 : at + 112, 64:128] = x[:, 64:128]
        x = rec[1, 128 * i : 128 * i + 128, :]
        r32, r64, r96 = (pltpu.roll(x, n, 1) for n in (32, 64, 96))
        at = QFRONT + 128 * i
        for e, parts in enumerate(((x, r32, r32, r64), (r64, r96, r96, x))):
            for n, part in enumerate(parts):
                to = at + e * ROW - 8 * (n % 2)
                qseq[to : to + 128, 32 * n : 32 * n + 32] = part[:, 32 * n : 32 * n + 32]
    for i in range(SEQ // 128):
        turned[:, 128 * i : 128 * i + 128] = pseq[128 * i : 128 * i + 128, :].T
    acc = rest[9] if last else total
    start = 0
    for n, width in enumerate(CHUNKS):
        for m in range(8):
            wide = turned[16 * m : 16 * m + 16, start : start + width + 128]
            for r, rot in enumerate(ROT):
                hi, lo = split(pltpu.roll(wide, width + 128 - rot, 1)[:, 0:width])
                lhs_hi[128 * r + 16 * m : 128 * r + 16 * m + 16, start : start + width] = hi
                lhs_lo[128 * r + 16 * m : 128 * r + 16 * m + 16, start : start + width] = lo
        for s in range(4):
            for m in range(width // 128):
                at = start + 128 * m
                hi, lo = split(qseq[at + s : at + s + 128, :])
                rhs_hi[at : at + 128, 128 * s : 128 * s + 128] = hi
                rhs_lo[at : at + 128, 128 * s : 128 * s + 128] = lo
        span = slice(start, start + width)
        part = jnp.dot(lhs_hi[:, span], rhs_hi[span, :], preferred_element_type=jnp.float32)
        part += jnp.dot(lhs_hi[:, span], rhs_lo[span, :], preferred_element_type=jnp.float32)
        part += jnp.dot(lhs_lo[:, span], rhs_hi[span, :], preferred_element_type=jnp.float32)
        if n:
            acc[...] += part
        elif last:
            acc[...] = before[...] + part
        else:
            acc[...] = part
        start += width
    if not last:
        return
    low = lanes((16, 128)) < 64
    first = me[1] == 0
    for g in range(8):
        for x in range(4):
            at = 64 * g + 16 * x
            for s2 in range(2):
                a = acc[at : at + 16, 256 * s2 : 256 * s2 + 128]
                b = acc[at : at + 16, 256 * s2 + 128 : 256 * s2 + 256]
                one = jnp.where(low, a, pltpu.roll(b, 64, 1))
                two = jnp.where(low, pltpu.roll(a, 64, 1), b)
                keep[x, g, s2] = jnp.where(first, one, two)
                send[x, g, s2] = jnp.where(first, two, one)


def final_kernel(got, out):
    lane = lanes((16, 128))
    for g in range(8):
        r, j = g // 2, g % 2
        r0, r1 = r % 2, r // 2
        for s2 in range(2):
            parts = [got[x, g, s2] for x in range(4)]
            for sb in range(2):
                for i in range(2):
                    mu = 2 * s2 + sb + 4 * (1 - r0) + 8 * i + 16 * (1 - j) + 32 * (1 - r1)
                    if mu == 0:
                        continue
                    n = 2 * sb + i
                    moved = [pltpu.roll(parts[x], (32 * (x - n)) % 128, 1) if x != n else parts[x] for x in range(4)]
                    value = jnp.where(lane < 32, moved[0], jnp.where(lane < 64, moved[1], jnp.where(lane < 96, moved[2], moved[3])))
                    out[mu - 1] = value * (1.0 / SAMPLES)


def sds(*shape, dtype=jnp.float32):
    return jax.ShapeDtypeStruct(shape, dtype)


def around(v, d):
    return lax.ppermute(v, "x", [(i, (i + d) % 4) for i in range(4)])


def spread(v):
    return lax.all_to_all(jnp.broadcast_to(v[None], (8,) + v.shape), "z", 0, 0, tiled=True)


def local(raw):
    x = lax.axis_index("x")
    me = jnp.stack([x, lax.axis_index("core")]).astype(jnp.int32)
    sent = pl.pallas_call(prepack, out_shape=sds(8, TAU, 768), in_specs=[VMEM], out_specs=VMEM, compiler_params=SMALL, name="prepack")(raw[0])
    got = lax.all_to_all(sent, ("yh", "yl"), 0, 0, tiled=True)
    p_send, q_send = pl.pallas_call(
        repack, out_shape=(sds(8, 2, 2, TAU, 128), sds(2, 4, 2, TAU, 128)), in_specs=[VMEM], out_specs=(VMEM, VMEM), compiler_params=SMALL, name="repack"
    )(got)
    p_mine = lax.all_to_all(p_send, "z", 0, 0, tiled=True)
    picked = [lax.dynamic_index_in_dim(q_send, lax.rem(x + d, 4), 1, keepdims=False) for d in range(4)]
    q_mine = [picked[0]] + [around(picked[d], d) for d in (1, 2, 3)]
    first = jnp.stack([q[0] for q in q_mine])
    second = jnp.stack([q[1] for q in q_mine])
    q_all = [spread(first)]
    second, *p_all = lax.optimization_barrier((second, p_mine, *(around(p_mine, d) for d in (1, 2, 3))))
    q_all.append(spread(second))
    scratch = [
        pltpu.VMEM((2, SAMPLES, 128), jnp.float32),
        pltpu.VMEM((SAMPLES + 2 * HALF, 256), jnp.bfloat16),
        pltpu.VMEM((SEQ, 128), jnp.float32),
        pltpu.VMEM((SEQ, 128), jnp.float32),
        pltpu.VMEM((128, SEQ), jnp.float32),
        pltpu.VMEM((512, K), jnp.bfloat16),
        pltpu.VMEM((512, K), jnp.bfloat16),
        pltpu.VMEM((K, 512), jnp.bfloat16),
        pltpu.VMEM((K, 512), jnp.bfloat16),
    ]
    params = pltpu.CompilerParams(vmem_limit_bytes=BIG)
    cost = pl.CostEstimate(flops=5 * 10**9, bytes_accessed=4 * 10**6, transcendentals=0)
    total = pl.pallas_call(
        functools.partial(correlate, False, 0),
        out_shape=sds(512, 512),
        in_specs=[SMEM] + [VMEM] * 5,
        out_specs=VMEM,
        scratch_shapes=scratch,
        compiler_params=params,
        cost_estimate=cost,
        name="first_pair",
    )(me, *p_all, q_all[0])
    keep, send = pl.pallas_call(
        functools.partial(correlate, True, 1),
        out_shape=(sds(4, 8, 2, 16, 128), sds(4, 8, 2, 16, 128)),
        in_specs=[SMEM] + [VMEM] * 6,
        out_specs=(VMEM, VMEM),
        scratch_shapes=scratch + [pltpu.VMEM((512, 512), jnp.float32)],
        compiler_params=params,
        cost_estimate=cost,
        name="second_pair",
    )(me, *p_all, q_all[1], total)
    summed = keep + lax.ppermute(send, "core", [(0, 1), (1, 0)])
    mine = lax.all_to_all(summed, "x", 0, 0, tiled=True)
    out = pl.pallas_call(final_kernel, out_shape=sds(LAGS, 16, 128), in_specs=[VMEM], out_specs=VMEM, compiler_params=SMALL, name="finish")(mine)
    return jnp.transpose(out, (1, 0, 2))


def solution(mesh):
    grid = Mesh(mesh.devices.reshape(2, 8, 4, 4, 2), ("yh", "z", "x", "yl", "core"))
    in_specs = (P(("yl", "core"), ("yh", "z", "x"), None),)
    out_specs = P(("yh", "z", "x"), None, ("yl", "core"))
    return jax.shard_map(local, mesh=grid, in_specs=in_specs, out_specs=out_specs, check_vma=False)
```

time: 147 us -> 144 us (0.980)
  waiting for transfers between devices: 20 us -> 54.6 us
  blocking collectives: 43.4 us -> 11.6 us
  Pallas kernels: 39.2 us -> 20.2 us
  starting transfers between devices: 36.8 us -> 52 us
    all_to_all x2 -> x0, blocking collectives: 31.1 us -> none  [the longest x1 21.9 us: local(): got = lax.all_to_all(sent, ('yh', 'yl'), 0, 0, tiled=True)]
    all_to_all x1 -> x3, waiting for transfers between devices: 2.1 us -> 30.7 us  [the longest x1 16.5 us: local(): got = lax.all_to_all(sent, ('yh', 'yl'), 0, 0, tiled=True)]
    pallas_call x4, Pallas kernels: 37.3 us -> 19.2 us  [the longest x1 8.7 us: local(): pl.pallas_call(functools.partial(correlate, True, 1), out_shape=(sds(4, 8...]
    all_to_all x1 -> x3, starting transfers between devices: 6.35 us -> 18.3 us  [the longest x2 10.6 us: spread(): lax.all_to_all(jnp.broadcast_to(v[None], (8,) + v.shape), 'z', 0, 0, tile...]
    ppermute x6, waiting for transfers between devices: 17.9 us -> 20.5 us  [around(): return lax.ppermute(v, 'x', [(i, (i + d) % 4) for i in range(4)])]
    ppermute x0 -> x1, starting transfers between devices: none -> 2.41 us  [local(): summed = keep + lax.ppermute(send, 'core', [(0, 1), (1, 0)])]
    pallas_call x1 -> x0, local copies, waits for them, and re-layouts: 2.13 us -> none  [local(): pl.pallas_call(final_kernel, out_shape=sds(16, LAGS, 128), in_specs=[VMEM...]
    all_to_all x1, waiting for transfers between devices: 0.01 us -> 1.9 us  [local(): p_mine = lax.all_to_all(p_send, 'z', 0, 0, tiled=True)]
  transfers between devices with their start and end apart: 8 -> 11, of which waited for: 6 -> 8; matrix products, arithmetic and copies ran while one was open for 1% -> 0% of each run, Pallas kernels for 8% -> 6%
where the time goes in v2:
time: 144 us
  waiting for transfers between devices  54.6 us (38%)
  starting transfers between devices  52 us (36%)
  Pallas kernels  20.2 us (14%)
  blocking collectives  11.6 us (8%)
  local copies, waits for them, and re-layouts  5.06 us (4%)
    ppermute x6, waiting for transfers between devices, around(): return lax.ppermute(v, 'x', [(i, (i + d) % 4) for i in range(4)])  20.5 us
    ppermute x6, starting transfers between devices, around(): return lax.ppermute(v, 'x', [(i, (i + d) % 4) for i in range(4)])  18.4 us
    all_to_all x1, waiting for transfers between devices, local(): got = lax.all_to_all(sent, ('yh', 'yl'), 0, 0, tiled=True)  16.5 us
    all_to_all x2, waiting for transfers between devices, spread(): lax.all_to_all(jnp.broadcast_to(v[None], (8,) + v.shape), 'z', 0, 0, tile...  14.2 us
    all_to_all x1, starting transfers between devices, local(): p_mine = lax.all_to_all(p_send, 'z', 0, 0, tiled=True)  12.9 us
    all_to_all x1, blocking collectives, local(): mine = lax.all_to_all(summed, 'x', 0, 0, tiled=True)  11.6 us
    all_to_all x2, starting transfers between devices, spread(): lax.all_to_all(jnp.broadcast_to(v[None], (8,) + v.shape), 'z', 0, 0, tile...  10.6 us
    pallas_call x1, Pallas kernels, local(): pl.pallas_call(functools.partial(correlate, True, 1), out_shape=(sds(4, 8...  8.7 us
  transfers between devices with their start and end apart: 11, of which 8 were waited for; matrix products, arithmetic and copies ran while one was open for 0% of the time, Pallas kernels for 6%

profile of v2, /device:TPU:1, one launch (start us, length us, event | category | flops | bytes accessed | tf_op | source)
XLA Modules:
  0.0 143.8 jit_solution(15030484001594095950)
XLA Ops:
  0.0 0.0 copy-start
  0.0 0.9 copy-done
  0.9 1.0 prepack.1
  1.9 7.7 %all-to-all-start = ((f32[8,24,768]{2,1,0:T(8,128)}), f32[8,24,768]{2,1,0:T(8,128)S(1)}, u32[]{:S(2)}, u32[]{:S(2)}) async-start(f32[8,24,768]{2,1,0:T(8,128)} %prepack.1), calls=%async_computation | async-start | bytes 1179648 | tf_op jit(solution)/shard_map/all_to_all | solution.py:212
  9.5 16.5 %all-to-all-done.got = f32[8,24,768]{2,1,0:T(8,128)S(1)} async-done(((f32[8,24,768]{2,1,0:T(8,128)}), f32[8,24,768]{2,1,0:T(8,128)S(1)}, u32[]{:S(2)}, u32[]{:S(2)}) %all-to-all-start) | async-done | bytes 589856 | tf_op jit(solution)/shard_map/all_to_all | solution.py:212
  26.0 1.0 repack.1
  27.0 12.9 %all-to-all-start.1 = ((f32[8,2,2,24,128]{4,3,2,1,0:T(8,128)}), f32[8,2,2,24,128]{4,3,2,1,0:T(8,128)S(1)}, u32[]{:S(2)}, u32[]{:S(2)}) async-start(f32[8,2,2,24,128]{4,3,2,1,0:T(8,128)} %get-tuple-element.15), calls=%async_computation.1 | async-start | bytes 786432 | tf_op jit(solution)/shard_map/all_to_all | solution.py:216
  39.9 3.1 %collective-permute-start = (f32[2,2,24,128]{3,2,1,0:T(8,128)S(1)}, f32[2,2,24,128]{3,2,1,0:T(8,128)S(1)}, u32[]{:S(2)}, u32[]{:S(2)}) collective-permute-start(f32[2,2,24,128]{3,2,1,0:T(8,128)S(1)} %get-tuple-element.25), channel_id=1, source_target_pairs={{0,8},{8,16},{16,24},{24,0},{1,9},{9,17},{17,25},{25,1},{2,10},{10... | collective-permute-start | bytes 147464 | tf_op jit(solution)/shard_map/ppermute | solution.py:201
  43.0 3.4 %collective-permute-start.2 = (f32[2,2,24,128]{3,2,1,0:T(8,128)S(1)}, f32[2,2,24,128]{3,2,1,0:T(8,128)S(1)}, u32[]{:S(2)}, u32[]{:S(2)}) collective-permute-start(f32[2,2,24,128]{3,2,1,0:T(8,128)S(1)} %get-tuple-element.26), channel_id=1, source_target_pairs={{0,24},{8,0},{16,8},{24,16},{1,25},{9,1},{17,9},{25,17},{2,26},{10... | collective-permute-start | bytes 147464 | tf_op jit(solution)/shard_map/ppermute | solution.py:201
  46.4 3.4 %collective-permute-start.1 = (f32[2,2,24,128]{3,2,1,0:T(8,128)S(1)}, f32[2,2,24,128]{3,2,1,0:T(8,128)S(1)}, u32[]{:S(2)}, u32[]{:S(2)}) collective-permute-start(f32[2,2,24,128]{3,2,1,0:T(8,128)S(1)} %get-tuple-element.27), channel_id=1, source_target_pairs={{0,16},{8,24},{16,0},{24,8},{1,17},{9,25},{17,1},{25,9},{2,18},{10... | collective-permute-start | bytes 147464 | tf_op jit(solution)/shard_map/ppermute | solution.py:201
  49.9 0.0 collective-permute-done
  49.9 0.0 collective-permute-done.2
  49.9 3.1 %collective-permute-done.1 = f32[2,2,24,128]{3,2,1,0:T(8,128)S(1)} collective-permute-done((f32[2,2,24,128]{3,2,1,0:T(8,128)S(1)}, f32[2,2,24,128]{3,2,1,0:T(8,128)S(1)}, u32[]{:S(2)}, u32[]{:S(2)}) %collective-permute-start.1) | collective-permute-done | bytes 49184 | tf_op jit(solution)/shard_map/ppermute | solution.py:201
  53.1 1.9 %all-to-all-done.1.p0 = f32[8,2,2,24,128]{4,3,2,1,0:T(8,128)S(1)} async-done(((f32[8,2,2,24,128]{4,3,2,1,0:T(8,128)}), f32[8,2,2,24,128]{4,3,2,1,0:T(8,128)S(1)}, u32[]{:S(2)}, u32[]{:S(2)}) %all-to-all-start.1) | async-done | bytes 393248 | tf_op jit(solution)/shard_map/all_to_all | solution.py:216
  55.0 0.9 broadcast_in_dim.5
  55.9 4.5 %all-to-all-start.3 = ((f32[8,4,2,24,128]{4,3,2,1,0:T(8,128)}), f32[8,4,2,24,128]{4,3,2,1,0:T(8,128)S(1)}, u32[]{:S(2)}, u32[]{:S(2)}) async-start(f32[8,4,2,24,128]{4,3,2,1,0:T(8,128)} %broadcast_in_dim.5), calls=%async_computation.3 | async-start | bytes 1572864 | tf_op jit(solution)/shard_map/all_to_all | solution.py:205
  60.4 3.5 %collective-permute-start.5 = (f32[8,2,2,24,128]{4,3,2,1,0:T(8,128)S(1)}, f32[8,2,2,24,128]{4,3,2,1,0:T(8,128)S(1)}, u32[]{:S(2)}, u32[]{:S(2)}) collective-permute-start(f32[8,2,2,24,128]{4,3,2,1,0:T(8,128)S(1)} %all-to-all-done.1.p0), channel_id=1, source_target_pairs={{0,24},{8,0},{16,8},{24,16},{1,25},{9,1},{17,9},{25,17},{2,26},{10... | collective-permute-start | bytes 1179656 | tf_op jit(solution)/shard_map/ppermute | solution.py:201
  63.9 2.4 %collective-permute-start.4 = (f32[8,2,2,24,128]{4,3,2,1,0:T(8,128)S(1)}, f32[8,2,2,24,128]{4,3,2,1,0:T(8,128)S(1)}, u32[]{:S(2)}, u32[]{:S(2)}) collective-permute-start(f32[8,2,2,24,128]{4,3,2,1,0:T(8,128)S(1)} %all-to-all-done.1.p0), channel_id=1, source_target_pairs={{0,16},{8,24},{16,0},{24,8},{1,17},{9,25},{17,1},{25,9},{2,18},{10... | collective-permute-start | bytes 1179656 | tf_op jit(solution)/shard_map/ppermute | solution.py:201
  66.3 2.5 %collective-permute-start.3 = (f32[8,2,2,24,128]{4,3,2,1,0:T(8,128)S(1)}, f32[8,2,2,24,128]{4,3,2,1,0:T(8,128)S(1)}, u32[]{:S(2)}, u32[]{:S(2)}) collective-permute-start(f32[8,2,2,24,128]{4,3,2,1,0:T(8,128)S(1)} %all-to-all-done.1.p0), channel_id=1, source_target_pairs={{0,8},{8,16},{16,24},{24,0},{1,9},{9,17},{17,25},{25,1},{2,10},{10... | collective-permute-start | bytes 1179656 | tf_op jit(solution)/shard_map/ppermute | solution.py:201
  68.8 1.0 collective-permute-done.5.p3
  69.8 5.1 %collective-permute-done.4.p2 = f32[8,2,2,24,128]{4,3,2,1,0:T(8,128)S(1)} collective-permute-done((f32[8,2,2,24,128]{4,3,2,1,0:T(8,128)S(1)}, f32[8,2,2,24,128]{4,3,2,1,0:T(8,128)S(1)}, u32[]{:S(2)}, u32[]{:S(2)}) %collective-permute-start.4) | collective-permute-done | bytes 393248 | tf_op jit(solution)/shard_map/ppermute | solution.py:201
  74.9 11.3 %collective-permute-done.3.p1 = f32[8,2,2,24,128]{4,3,2,1,0:T(8,128)S(1)} collective-permute-done((f32[8,2,2,24,128]{4,3,2,1,0:T(8,128)S(1)}, f32[8,2,2,24,128]{4,3,2,1,0:T(8,128)S(1)}, u32[]{:S(2)}, u32[]{:S(2)}) %collective-permute-start.3) | collective-permute-done | bytes 393248 | tf_op jit(solution)/shard_map/ppermute | solution.py:201
  86.2 0.0 all-to-all-done.3.q_in
  86.2 1.0 broadcast_in_dim.4
  87.2 6.2 %all-to-all-start.2 = ((f32[8,4,2,24,128]{4,3,2,1,0:T(8,128)}), f32[8,4,2,24,128]{4,3,2,1,0:T(8,128)S(1)}, u32[]{:S(2)}, u32[]{:S(2)}) async-start(f32[8,4,2,24,128]{4,3,2,1,0:T(8,128)} %broadcast_in_dim.4), calls=%async_computation.2 | async-start | bytes 1572864 | tf_op jit(solution)/shard_map/all_to_all | solution.py:205
  93.4 0.1 pad_add_fusion.me
  93.5 8.3 %first_pair.1.rest_0_ = f32[512,512]{1,0:T(8,128)S(1)} custom-call(s32[2]{0:T(128)S(1)} %pad_add_fusion.me, f32[8,2,2,24,128]{4,3,2,1,0:T(8,128)S(1)} %all-to-all-done.1.p0, f32[8,2,2,24,128]{4,3,2,1,0:T(8,128)S(1)} %collective-permute-done.3.p1, f32[8,2,2,24,128]{4,3,2,1,0:T(8,128)S(1)} %collective-permute-done.4.p2, ...), custom_call_target="tpu_custom_call" | custom-call | flops 5000000000 | bytes 4000000 | tf_op jit(solution)/shard_map/first_pair/pallas_call | solution.py:237
  101.8 0.0 copy-start.1
  101.8 1.0 copy-done.1
  102.8 14.2 %all-to-all-done.2.q_in = f32[8,4,2,24,128]{4,3,2,1,0:T(8,128)S(1)} async-done(((f32[8,4,2,24,128]{4,3,2,1,0:T(8,128)}), f32[8,4,2,24,128]{4,3,2,1,0:T(8,128)S(1)}, u32[]{:S(2)}, u32[]{:S(2)}) %all-to-all-start.2) | async-done | bytes 786464 | tf_op jit(solution)/shard_map/all_to_all | solution.py:205
  117.0 0.0 copy-start.2
  117.0 1.2 copy-done.2
  118.2 8.7 %second_pair.1 = (f32[4,8,2,16,128]{4,3,2,1,0:T(8,128)S(1)}, f32[4,8,2,16,128]{4,3,2,1,0:T(8,128)S(1)}) custom-call(s32[2]{0:T(128)S(1)} %pad_add_fusion.me, f32[8,2,2,24,128]{4,3,2,1,0:T(8,128)S(1)} %all-to-all-done.1.p0, f32[8,2,2,24,128]{4,3,2,1,0:T(8,128)S(1)} %collective-permute-done.3.p1, f32[8,2,2,24,128]{4,3,2,1,0:T(8,128)S(1)} %collective-permute-done.4.p2, ...), custom_call_target="tpu_custom_call" | custom-call | flops 5000000000 | bytes 4000000 | tf_op jit(solution)/shard_map/second_pair/pallas_call | solution.py:247
  126.9 2.4 %collective-permute-start.6 = (f32[4,8,2,16,128]{4,3,2,1,0:T(8,128)S(1)}, f32[4,8,2,16,128]{4,3,2,1,0:T(8,128)S(1)}, u32[]{:S(2)}, u32[]{:S(2)}) collective-permute-start(f32[4,8,2,16,128]{4,3,2,1,0:T(8,128)S(1)} %get-tuple-element.22), channel_id=1, source_target_pairs={{0,1},{1,0},{2,3},{3,2},{4,5},{5,4},{6,7},{7,6},{8,9},{9,8},{10,11... | collective-permute-start | bytes 1572872 | tf_op jit(solution)/shard_map/ppermute | solution.py:257
  129.3 1.5 %collective-permute-done.6 = f32[4,8,2,16,128]{4,3,2,1,0:T(8,128)S(1)} collective-permute-done((f32[4,8,2,16,128]{4,3,2,1,0:T(8,128)S(1)}, f32[4,8,2,16,128]{4,3,2,1,0:T(8,128)S(1)}, u32[]{:S(2)}, u32[]{:S(2)}) %collective-permute-start.6) | collective-permute-done | bytes 524320 | tf_op jit(solution)/shard_map/ppermute | solution.py:257
  130.8 0.1 add.32
  130.9 11.6 %all_to_all.25.got = f32[4,8,2,16,128]{4,3,2,1,0:T(8,128)S(1)} all-to-all(f32[4,8,2,16,128]{4,3,2,1,0:T(8,128)S(1)} %add.32), channel_id=1, replica_groups=mesh['yh'=2,'z'=8,'x'=4,'yl'=4,'core'=2] {'x'}, dimensions={0} | all-to-all | bytes 1048576 | tf_op jit(solution)/shard_map/all_to_all | solution.py:258
  142.5 1.3 finish.1
  (7 shorter events, 0.1 us)
Async XLA Ops:
  0.0 0.9 copy-start
  1.9 24.1 %all-to-all-start = ((f32[8,24,768]{2,1,0:T(8,128)}), f32[8,24,768]{2,1,0:T(8,128)S(1)}, u32[]{:S(2)}, u32[]{:S(2)}) async-start(f32[8,24,768]{2,1,0:T(8,128)} %prepack.1), calls=%async_computation | async-start | bytes 1179648 | tf_op jit(solution)/shard_map/all_to_all | solution.py:212
  27.0 28.0 %all-to-all-start.1 = ((f32[8,2,2,24,128]{4,3,2,1,0:T(8,128)}), f32[8,2,2,24,128]{4,3,2,1,0:T(8,128)S(1)}, u32[]{:S(2)}, u32[]{:S(2)}) async-start(f32[8,2,2,24,128]{4,3,2,1,0:T(8,128)} %get-tuple-element.15), calls=%async_computation.1 | async-start | bytes 786432 | tf_op jit(solution)/shard_map/all_to_all | solution.py:216
  39.9 10.0 %collective-permute-start = (f32[2,2,24,128]{3,2,1,0:T(8,128)S(1)}, f32[2,2,24,128]{3,2,1,0:T(8,128)S(1)}, u32[]{:S(2)}, u32[]{:S(2)}) collective-permute-start(f32[2,2,24,128]{3,2,1,0:T(8,128)S(1)} %get-tuple-element.25), channel_id=1, source_target_pairs={{0,8},{8,16},{16,24},{24,0},{1,9},{9,17},{17,25},{25,1},{2,10},{10... | collective-permute-start | bytes 147464 | tf_op jit(solution)/shard_map/ppermute | solution.py:201
  43.0 6.9 %collective-permute-start.2 = (f32[2,2,24,128]{3,2,1,0:T(8,128)S(1)}, f32[2,2,24,128]{3,2,1,0:T(8,128)S(1)}, u32[]{:S(2)}, u32[]{:S(2)}) collective-permute-start(f32[2,2,24,128]{3,2,1,0:T(8,128)S(1)} %get-tuple-element.26), channel_id=1, source_target_pairs={{0,24},{8,0},{16,8},{24,16},{1,25},{9,1},{17,9},{25,17},{2,26},{10... | collective-permute-start | bytes 147464 | tf_op jit(solution)/shard_map/ppermute | solution.py:201
  46.4 6.6 %collective-permute-start.1 = (f32[2,2,24,128]{3,2,1,0:T(8,128)S(1)}, f32[2,2,24,128]{3,2,1,0:T(8,128)S(1)}, u32[]{:S(2)}, u32[]{:S(2)}) collective-permute-start(f32[2,2,24,128]{3,2,1,0:T(8,128)S(1)} %get-tuple-element.27), channel_id=1, source_target_pairs={{0,16},{8,24},{16,0},{24,8},{1,17},{9,25},{17,1},{25,9},{2,18},{10... | collective-permute-start | bytes 147464 | tf_op jit(solution)/shard_map/ppermute | solution.py:201
  55.9 30.3 %all-to-all-start.3 = ((f32[8,4,2,24,128]{4,3,2,1,0:T(8,128)}), f32[8,4,2,24,128]{4,3,2,1,0:T(8,128)S(1)}, u32[]{:S(2)}, u32[]{:S(2)}) async-start(f32[8,4,2,24,128]{4,3,2,1,0:T(8,128)} %broadcast_in_dim.5), calls=%async_computation.3 | async-start | bytes 1572864 | tf_op jit(solution)/shard_map/all_to_all | solution.py:205
  60.4 9.4 %collective-permute-start.5 = (f32[8,2,2,24,128]{4,3,2,1,0:T(8,128)S(1)}, f32[8,2,2,24,128]{4,3,2,1,0:T(8,128)S(1)}, u32[]{:S(2)}, u32[]{:S(2)}) collective-permute-start(f32[8,2,2,24,128]{4,3,2,1,0:T(8,128)S(1)} %all-to-all-done.1.p0), channel_id=1, source_target_pairs={{0,24},{8,0},{16,8},{24,16},{1,25},{9,1},{17,9},{25,17},{2,26},{10... | collective-permute-start | bytes 1179656 | tf_op jit(solution)/shard_map/ppermute | solution.py:201
  63.9 11.0 %collective-permute-start.4 = (f32[8,2,2,24,128]{4,3,2,1,0:T(8,128)S(1)}, f32[8,2,2,24,128]{4,3,2,1,0:T(8,128)S(1)}, u32[]{:S(2)}, u32[]{:S(2)}) collective-permute-start(f32[8,2,2,24,128]{4,3,2,1,0:T(8,128)S(1)} %all-to-all-done.1.p0), channel_id=1, source_target_pairs={{0,16},{8,24},{16,0},{24,8},{1,17},{9,25},{17,1},{25,9},{2,18},{10... | collective-permute-start | bytes 1179656 | tf_op jit(solution)/shard_map/ppermute | solution.py:201
  66.3 19.9 %collective-permute-start.3 = (f32[8,2,2,24,128]{4,3,2,1,0:T(8,128)S(1)}, f32[8,2,2,24,128]{4,3,2,1,0:T(8,128)S(1)}, u32[]{:S(2)}, u32[]{:S(2)}) collective-permute-start(f32[8,2,2,24,128]{4,3,2,1,0:T(8,128)S(1)} %all-to-all-done.1.p0), channel_id=1, source_target_pairs={{0,8},{8,16},{16,24},{24,0},{1,9},{9,17},{17,25},{25,1},{2,10},{10... | collective-permute-start | bytes 1179656 | tf_op jit(solution)/shard_map/ppermute | solution.py:201
  87.2 29.8 %all-to-all-start.2 = ((f32[8,4,2,24,128]{4,3,2,1,0:T(8,128)}), f32[8,4,2,24,128]{4,3,2,1,0:T(8,128)S(1)}, u32[]{:S(2)}, u32[]{:S(2)}) async-start(f32[8,4,2,24,128]{4,3,2,1,0:T(8,128)} %broadcast_in_dim.4), calls=%async_computation.2 | async-start | bytes 1572864 | tf_op jit(solution)/shard_map/all_to_all | solution.py:205
  101.8 1.0 copy-start.1
  117.0 1.2 copy-start.2
  126.9 3.9 %collective-permute-start.6 = (f32[4,8,2,16,128]{4,3,2,1,0:T(8,128)S(1)}, f32[4,8,2,16,128]{4,3,2,1,0:T(8,128)S(1)}, u32[]{:S(2)}, u32[]{:S(2)}) collective-permute-start(f32[4,8,2,16,128]{4,3,2,1,0:T(8,128)S(1)} %get-tuple-element.22), channel_id=1, source_target_pairs={{0,1},{1,0},{2,3},{3,2},{4,5},{5,4},{6,7},{7,6},{8,9},{9,8},{10,11... | collective-permute-start | bytes 1572872 | tf_op jit(solution)/shard_map/ppermute | solution.py:257

commit v3 on v2

--- a/solution.py
+++ b/solution.py
@@ -49,22 +49,27 @@
             out[4 * high + low, :, 0:512] = raw[:, 512 * high : 512 * high + 512]
 
 
-def repack(got, p_out, q_out):
+def pairs(got, high, pair, at):
     low = lanes((TAU, 128)) < 64
+    a = got[4 * high + 2 * pair, :, at : at + 128]
+    b = got[4 * high + 2 * pair + 1, :, at : at + 128]
+    return jnp.where(low, a, pltpu.roll(b, 64, 1)), jnp.where(low, pltpu.roll(a, 64, 1), b)
+
+
+def repack_p(got, out, rest):
     for high in range(2):
         for pair in range(2):
-            one, two = 4 * high + 2 * pair, 4 * high + 2 * pair + 1
-            for v in range(6):
-                a = got[one, :, 128 * v : 128 * v + 128]
-                b = got[two, :, 128 * v : 128 * v + 128]
-                even = jnp.where(low, a, pltpu.roll(b, 64, 1))
-                odd = jnp.where(low, pltpu.roll(a, 64, 1), b)
-                if v < 4:
-                    p_out[2 * v, pair, high] = even
-                    p_out[2 * v + 1, pair, high] = odd
-                else:
-                    q_out[pair, 2 * (v - 4), high] = even
-                    q_out[pair, 2 * (v - 4) + 1, high] = odd
+            for v in range(4):
+                out[2 * v, pair, high], out[2 * v + 1, pair, high] = pairs(got, high, pair, 128 * v)
+    rest[...] = got[:, :, 512:768]
+
+
+def repack_q(me, got, out):
+    for high in range(2):
+        for pair in range(2):
+            for v in range(2):
+                for n, block in enumerate(pairs(got, high, pair, 128 * v)):
+                    out[lax.rem(2 * v + n + 4 - me[0], 4), pair, high] = block
 
 
 def split(x):
@@ -95,7 +100,7 @@
             rec[pair, 128 * i : 128 * i + 128, :] = rec[pair, 128 * i : 128 * i + 128, :] / (running + epsilon)
 
 
-def correlate(last, pair, me, p0, p1, p2, p3, q_in, *rest):
+def correlate(last, me, p0, p1, p2, p3, q_in, *rest):
     if last:
         before, keep, send, *rest = rest
     else:
@@ -106,7 +111,7 @@
         for high in range(2):
             for z in range(8):
                 at = pl.multiple_of(((high * 8 + z) * 4) * TAU + x * TAU, 8)
-                rec[0, pl.ds(at, TAU), :] = ref[z, pair, high]
+                rec[0, pl.ds(at, TAU), :] = ref[z, high]
                 rec[1, pl.ds(at, TAU), :] = q_in[z, d, high]
     normalize(rec, mag)
     for seq in (pseq, qseq):
@@ -201,8 +206,12 @@
     return lax.ppermute(v, "x", [(i, (i + d) % 4) for i in range(4)])
 
 
-def spread(v):
-    return lax.all_to_all(jnp.broadcast_to(v[None], (8,) + v.shape), "z", 0, 0, tiled=True)
+def copies(v):
+    return jnp.broadcast_to(v[None], (8,) + v.shape)
+
+
+def to_all(v):
+    return lax.all_to_all(v, "z", 0, 0, tiled=True)
 
 
 def local(raw):
@@ -210,17 +219,33 @@
     me = jnp.stack([x, lax.axis_index("core")]).astype(jnp.int32)
     sent = pl.pallas_call(prepack, out_shape=sds(8, TAU, 768), in_specs=[VMEM], out_specs=VMEM, compiler_params=SMALL, name="prepack")(raw[0])
     got = lax.all_to_all(sent, ("yh", "yl"), 0, 0, tiled=True)
-    p_send, q_send = pl.pallas_call(
-        repack, out_shape=(sds(8, 2, 2, TAU, 128), sds(2, 4, 2, TAU, 128)), in_specs=[VMEM], out_specs=(VMEM, VMEM), compiler_params=SMALL, name="repack"
+    p_send, rest = pl.pallas_call(
+        repack_p,
+        out_shape=(sds(8, 2, 2, TAU, 128), sds(8, TAU, 256)),
+        in_specs=[VMEM],
+        out_specs=(VMEM, VMEM),
+        compiler_params=SMALL,
+        name="repack_p",
     )(got)
-    p_mine = lax.all_to_all(p_send, "z", 0, 0, tiled=True)
-    picked = [lax.dynamic_index_in_dim(q_send, lax.rem(x + d, 4), 1, keepdims=False) for d in range(4)]
-    q_mine = [picked[0]] + [around(picked[d], d) for d in (1, 2, 3)]
+    p_mine = to_all(p_send)
+    q_send = pl.pallas_call(
+        repack_q,
+        out_shape=sds(4, 2, 2, TAU, 128),
+        in_specs=[SMEM, VMEM],
+        out_specs=VMEM,
+        compiler_params=SMALL,
+        cost_estimate=pl.CostEstimate(flops=0, bytes_accessed=6 * 10**7, transcendentals=0),
+        name="repack_q",
+    )(me, rest)
+    q_mine = [q_send[0]] + [around(q_send[d], d) for d in (1, 2, 3)]
     first = jnp.stack([q[0] for q in q_mine])
-    second = jnp.stack([q[1] for q in q_mine])
-    q_all = [spread(first)]
-    second, *p_all = lax.optimization_barrier((second, p_mine, *(around(p_mine, d) for d in (1, 2, 3))))
-    q_all.append(spread(second))
+    second = copies(jnp.stack([q[1] for q in q_mine]))
+    p_first, p_second = p_mine[:, 0], p_mine[:, 1]
+    q_first = to_all(copies(first))
+    second, *p_first = lax.optimization_barrier((second, p_first, *(around(p_first, d) for d in (1, 2, 3))))
+    q_second = to_all(second)
+    p_second, q_first = lax.optimization_barrier((p_second, q_first))
+    p_second = [p_second] + [around(p_second, d) for d in (1, 2, 3)]
     scratch = [
         pltpu.VMEM((2, SAMPLES, 128), jnp.float32),
         pltpu.VMEM((SAMPLES + 2 * HALF, 256), jnp.bfloat16),
@@ -235,7 +260,7 @@
     params = pltpu.CompilerParams(vmem_limit_bytes=BIG)
     cost = pl.CostEstimate(flops=5 * 10**9, bytes_accessed=4 * 10**6, transcendentals=0)
     total = pl.pallas_call(
-        functools.partial(correlate, False, 0),
+        functools.partial(correlate, False),
         out_shape=sds(512, 512),
         in_specs=[SMEM] + [VMEM] * 5,
         out_specs=VMEM,
@@ -243,9 +268,9 @@
         compiler_params=params,
         cost_estimate=cost,
         name="first_pair",
-    )(me, *p_all, q_all[0])
+    )(me, *p_first, q_first)
     keep, send = pl.pallas_call(
-        functools.partial(correlate, True, 1),
+        functools.partial(correlate, True),
         out_shape=(sds(4, 8, 2, 16, 128), sds(4, 8, 2, 16, 128)),
         in_specs=[SMEM] + [VMEM] * 6,
         out_specs=(VMEM, VMEM),
@@ -253,7 +278,7 @@
         compiler_params=params,
         cost_estimate=cost,
         name="second_pair",
-    )(me, *p_all, q_all[1], total)
+    )(me, *p_second, q_second, total)
     summed = keep + lax.ppermute(send, "core", [(0, 1), (1, 0)])
     mine = lax.all_to_all(summed, "x", 0, 0, tiled=True)
     out = pl.pallas_call(final_kernel, out_shape=sds(LAGS, 16, 128), in_specs=[VMEM], out_specs=VMEM, compiler_params=SMALL, name="finish")(mine)

time: 144 us -> 143 us (level)
  waiting for transfers between devices: 54.6 us -> 43.6 us
  starting transfers between devices: 52 us -> 61.1 us
    ppermute x6 -> x9, waiting for transfers between devices: 20.5 us -> 4.45 us  [around(): return lax.ppermute(v, 'x', [(i, (i + d) % 4) for i in range(4)])]
    ppermute x6 -> x9, starting transfers between devices: 18.4 us -> 30.7 us  [around(): return lax.ppermute(v, 'x', [(i, (i + d) % 4) for i in range(4)])]
    all_to_all x3, starting transfers between devices: 23.6 us -> 17.1 us  [to_all(): return lax.all_to_all(v, 'z', 0, 0, tiled=True)]
    all_to_all x3, waiting for transfers between devices: 16.1 us -> 21.2 us  [to_all(): return lax.all_to_all(v, 'z', 0, 0, tiled=True)]
    ppermute x1, starting transfers between devices: 2.41 us -> 5.7 us  [local(): summed = keep + lax.ppermute(send, 'core', [(0, 1), (1, 0)])]
    pallas_call x3 -> x4, Pallas kernels: 18 us -> 18.6 us  [the longest x1 8.71 us: local(): pl.pallas_call(functools.partial(correlate, True), out_shape=(sds(4, 8, 2...]
  transfers between devices with their start and end apart: 11 -> 14, of which waited for: 8 -> 7; matrix products, arithmetic and copies ran while one was open for 0% -> 1% of each run, Pallas kernels for 6% -> 6%
where the time goes in v3:
time: 143 us
  starting transfers between devices  61.1 us (43%)
  waiting for transfers between devices  43.6 us (30%)
  Pallas kernels  20.9 us (15%)
  blocking collectives  11.5 us (8%)
  local copies, waits for them, and re-layouts  5.1 us (4%)
    ppermute x9, starting transfers between devices, around(): return lax.ppermute(v, 'x', [(i, (i + d) % 4) for i in range(4)])  30.7 us
    all_to_all x3, waiting for transfers between devices, to_all(): return lax.all_to_all(v, 'z', 0, 0, tiled=True)  21.2 us
    all_to_all x3, starting transfers between devices, to_all(): return lax.all_to_all(v, 'z', 0, 0, tiled=True)  17.1 us
    all_to_all x1, waiting for transfers between devices, local(): got = lax.all_to_all(sent, ('yh', 'yl'), 0, 0, tiled=True)  16.4 us
    all_to_all x1, blocking collectives, local(): mine = lax.all_to_all(summed, 'x', 0, 0, tiled=True)  11.5 us
    pallas_call x1, Pallas kernels, local(): pl.pallas_call(functools.partial(correlate, True), out_shape=(sds(4, 8, 2...  8.71 us
    pallas_call x1, Pallas kernels, local(): pl.pallas_call(functools.partial(correlate, False), out_shape=sds(512, 51...  8.32 us
    all_to_all x1, starting transfers between devices, local(): got = lax.all_to_all(sent, ('yh', 'yl'), 0, 0, tiled=True)  7.65 us
  transfers between devices with their start and end apart: 14, of which 7 were waited for; matrix products, arithmetic and copies ran while one was open for 1% of the time, Pallas kernels for 6%

profile of v3, /device:TPU:1, one launch (start us, length us, event | category | flops | bytes accessed | tf_op | source)
XLA Modules:
  0.0 142.6 jit_solution(16617365845296105586)
XLA Ops:
  0.0 0.0 copy-start
  0.0 0.9 copy-done
  0.9 1.0 prepack.1
  1.9 7.7 %all-to-all-start = ((f32[8,24,768]{2,1,0:T(8,128)}), f32[8,24,768]{2,1,0:T(8,128)S(1)}, u32[]{:S(2)}, u32[]{:S(2)}) async-start(f32[8,24,768]{2,1,0:T(8,128)} %prepack.1), calls=%async_computation | async-start | bytes 1179648 | tf_op jit(solution)/shard_map/all_to_all | solution.py:221
  9.6 0.1 pad_add_fusion.me
  9.6 16.4 %all-to-all-done.got = f32[8,24,768]{2,1,0:T(8,128)S(1)} async-done(((f32[8,24,768]{2,1,0:T(8,128)}), f32[8,24,768]{2,1,0:T(8,128)S(1)}, u32[]{:S(2)}, u32[]{:S(2)}) %all-to-all-start) | async-done | bytes 589856 | tf_op jit(solution)/shard_map/all_to_all | solution.py:221
  26.0 0.9 repack_p.1
  26.9 0.7 repack_q.1
  27.6 6.0 %collective-permute-start = (f32[2,2,24,128]{3,2,1,0:T(8,128)S(1)}, f32[2,2,24,128]{3,2,1,0:T(8,128)S(1)}, u32[]{:S(2)}, u32[]{:S(2)}) collective-permute-start(f32[2,2,24,128]{3,2,1,0:T(8,128)S(1)} %get-tuple-element.31), channel_id=1, source_target_pairs={{0,8},{8,16},{16,24},{24,0},{1,9},{9,17},{17,25},{25,1},{2,10},{10... | collective-permute-start | bytes 147464 | tf_op jit(solution)/shard_map/ppermute | solution.py:206
  33.6 4.4 %collective-permute-start.1 = (f32[2,2,24,128]{3,2,1,0:T(8,128)S(1)}, f32[2,2,24,128]{3,2,1,0:T(8,128)S(1)}, u32[]{:S(2)}, u32[]{:S(2)}) collective-permute-start(f32[2,2,24,128]{3,2,1,0:T(8,128)S(1)} %get-tuple-element.33), channel_id=1, source_target_pairs={{0,16},{8,24},{16,0},{24,8},{1,17},{9,25},{17,1},{25,9},{2,18},{10... | collective-permute-start | bytes 147464 | tf_op jit(solution)/shard_map/ppermute | solution.py:206
  38.0 3.1 %collective-permute-start.2 = (f32[2,2,24,128]{3,2,1,0:T(8,128)S(1)}, f32[2,2,24,128]{3,2,1,0:T(8,128)S(1)}, u32[]{:S(2)}, u32[]{:S(2)}) collective-permute-start(f32[2,2,24,128]{3,2,1,0:T(8,128)S(1)} %get-tuple-element.32), channel_id=1, source_target_pairs={{0,24},{8,0},{16,8},{24,16},{1,25},{9,1},{17,9},{25,17},{2,26},{10... | collective-permute-start | bytes 147464 | tf_op jit(solution)/shard_map/ppermute | solution.py:206
  41.1 10.0 %all-to-all-start.1 = ((f32[8,2,2,24,128]{4,3,2,1,0:T(8,128)}), f32[8,2,2,24,128]{4,3,2,1,0:T(8,128)S(1)}, u32[]{:S(2)}, u32[]{:S(2)}) async-start(f32[8,2,2,24,128]{4,3,2,1,0:T(8,128)} %get-tuple-element.16), calls=%async_computation.1 | async-start | bytes 786432 | tf_op jit(solution)/shard_map/all_to_all | solution.py:214
  51.1 0.0 collective-permute-done
  51.2 0.0 collective-permute-done.1
  51.2 0.0 collective-permute-done.2
  51.2 12.5 %all-to-all-done.1 = f32[8,2,2,24,128]{4,3,2,1,0:T(8,128)S(1)} async-done(((f32[8,2,2,24,128]{4,3,2,1,0:T(8,128)}), f32[8,2,2,24,128]{4,3,2,1,0:T(8,128)S(1)}, u32[]{:S(2)}, u32[]{:S(2)}) %all-to-all-start.1) | async-done | bytes 393248 | tf_op jit(solution)/shard_map/all_to_all | solution.py:214
  63.7 1.0 broadcast_in_dim.4
  64.7 3.5 %all-to-all-start.2 = ((f32[8,4,2,24,128]{4,3,2,1,0:T(8,128)}), f32[8,4,2,24,128]{4,3,2,1,0:T(8,128)S(1)}, u32[]{:S(2)}, u32[]{:S(2)}) async-start(f32[8,4,2,24,128]{4,3,2,1,0:T(8,128)} %broadcast_in_dim.4), calls=%async_computation.2 | async-start | bytes 1572864 | tf_op jit(solution)/shard_map/all_to_all | solution.py:214
  68.2 2.2 %collective-permute-start.6 = (f32[8,2,24,128]{3,2,1,0:T(8,128)S(1)}, f32[8,2,24,128]{3,2,1,0:T(8,128)S(1)}, u32[]{:S(2)}, u32[]{:S(2)}) collective-permute-start(f32[8,2,24,128]{3,2,1,0:T(8,128)S(1)} %get-tuple-element.20.p0), channel_id=1, source_target_pairs={{0,8},{8,16},{16,24},{24,0},{1,9},{9,17},{17,25},{25,1},{2,10},{10... | collective-permute-start | bytes 589832 | tf_op jit(solution)/shard_map/ppermute | solution.py:206
  70.5 3.6 %collective-permute-start.7 = (f32[8,2,24,128]{3,2,1,0:T(8,128)S(1)}, f32[8,2,24,128]{3,2,1,0:T(8,128)S(1)}, u32[]{:S(2)}, u32[]{:S(2)}) collective-permute-start(f32[8,2,24,128]{3,2,1,0:T(8,128)S(1)} %get-tuple-element.20.p0), channel_id=1, source_target_pairs={{0,16},{8,24},{16,0},{24,8},{1,17},{9,25},{17,1},{25,9},{2,18},{10... | collective-permute-start | bytes 589832 | tf_op jit(solution)/shard_map/ppermute | solution.py:206
  74.1 2.6 %collective-permute-start.8 = (f32[8,2,24,128]{3,2,1,0:T(8,128)S(1)}, f32[8,2,24,128]{3,2,1,0:T(8,128)S(1)}, u32[]{:S(2)}, u32[]{:S(2)}) collective-permute-start(f32[8,2,24,128]{3,2,1,0:T(8,128)S(1)} %get-tuple-element.20.p0), channel_id=1, source_target_pairs={{0,24},{8,0},{16,8},{24,16},{1,25},{9,1},{17,9},{25,17},{2,26},{10... | collective-permute-start | bytes 589832 | tf_op jit(solution)/shard_map/ppermute | solution.py:206
  76.7 0.0 collective-permute-done.6.p1
  76.7 3.6 %collective-permute-done.7.p2 = f32[8,2,24,128]{3,2,1,0:T(8,128)S(1)} collective-permute-done((f32[8,2,24,128]{3,2,1,0:T(8,128)S(1)}, f32[8,2,24,128]{3,2,1,0:T(8,128)S(1)}, u32[]{:S(2)}, u32[]{:S(2)}) %collective-permute-start.7) | collective-permute-done | bytes 196640 | tf_op jit(solution)/shard_map/ppermute | solution.py:206
  80.3 0.8 collective-permute-done.8.p3
  81.2 1.0 broadcast_in_dim.5
  82.1 6.7 %all-to-all-done.2.q_in = f32[8,4,2,24,128]{4,3,2,1,0:T(8,128)S(1)} async-done(((f32[8,4,2,24,128]{4,3,2,1,0:T(8,128)}), f32[8,4,2,24,128]{4,3,2,1,0:T(8,128)S(1)}, u32[]{:S(2)}, u32[]{:S(2)}) %all-to-all-start.2) | async-done | bytes 786464 | tf_op jit(solution)/shard_map/all_to_all | solution.py:214
  88.8 3.5 %all-to-all-start.3 = ((f32[8,4,2,24,128]{4,3,2,1,0:T(8,128)}), f32[8,4,2,24,128]{4,3,2,1,0:T(8,128)S(1)}, u32[]{:S(2)}, u32[]{:S(2)}) async-start(f32[8,4,2,24,128]{4,3,2,1,0:T(8,128)} %broadcast_in_dim.5), calls=%async_computation.3 | async-start | bytes 1572864 | tf_op jit(solution)/shard_map/all_to_all | solution.py:214
  92.4 2.2 %collective-permute-start.3 = (f32[8,2,24,128]{3,2,1,0:T(8,128)S(1)}, f32[8,2,24,128]{3,2,1,0:T(8,128)S(1)}, u32[]{:S(2)}, u32[]{:S(2)}) collective-permute-start(f32[8,2,24,128]{3,2,1,0:T(8,128)S(1)} %get-tuple-element.18.p0), channel_id=1, source_target_pairs={{0,8},{8,16},{16,24},{24,0},{1,9},{9,17},{17,25},{25,1},{2,10},{10... | collective-permute-start | bytes 589832 | tf_op jit(solution)/shard_map/ppermute | solution.py:206
  94.6 4.6 %collective-permute-start.4 = (f32[8,2,24,128]{3,2,1,0:T(8,128)S(1)}, f32[8,2,24,128]{3,2,1,0:T(8,128)S(1)}, u32[]{:S(2)}, u32[]{:S(2)}) collective-permute-start(f32[8,2,24,128]{3,2,1,0:T(8,128)S(1)} %get-tuple-element.18.p0), channel_id=1, source_target_pairs={{0,16},{8,24},{16,0},{24,8},{1,17},{9,25},{17,1},{25,9},{2,18},{10... | collective-permute-start | bytes 589832 | tf_op jit(solution)/shard_map/ppermute | solution.py:206
  99.2 1.9 %collective-permute-start.5 = (f32[8,2,24,128]{3,2,1,0:T(8,128)S(1)}, f32[8,2,24,128]{3,2,1,0:T(8,128)S(1)}, u32[]{:S(2)}, u32[]{:S(2)}) collective-permute-start(f32[8,2,24,128]{3,2,1,0:T(8,128)S(1)} %get-tuple-element.18.p0), channel_id=1, source_target_pairs={{0,24},{8,0},{16,8},{24,16},{1,25},{9,1},{17,9},{25,17},{2,26},{10... | collective-permute-start | bytes 589832 | tf_op jit(solution)/shard_map/ppermute | solution.py:206
  101.2 8.3 %first_pair.1.rest_0_ = f32[512,512]{1,0:T(8,128)S(1)} custom-call(s32[2]{0:T(128)S(1)} %pad_add_fusion.me, f32[8,2,24,128]{3,2,1,0:T(8,128)S(1)} %get-tuple-element.20.p0, f32[8,2,24,128]{3,2,1,0:T(8,128)S(1)} %collective-permute-done.6.p1, f32[8,2,24,128]{3,2,1,0:T(8,128)S(1)} %collective-permute-done.7.p2, ...), custom_call_target="tpu_custom_call" | custom-call | flops 5000000000 | bytes 4000000 | tf_op jit(solution)/shard_map/first_pair/pallas_call | solution.py:262
  109.5 0.0 copy-start.1
  109.5 1.0 copy-done.1
  110.5 0.0 collective-permute-done.3.p1
  110.5 0.0 collective-permute-done.4.p2
  110.5 0.0 collective-permute-done.5.p3
  110.5 2.1 %all-to-all-done.3.q_in = f32[8,4,2,24,128]{4,3,2,1,0:T(8,128)S(1)} async-done(((f32[8,4,2,24,128]{4,3,2,1,0:T(8,128)}), f32[8,4,2,24,128]{4,3,2,1,0:T(8,128)S(1)}, u32[]{:S(2)}, u32[]{:S(2)}) %all-to-all-start.3) | async-done | bytes 786464 | tf_op jit(solution)/shard_map/all_to_all | solution.py:214
  112.6 0.0 copy-start.2
  112.6 1.2 copy-done.2
  113.8 8.7 %second_pair.1 = (f32[4,8,2,16,128]{4,3,2,1,0:T(8,128)S(1)}, f32[4,8,2,16,128]{4,3,2,1,0:T(8,128)S(1)}) custom-call(s32[2]{0:T(128)S(1)} %pad_add_fusion.me, f32[8,2,24,128]{3,2,1,0:T(8,128)S(1)} %get-tuple-element.18.p0, f32[8,2,24,128]{3,2,1,0:T(8,128)S(1)} %collective-permute-done.3.p1, f32[8,2,24,128]{3,2,1,0:T(8,128)S(1)} %collective-permute-done.4.p2, ...), custom_call_target="tpu_custom_call" | custom-call | flops 5000000000 | bytes 4000000 | tf_op jit(solution)/shard_map/second_pair/pallas_call | solution.py:272
  122.5 5.7 %collective-permute-start.9 = (f32[4,8,2,16,128]{4,3,2,1,0:T(8,128)S(1)}, f32[4,8,2,16,128]{4,3,2,1,0:T(8,128)S(1)}, u32[]{:S(2)}, u32[]{:S(2)}) collective-permute-start(f32[4,8,2,16,128]{4,3,2,1,0:T(8,128)S(1)} %get-tuple-element.26), channel_id=1, source_target_pairs={{0,1},{1,0},{2,3},{3,2},{4,5},{5,4},{6,7},{7,6},{8,9},{9,8},{10,11... | collective-permute-start | bytes 1572872 | tf_op jit(solution)/shard_map/ppermute | solution.py:282
  128.2 1.5 %collective-permute-done.9 = f32[4,8,2,16,128]{4,3,2,1,0:T(8,128)S(1)} collective-permute-done((f32[4,8,2,16,128]{4,3,2,1,0:T(8,128)S(1)}, f32[4,8,2,16,128]{4,3,2,1,0:T(8,128)S(1)}, u32[]{:S(2)}, u32[]{:S(2)}) %collective-permute-start.9) | collective-permute-done | bytes 524320 | tf_op jit(solution)/shard_map/ppermute | solution.py:282
  129.8 0.1 add.3
  129.8 11.5 %all_to_all.25.got = f32[4,8,2,16,128]{4,3,2,1,0:T(8,128)S(1)} all-to-all(f32[4,8,2,16,128]{4,3,2,1,0:T(8,128)S(1)} %add.3), channel_id=1, replica_groups=mesh['yh'=2,'z'=8,'x'=4,'yl'=4,'core'=2] {'x'}, dimensions={0} | all-to-all | bytes 1048576 | tf_op jit(solution)/shard_map/all_to_all | solution.py:283
  141.3 1.3 finish.1
  (8 shorter events, 0.1 us)
Async XLA Ops:
  0.0 0.9 copy-start
  1.9 24.1 %all-to-all-start = ((f32[8,24,768]{2,1,0:T(8,128)}), f32[8,24,768]{2,1,0:T(8,128)S(1)}, u32[]{:S(2)}, u32[]{:S(2)}) async-start(f32[8,24,768]{2,1,0:T(8,128)} %prepack.1), calls=%async_computation | async-start | bytes 1179648 | tf_op jit(solution)/shard_map/all_to_all | solution.py:221
  27.6 23.5 %collective-permute-start = (f32[2,2,24,128]{3,2,1,0:T(8,128)S(1)}, f32[2,2,24,128]{3,2,1,0:T(8,128)S(1)}, u32[]{:S(2)}, u32[]{:S(2)}) collective-permute-start(f32[2,2,24,128]{3,2,1,0:T(8,128)S(1)} %get-tuple-element.31), channel_id=1, source_target_pairs={{0,8},{8,16},{16,24},{24,0},{1,9},{9,17},{17,25},{25,1},{2,10},{10... | collective-permute-start | bytes 147464 | tf_op jit(solution)/shard_map/ppermute | solution.py:206
  33.6 17.5 %collective-permute-start.1 = (f32[2,2,24,128]{3,2,1,0:T(8,128)S(1)}, f32[2,2,24,128]{3,2,1,0:T(8,128)S(1)}, u32[]{:S(2)}, u32[]{:S(2)}) collective-permute-start(f32[2,2,24,128]{3,2,1,0:T(8,128)S(1)} %get-tuple-element.33), channel_id=1, source_target_pairs={{0,16},{8,24},{16,0},{24,8},{1,17},{9,25},{17,1},{25,9},{2,18},{10... | collective-permute-start | bytes 147464 | tf_op jit(solution)/shard_map/ppermute | solution.py:206
  38.0 13.2 %collective-permute-start.2 = (f32[2,2,24,128]{3,2,1,0:T(8,128)S(1)}, f32[2,2,24,128]{3,2,1,0:T(8,128)S(1)}, u32[]{:S(2)}, u32[]{:S(2)}) collective-permute-start(f32[2,2,24,128]{3,2,1,0:T(8,128)S(1)} %get-tuple-element.32), channel_id=1, source_target_pairs={{0,24},{8,0},{16,8},{24,16},{1,25},{9,1},{17,9},{25,17},{2,26},{10... | collective-permute-start | bytes 147464 | tf_op jit(solution)/shard_map/ppermute | solution.py:206
  41.1 22.6 %all-to-all-start.1 = ((f32[8,2,2,24,128]{4,3,2,1,0:T(8,128)}), f32[8,2,2,24,128]{4,3,2,1,0:T(8,128)S(1)}, u32[]{:S(2)}, u32[]{:S(2)}) async-start(f32[8,2,2,24,128]{4,3,2,1,0:T(8,128)} %get-tuple-element.16), calls=%async_computation.1 | async-start | bytes 786432 | tf_op jit(solution)/shard_map/all_to_all | solution.py:214
  64.7 24.1 %all-to-all-start.2 = ((f32[8,4,2,24,128]{4,3,2,1,0:T(8,128)}), f32[8,4,2,24,128]{4,3,2,1,0:T(8,128)S(1)}, u32[]{:S(2)}, u32[]{:S(2)}) async-start(f32[8,4,2,24,128]{4,3,2,1,0:T(8,128)} %broadcast_in_dim.4), calls=%async_computation.2 | async-start | bytes 1572864 | tf_op jit(solution)/shard_map/all_to_all | solution.py:214
  68.2 8.5 %collective-permute-start.6 = (f32[8,2,24,128]{3,2,1,0:T(8,128)S(1)}, f32[8,2,24,128]{3,2,1,0:T(8,128)S(1)}, u32[]{:S(2)}, u32[]{:S(2)}) collective-permute-start(f32[8,2,24,128]{3,2,1,0:T(8,128)S(1)} %get-tuple-element.20.p0), channel_id=1, source_target_pairs={{0,8},{8,16},{16,24},{24,0},{1,9},{9,17},{17,25},{25,1},{2,10},{10... | collective-permute-start | bytes 589832 | tf_op jit(solution)/shard_map/ppermute | solution.py:206
  70.5 9.9 %collective-permute-start.7 = (f32[8,2,24,128]{3,2,1,0:T(8,128)S(1)}, f32[8,2,24,128]{3,2,1,0:T(8,128)S(1)}, u32[]{:S(2)}, u32[]{:S(2)}) collective-permute-start(f32[8,2,24,128]{3,2,1,0:T(8,128)S(1)} %get-tuple-element.20.p0), channel_id=1, source_target_pairs={{0,16},{8,24},{16,0},{24,8},{1,17},{9,25},{17,1},{25,9},{2,18},{10... | collective-permute-start | bytes 589832 | tf_op jit(solution)/shard_map/ppermute | solution.py:206
  74.1 7.1 %collective-permute-start.8 = (f32[8,2,24,128]{3,2,1,0:T(8,128)S(1)}, f32[8,2,24,128]{3,2,1,0:T(8,128)S(1)}, u32[]{:S(2)}, u32[]{:S(2)}) collective-permute-start(f32[8,2,24,128]{3,2,1,0:T(8,128)S(1)} %get-tuple-element.20.p0), channel_id=1, source_target_pairs={{0,24},{8,0},{16,8},{24,16},{1,25},{9,1},{17,9},{25,17},{2,26},{10... | collective-permute-start | bytes 589832 | tf_op jit(solution)/shard_map/ppermute | solution.py:206
  88.8 23.8 %all-to-all-start.3 = ((f32[8,4,2,24,128]{4,3,2,1,0:T(8,128)}), f32[8,4,2,24,128]{4,3,2,1,0:T(8,128)S(1)}, u32[]{:S(2)}, u32[]{:S(2)}) async-start(f32[8,4,2,24,128]{4,3,2,1,0:T(8,128)} %broadcast_in_dim.5), calls=%async_computation.3 | async-start | bytes 1572864 | tf_op jit(solution)/shard_map/all_to_all | solution.py:214
  92.4 18.1 %collective-permute-start.3 = (f32[8,2,24,128]{3,2,1,0:T(8,128)S(1)}, f32[8,2,24,128]{3,2,1,0:T(8,128)S(1)}, u32[]{:S(2)}, u32[]{:S(2)}) collective-permute-start(f32[8,2,24,128]{3,2,1,0:T(8,128)S(1)} %get-tuple-element.18.p0), channel_id=1, source_target_pairs={{0,8},{8,16},{16,24},{24,0},{1,9},{9,17},{17,25},{25,1},{2,10},{10... | collective-permute-start | bytes 589832 | tf_op jit(solution)/shard_map/ppermute | solution.py:206
  94.6 15.9 %collective-permute-start.4 = (f32[8,2,24,128]{3,2,1,0:T(8,128)S(1)}, f32[8,2,24,128]{3,2,1,0:T(8,128)S(1)}, u32[]{:S(2)}, u32[]{:S(2)}) collective-permute-start(f32[8,2,24,128]{3,2,1,0:T(8,128)S(1)} %get-tuple-element.18.p0), channel_id=1, source_target_pairs={{0,16},{8,24},{16,0},{24,8},{1,17},{9,25},{17,1},{25,9},{2,18},{10... | collective-permute-start | bytes 589832 | tf_op jit(solution)/shard_map/ppermute | solution.py:206
  99.2 11.3 %collective-permute-start.5 = (f32[8,2,24,128]{3,2,1,0:T(8,128)S(1)}, f32[8,2,24,128]{3,2,1,0:T(8,128)S(1)}, u32[]{:S(2)}, u32[]{:S(2)}) collective-permute-start(f32[8,2,24,128]{3,2,1,0:T(8,128)S(1)} %get-tuple-element.18.p0), channel_id=1, source_target_pairs={{0,24},{8,0},{16,8},{24,16},{1,25},{9,1},{17,9},{25,17},{2,26},{10... | collective-permute-start | bytes 589832 | tf_op jit(solution)/shard_map/ppermute | solution.py:206
  109.5 1.0 copy-start.1
  112.6 1.2 copy-start.2
  122.5 7.2 %collective-permute-start.9 = (f32[4,8,2,16,128]{4,3,2,1,0:T(8,128)S(1)}, f32[4,8,2,16,128]{4,3,2,1,0:T(8,128)S(1)}, u32[]{:S(2)}, u32[]{:S(2)}) collective-permute-start(f32[4,8,2,16,128]{4,3,2,1,0:T(8,128)S(1)} %get-tuple-element.26), channel_id=1, source_target_pairs={{0,1},{1,0},{2,3},{3,2},{4,5},{5,4},{6,7},{7,6},{8,9},{9,8},{10,11... | collective-permute-start | bytes 1572872 | tf_op jit(solution)/shard_map/ppermute | solution.py:282

commit v4 on v3

--- a/solution.py
+++ b/solution.py
@@ -238,13 +238,13 @@
         name="repack_q",
     )(me, rest)
     q_mine = [q_send[0]] + [around(q_send[d], d) for d in (1, 2, 3)]
+    p_mine, *q_mine = lax.optimization_barrier((p_mine, *q_mine))
     first = jnp.stack([q[0] for q in q_mine])
     second = copies(jnp.stack([q[1] for q in q_mine]))
     p_first, p_second = p_mine[:, 0], p_mine[:, 1]
     q_first = to_all(copies(first))
-    second, *p_first = lax.optimization_barrier((second, p_first, *(around(p_first, d) for d in (1, 2, 3))))
+    second, p_second, *p_first = lax.optimization_barrier((second, p_second, p_first, *(around(p_first, d) for d in (1, 2, 3))))
     q_second = to_all(second)
-    p_second, q_first = lax.optimization_barrier((p_second, q_first))
     p_second = [p_second] + [around(p_second, d) for d in (1, 2, 3)]
     scratch = [
         pltpu.VMEM((2, SAMPLES, 128), jnp.float32),

time: 143 us -> 133 us (0.930)
  waiting for transfers between devices: 43.6 us -> 14.8 us
  blocking collectives: 11.5 us -> 35.4 us
  starting transfers between devices: 61.1 us -> 57 us
    all_to_all x0 -> x1, blocking collectives: none -> 23.4 us  [local(): got = lax.all_to_all(sent, ('yh', 'yl'), 0, 0, tiled=True)]
    all_to_all x1 -> x0, waiting for transfers between devices: 16.4 us -> none  [local(): got = lax.all_to_all(sent, ('yh', 'yl'), 0, 0, tiled=True)]
    all_to_all x3, waiting for transfers between devices: 21.2 us -> 5.58 us  [to_all(): return lax.all_to_all(v, 'z', 0, 0, tiled=True)]
    all_to_all x1 -> x0, starting transfers between devices: 7.65 us -> none  [local(): got = lax.all_to_all(sent, ('yh', 'yl'), 0, 0, tiled=True)]
    all_to_all x3, starting transfers between devices: 17.1 us -> 22 us  [to_all(): return lax.all_to_all(v, 'z', 0, 0, tiled=True)]
    ppermute x9, waiting for transfers between devices: 4.45 us -> 7.71 us  [around(): return lax.ppermute(v, 'x', [(i, (i + d) % 4) for i in range(4)])]
    ppermute x9, starting transfers between devices: 30.7 us -> 29 us  [around(): return lax.ppermute(v, 'x', [(i, (i + d) % 4) for i in range(4)])]
  transfers between devices with their start and end apart: 14 -> 13, of which waited for: 7 -> 6; matrix products, arithmetic and copies ran while one was open for 1% -> 1% of each run, Pallas kernels for 6% -> 7%
where the time goes in v4:
time: 133 us
  starting transfers between devices  57 us (43%)
  blocking collectives  35.4 us (27%)
  Pallas kernels  20 us (15%)
  waiting for transfers between devices  14.8 us (11%)
  local copies, waits for them, and re-layouts  5.08 us (4%)
    ppermute x9, starting transfers between devices, around(): return lax.ppermute(v, 'x', [(i, (i + d) % 4) for i in range(4)])  29 us
    all_to_all x1, blocking collectives, local(): got = lax.all_to_all(sent, ('yh', 'yl'), 0, 0, tiled=True)  23.4 us
    all_to_all x3, starting transfers between devices, to_all(): return lax.all_to_all(v, 'z', 0, 0, tiled=True)  22 us
    all_to_all x1, blocking collectives, local(): mine = lax.all_to_all(summed, 'x', 0, 0, tiled=True)  12 us
    pallas_call x1, Pallas kernels, local(): pl.pallas_call(functools.partial(correlate, True), out_shape=(sds(4, 8, 2...  8.7 us
    pallas_call x1, Pallas kernels, local(): pl.pallas_call(functools.partial(correlate, False), out_shape=sds(512, 51...  8.32 us
    ppermute x9, waiting for transfers between devices, around(): return lax.ppermute(v, 'x', [(i, (i + d) % 4) for i in range(4)])  7.71 us
    ppermute x1, starting transfers between devices, local(): summed = keep + lax.ppermute(send, 'core', [(0, 1), (1, 0)])  5.97 us
  transfers between devices with their start and end apart: 13, of which 6 were waited for; matrix products, arithmetic and copies ran while one was open for 1% of the time, Pallas kernels for 7%

profile of v4, /device:TPU:1, one launch (start us, length us, event | category | flops | bytes accessed | tf_op | source)
XLA Modules:
  0.0 132.6 jit_solution(8071535861332981983)
XLA Ops:
  0.0 0.0 copy-start
  0.0 0.9 copy-done
  0.9 0.1 prepack.1
  1.0 23.4 %all_to_all.25.got = f32[8,24,768]{2,1,0:T(8,128)S(1)} all-to-all(f32[8,24,768]{2,1,0:T(8,128)S(1)} %prepack.1), channel_id=1, replica_groups=mesh['yh'=2,'z'=8,'x'=4,'yl'=4,'core'=2] {'yh','yl'}, dimensions={0} | all-to-all | bytes 1179648 | tf_op jit(solution)/shard_map/all_to_all | solution.py:221
  24.4 0.9 repack_p.1
  25.3 11.6 %all-to-all-start.1 = ((f32[8,2,2,24,128]{4,3,2,1,0:T(8,128)}), f32[8,2,2,24,128]{4,3,2,1,0:T(8,128)S(1)}, u32[]{:S(2)}, u32[]{:S(2)}) async-start(f32[8,2,2,24,128]{4,3,2,1,0:T(8,128)} %get-tuple-element.20), calls=%async_computation.1 | async-start | bytes 786432 | tf_op jit(solution)/shard_map/all_to_all | solution.py:214
  36.9 0.1 pad_add_fusion.me
  37.0 0.7 repack_q.1
  37.6 3.1 %collective-permute-start = (f32[2,2,24,128]{3,2,1,0:T(8,128)S(1)}, f32[2,2,24,128]{3,2,1,0:T(8,128)S(1)}, u32[]{:S(2)}, u32[]{:S(2)}) collective-permute-start(f32[2,2,24,128]{3,2,1,0:T(8,128)S(1)} %get-tuple-element.39), channel_id=1, source_target_pairs={{0,8},{8,16},{16,24},{24,0},{1,9},{9,17},{17,25},{25,1},{2,10},{10... | collective-permute-start | bytes 147464 | tf_op jit(solution)/shard_map/ppermute | solution.py:206
  40.8 4.4 %collective-permute-start.1 = (f32[2,2,24,128]{3,2,1,0:T(8,128)S(1)}, f32[2,2,24,128]{3,2,1,0:T(8,128)S(1)}, u32[]{:S(2)}, u32[]{:S(2)}) collective-permute-start(f32[2,2,24,128]{3,2,1,0:T(8,128)S(1)} %get-tuple-element.38), channel_id=1, source_target_pairs={{0,16},{8,24},{16,0},{24,8},{1,17},{9,25},{17,1},{25,9},{2,18},{10... | collective-permute-start | bytes 147464 | tf_op jit(solution)/shard_map/ppermute | solution.py:206
  45.1 3.1 %collective-permute-start.2 = (f32[2,2,24,128]{3,2,1,0:T(8,128)S(1)}, f32[2,2,24,128]{3,2,1,0:T(8,128)S(1)}, u32[]{:S(2)}, u32[]{:S(2)}) collective-permute-start(f32[2,2,24,128]{3,2,1,0:T(8,128)S(1)} %get-tuple-element.37), channel_id=1, source_target_pairs={{0,24},{8,0},{16,8},{24,16},{1,25},{9,1},{17,9},{25,17},{2,26},{10... | collective-permute-start | bytes 147464 | tf_op jit(solution)/shard_map/ppermute | solution.py:206
  48.2 0.0 collective-permute-done
  48.2 0.0 collective-permute-done.1
  48.2 2.2 %collective-permute-done.2 = f32[2,2,24,128]{3,2,1,0:T(8,128)S(1)} collective-permute-done((f32[2,2,24,128]{3,2,1,0:T(8,128)S(1)}, f32[2,2,24,128]{3,2,1,0:T(8,128)S(1)}, u32[]{:S(2)}, u32[]{:S(2)}) %collective-permute-start.2) | collective-permute-done | bytes 49184 | tf_op jit(solution)/shard_map/ppermute | solution.py:206
  50.4 0.0 all-to-all-done.1
  50.5 0.9 broadcast_in_dim.5
  51.4 6.9 %all-to-all-start.3 = ((f32[8,4,2,24,128]{4,3,2,1,0:T(8,128)}), f32[8,4,2,24,128]{4,3,2,1,0:T(8,128)S(1)}, u32[]{:S(2)}, u32[]{:S(2)}) async-start(f32[8,4,2,24,128]{4,3,2,1,0:T(8,128)} %broadcast_in_dim.5), calls=%async_computation.3 | async-start | bytes 1572864 | tf_op jit(solution)/shard_map/all_to_all | solution.py:214
  58.4 1.9 %collective-permute-start.3 = (f32[8,2,24,128]{3,2,1,0:T(8,128)S(1)}, f32[8,2,24,128]{3,2,1,0:T(8,128)S(1)}, u32[]{:S(2)}, u32[]{:S(2)}) collective-permute-start(f32[8,2,24,128]{3,2,1,0:T(8,128)S(1)} %get-tuple-element.29.p0), channel_id=1, source_target_pairs={{0,8},{8,16},{16,24},{24,0},{1,9},{9,17},{17,25},{25,1},{2,10},{10... | collective-permute-start | bytes 589832 | tf_op jit(solution)/shard_map/ppermute | solution.py:206
  60.3 5.4 %collective-permute-start.4 = (f32[8,2,24,128]{3,2,1,0:T(8,128)S(1)}, f32[8,2,24,128]{3,2,1,0:T(8,128)S(1)}, u32[]{:S(2)}, u32[]{:S(2)}) collective-permute-start(f32[8,2,24,128]{3,2,1,0:T(8,128)S(1)} %get-tuple-element.29.p0), channel_id=1, source_target_pairs={{0,16},{8,24},{16,0},{24,8},{1,17},{9,25},{17,1},{25,9},{2,18},{10... | collective-permute-start | bytes 589832 | tf_op jit(solution)/shard_map/ppermute | solution.py:206
  65.7 1.9 %collective-permute-start.5 = (f32[8,2,24,128]{3,2,1,0:T(8,128)S(1)}, f32[8,2,24,128]{3,2,1,0:T(8,128)S(1)}, u32[]{:S(2)}, u32[]{:S(2)}) collective-permute-start(f32[8,2,24,128]{3,2,1,0:T(8,128)S(1)} %get-tuple-element.29.p0), channel_id=1, source_target_pairs={{0,24},{8,0},{16,8},{24,16},{1,25},{9,1},{17,9},{25,17},{2,26},{10... | collective-permute-start | bytes 589832 | tf_op jit(solution)/shard_map/ppermute | solution.py:206
  67.7 0.0 collective-permute-done.3.p1
  67.7 1.7 %collective-permute-done.4.p2 = f32[8,2,24,128]{3,2,1,0:T(8,128)S(1)} collective-permute-done((f32[8,2,24,128]{3,2,1,0:T(8,128)S(1)}, f32[8,2,24,128]{3,2,1,0:T(8,128)S(1)}, u32[]{:S(2)}, u32[]{:S(2)}) %collective-permute-start.4) | collective-permute-done | bytes 196640 | tf_op jit(solution)/shard_map/ppermute | solution.py:206
  69.4 3.7 %collective-permute-done.5.p3 = f32[8,2,24,128]{3,2,1,0:T(8,128)S(1)} collective-permute-done((f32[8,2,24,128]{3,2,1,0:T(8,128)S(1)}, f32[8,2,24,128]{3,2,1,0:T(8,128)S(1)}, u32[]{:S(2)}, u32[]{:S(2)}) %collective-permute-start.5) | collective-permute-done | bytes 196640 | tf_op jit(solution)/shard_map/ppermute | solution.py:206
  73.2 1.0 broadcast_in_dim.4
  74.1 4.2 %all-to-all-done.3.q_in = f32[8,4,2,24,128]{4,3,2,1,0:T(8,128)S(1)} async-done(((f32[8,4,2,24,128]{4,3,2,1,0:T(8,128)}), f32[8,4,2,24,128]{4,3,2,1,0:T(8,128)S(1)}, u32[]{:S(2)}, u32[]{:S(2)}) %all-to-all-start.3) | async-done | bytes 786464 | tf_op jit(solution)/shard_map/all_to_all | solution.py:214
  78.3 3.5 %all-to-all-start.2 = ((f32[8,4,2,24,128]{4,3,2,1,0:T(8,128)}), f32[8,4,2,24,128]{4,3,2,1,0:T(8,128)S(1)}, u32[]{:S(2)}, u32[]{:S(2)}) async-start(f32[8,4,2,24,128]{4,3,2,1,0:T(8,128)} %broadcast_in_dim.4), calls=%async_computation.2 | async-start | bytes 1572864 | tf_op jit(solution)/shard_map/all_to_all | solution.py:214
  81.9 1.9 %collective-permute-start.6 = (f32[8,2,24,128]{3,2,1,0:T(8,128)S(1)}, f32[8,2,24,128]{3,2,1,0:T(8,128)S(1)}, u32[]{:S(2)}, u32[]{:S(2)}) collective-permute-start(f32[8,2,24,128]{3,2,1,0:T(8,128)S(1)} %get-tuple-element.27.p0), channel_id=1, source_target_pairs={{0,8},{8,16},{16,24},{24,0},{1,9},{9,17},{17,25},{25,1},{2,10},{10... | collective-permute-start | bytes 589832 | tf_op jit(solution)/shard_map/ppermute | solution.py:206
  83.8 5.4 %collective-permute-start.7 = (f32[8,2,24,128]{3,2,1,0:T(8,128)S(1)}, f32[8,2,24,128]{3,2,1,0:T(8,128)S(1)}, u32[]{:S(2)}, u32[]{:S(2)}) collective-permute-start(f32[8,2,24,128]{3,2,1,0:T(8,128)S(1)} %get-tuple-element.27.p0), channel_id=1, source_target_pairs={{0,16},{8,24},{16,0},{24,8},{1,17},{9,25},{17,1},{25,9},{2,18},{10... | collective-permute-start | bytes 589832 | tf_op jit(solution)/shard_map/ppermute | solution.py:206
  89.2 1.9 %collective-permute-start.8 = (f32[8,2,24,128]{3,2,1,0:T(8,128)S(1)}, f32[8,2,24,128]{3,2,1,0:T(8,128)S(1)}, u32[]{:S(2)}, u32[]{:S(2)}) collective-permute-start(f32[8,2,24,128]{3,2,1,0:T(8,128)S(1)} %get-tuple-element.27.p0), channel_id=1, source_target_pairs={{0,24},{8,0},{16,8},{24,16},{1,25},{9,1},{17,9},{25,17},{2,26},{10... | collective-permute-start | bytes 589832 | tf_op jit(solution)/shard_map/ppermute | solution.py:206
  91.1 8.3 %first_pair.1.rest_0_ = f32[512,512]{1,0:T(8,128)S(1)} custom-call(s32[2]{0:T(128)S(1)} %pad_add_fusion.me, f32[8,2,24,128]{3,2,1,0:T(8,128)S(1)} %get-tuple-element.29.p0, f32[8,2,24,128]{3,2,1,0:T(8,128)S(1)} %collective-permute-done.3.p1, f32[8,2,24,128]{3,2,1,0:T(8,128)S(1)} %collective-permute-done.4.p2, ...), custom_call_target="tpu_custom_call" | custom-call | flops 5000000000 | bytes 4000000 | tf_op jit(solution)/shard_map/first_pair/pallas_call | solution.py:262
  99.5 0.0 copy-start.1
  99.5 1.0 copy-done.1
  100.4 0.0 collective-permute-done.6.p1
  100.5 0.0 collective-permute-done.7.p2
  100.5 0.0 collective-permute-done.8.p3
  100.5 1.4 %all-to-all-done.2.q_in = f32[8,4,2,24,128]{4,3,2,1,0:T(8,128)S(1)} async-done(((f32[8,4,2,24,128]{4,3,2,1,0:T(8,128)}), f32[8,4,2,24,128]{4,3,2,1,0:T(8,128)S(1)}, u32[]{:S(2)}, u32[]{:S(2)}) %all-to-all-start.2) | async-done | bytes 786464 | tf_op jit(solution)/shard_map/all_to_all | solution.py:214
  101.8 0.0 copy-start.2
  101.9 1.2 copy-done.2
  103.1 8.7 %second_pair.1 = (f32[4,8,2,16,128]{4,3,2,1,0:T(8,128)S(1)}, f32[4,8,2,16,128]{4,3,2,1,0:T(8,128)S(1)}) custom-call(s32[2]{0:T(128)S(1)} %pad_add_fusion.me, f32[8,2,24,128]{3,2,1,0:T(8,128)S(1)} %get-tuple-element.27.p0, f32[8,2,24,128]{3,2,1,0:T(8,128)S(1)} %collective-permute-done.6.p1, f32[8,2,24,128]{3,2,1,0:T(8,128)S(1)} %collective-permute-done.7.p2, ...), custom_call_target="tpu_custom_call" | custom-call | flops 5000000000 | bytes 4000000 | tf_op jit(solution)/shard_map/second_pair/pallas_call | solution.py:272
  111.8 6.0 %collective-permute-start.9 = (f32[4,8,2,16,128]{4,3,2,1,0:T(8,128)S(1)}, f32[4,8,2,16,128]{4,3,2,1,0:T(8,128)S(1)}, u32[]{:S(2)}, u32[]{:S(2)}) collective-permute-start(f32[4,8,2,16,128]{4,3,2,1,0:T(8,128)S(1)} %get-tuple-element.34), channel_id=1, source_target_pairs={{0,1},{1,0},{2,3},{3,2},{4,5},{5,4},{6,7},{7,6},{8,9},{9,8},{10,11... | collective-permute-start | bytes 1572872 | tf_op jit(solution)/shard_map/ppermute | solution.py:282
  117.8 1.5 %collective-permute-done.9 = f32[4,8,2,16,128]{4,3,2,1,0:T(8,128)S(1)} collective-permute-done((f32[4,8,2,16,128]{4,3,2,1,0:T(8,128)S(1)}, f32[4,8,2,16,128]{4,3,2,1,0:T(8,128)S(1)}, u32[]{:S(2)}, u32[]{:S(2)}) %collective-permute-start.9) | collective-permute-done | bytes 524320 | tf_op jit(solution)/shard_map/ppermute | solution.py:282
  119.3 0.1 add.3
  119.4 12.0 %all_to_all.26.got = f32[4,8,2,16,128]{4,3,2,1,0:T(8,128)S(1)} all-to-all(f32[4,8,2,16,128]{4,3,2,1,0:T(8,128)S(1)} %add.3), channel_id=1, replica_groups=mesh['yh'=2,'z'=8,'x'=4,'yl'=4,'core'=2] {'x'}, dimensions={0} | all-to-all | bytes 1048576 | tf_op jit(solution)/shard_map/all_to_all | solution.py:283
  131.4 1.3 finish.1
  (6 shorter events, 0.1 us)
Async XLA Ops:
  0.0 0.9 copy-start
  25.3 25.1 %all-to-all-start.1 = ((f32[8,2,2,24,128]{4,3,2,1,0:T(8,128)}), f32[8,2,2,24,128]{4,3,2,1,0:T(8,128)S(1)}, u32[]{:S(2)}, u32[]{:S(2)}) async-start(f32[8,2,2,24,128]{4,3,2,1,0:T(8,128)} %get-tuple-element.20), calls=%async_computation.1 | async-start | bytes 786432 | tf_op jit(solution)/shard_map/all_to_all | solution.py:214
  37.6 10.6 %collective-permute-start = (f32[2,2,24,128]{3,2,1,0:T(8,128)S(1)}, f32[2,2,24,128]{3,2,1,0:T(8,128)S(1)}, u32[]{:S(2)}, u32[]{:S(2)}) collective-permute-start(f32[2,2,24,128]{3,2,1,0:T(8,128)S(1)} %get-tuple-element.39), channel_id=1, source_target_pairs={{0,8},{8,16},{16,24},{24,0},{1,9},{9,17},{17,25},{25,1},{2,10},{10... | collective-permute-start | bytes 147464 | tf_op jit(solution)/shard_map/ppermute | solution.py:206
  40.8 7.4 %collective-permute-start.1 = (f32[2,2,24,128]{3,2,1,0:T(8,128)S(1)}, f32[2,2,24,128]{3,2,1,0:T(8,128)S(1)}, u32[]{:S(2)}, u32[]{:S(2)}) collective-permute-start(f32[2,2,24,128]{3,2,1,0:T(8,128)S(1)} %get-tuple-element.38), channel_id=1, source_target_pairs={{0,16},{8,24},{16,0},{24,8},{1,17},{9,25},{17,1},{25,9},{2,18},{10... | collective-permute-start | bytes 147464 | tf_op jit(solution)/shard_map/ppermute | solution.py:206
  45.1 5.3 %collective-permute-start.2 = (f32[2,2,24,128]{3,2,1,0:T(8,128)S(1)}, f32[2,2,24,128]{3,2,1,0:T(8,128)S(1)}, u32[]{:S(2)}, u32[]{:S(2)}) collective-permute-start(f32[2,2,24,128]{3,2,1,0:T(8,128)S(1)} %get-tuple-element.37), channel_id=1, source_target_pairs={{0,24},{8,0},{16,8},{24,16},{1,25},{9,1},{17,9},{25,17},{2,26},{10... | collective-permute-start | bytes 147464 | tf_op jit(solution)/shard_map/ppermute | solution.py:206
  51.4 26.9 %all-to-all-start.3 = ((f32[8,4,2,24,128]{4,3,2,1,0:T(8,128)}), f32[8,4,2,24,128]{4,3,2,1,0:T(8,128)S(1)}, u32[]{:S(2)}, u32[]{:S(2)}) async-start(f32[8,4,2,24,128]{4,3,2,1,0:T(8,128)} %broadcast_in_dim.5), calls=%async_computation.3 | async-start | bytes 1572864 | tf_op jit(solution)/shard_map/all_to_all | solution.py:214
  58.4 9.3 %collective-permute-start.3 = (f32[8,2,24,128]{3,2,1,0:T(8,128)S(1)}, f32[8,2,24,128]{3,2,1,0:T(8,128)S(1)}, u32[]{:S(2)}, u32[]{:S(2)}) collective-permute-start(f32[8,2,24,128]{3,2,1,0:T(8,128)S(1)} %get-tuple-element.29.p0), channel_id=1, source_target_pairs={{0,8},{8,16},{16,24},{24,0},{1,9},{9,17},{17,25},{25,1},{2,10},{10... | collective-permute-start | bytes 589832 | tf_op jit(solution)/shard_map/ppermute | solution.py:206
  60.3 9.1 %collective-permute-start.4 = (f32[8,2,24,128]{3,2,1,0:T(8,128)S(1)}, f32[8,2,24,128]{3,2,1,0:T(8,128)S(1)}, u32[]{:S(2)}, u32[]{:S(2)}) collective-permute-start(f32[8,2,24,128]{3,2,1,0:T(8,128)S(1)} %get-tuple-element.29.p0), channel_id=1, source_target_pairs={{0,16},{8,24},{16,0},{24,8},{1,17},{9,25},{17,1},{25,9},{2,18},{10... | collective-permute-start | bytes 589832 | tf_op jit(solution)/shard_map/ppermute | solution.py:206
  65.7 7.4 %collective-permute-start.5 = (f32[8,2,24,128]{3,2,1,0:T(8,128)S(1)}, f32[8,2,24,128]{3,2,1,0:T(8,128)S(1)}, u32[]{:S(2)}, u32[]{:S(2)}) collective-permute-start(f32[8,2,24,128]{3,2,1,0:T(8,128)S(1)} %get-tuple-element.29.p0), channel_id=1, source_target_pairs={{0,24},{8,0},{16,8},{24,16},{1,25},{9,1},{17,9},{25,17},{2,26},{10... | collective-permute-start | bytes 589832 | tf_op jit(solution)/shard_map/ppermute | solution.py:206
  78.3 23.5 %all-to-all-start.2 = ((f32[8,4,2,24,128]{4,3,2,1,0:T(8,128)}), f32[8,4,2,24,128]{4,3,2,1,0:T(8,128)S(1)}, u32[]{:S(2)}, u32[]{:S(2)}) async-start(f32[8,4,2,24,128]{4,3,2,1,0:T(8,128)} %broadcast_in_dim.4), calls=%async_computation.2 | async-start | bytes 1572864 | tf_op jit(solution)/shard_map/all_to_all | solution.py:214
  81.9 18.6 %collective-permute-start.6 = (f32[8,2,24,128]{3,2,1,0:T(8,128)S(1)}, f32[8,2,24,128]{3,2,1,0:T(8,128)S(1)}, u32[]{:S(2)}, u32[]{:S(2)}) collective-permute-start(f32[8,2,24,128]{3,2,1,0:T(8,128)S(1)} %get-tuple-element.27.p0), channel_id=1, source_target_pairs={{0,8},{8,16},{16,24},{24,0},{1,9},{9,17},{17,25},{25,1},{2,10},{10... | collective-permute-start | bytes 589832 | tf_op jit(solution)/shard_map/ppermute | solution.py:206
  83.8 16.6 %collective-permute-start.7 = (f32[8,2,24,128]{3,2,1,0:T(8,128)S(1)}, f32[8,2,24,128]{3,2,1,0:T(8,128)S(1)}, u32[]{:S(2)}, u32[]{:S(2)}) collective-permute-start(f32[8,2,24,128]{3,2,1,0:T(8,128)S(1)} %get-tuple-element.27.p0), channel_id=1, source_target_pairs={{0,16},{8,24},{16,0},{24,8},{1,17},{9,25},{17,1},{25,9},{2,18},{10... | collective-permute-start | bytes 589832 | tf_op jit(solution)/shard_map/ppermute | solution.py:206
  89.2 11.3 %collective-permute-start.8 = (f32[8,2,24,128]{3,2,1,0:T(8,128)S(1)}, f32[8,2,24,128]{3,2,1,0:T(8,128)S(1)}, u32[]{:S(2)}, u32[]{:S(2)}) collective-permute-start(f32[8,2,24,128]{3,2,1,0:T(8,128)S(1)} %get-tuple-element.27.p0), channel_id=1, source_target_pairs={{0,24},{8,0},{16,8},{24,16},{1,25},{9,1},{17,9},{25,17},{2,26},{10... | collective-permute-start | bytes 589832 | tf_op jit(solution)/shard_map/ppermute | solution.py:206
  99.5 1.0 copy-start.1
  101.8 1.2 copy-start.2
  111.8 7.5 %collective-permute-start.9 = (f32[4,8,2,16,128]{4,3,2,1,0:T(8,128)S(1)}, f32[4,8,2,16,128]{4,3,2,1,0:T(8,128)S(1)}, u32[]{:S(2)}, u32[]{:S(2)}) collective-permute-start(f32[4,8,2,16,128]{4,3,2,1,0:T(8,128)S(1)} %get-tuple-element.34), channel_id=1, source_target_pairs={{0,1},{1,0},{2,3},{3,2},{4,5},{5,4},{6,7},{7,6},{8,9},{9,8},{10,11... | collective-permute-start | bytes 1572872 | tf_op jit(solution)/shard_map/ppermute | solution.py:282

commit v5 on v1

v5 whole, which is shorter than its diff:
```python
import jax
import jax.numpy as jnp
from jax import lax
from jax.experimental import pallas as pl
from jax.experimental.pallas import tpu as pltpu
from jax.sharding import Mesh, PartitionSpec as P

C = 1024
MAXLAG = 31
HALF = 64
LAGS = 63
SAMPLES = 1536
epsilon = 1e-06

TAU = 24
ROW = SAMPLES + 32
K = 3328
FRONT = 40
QFRONT = FRONT - 24
SEQ = K + 128
CHUNKS = (768, 768, 768, 1024)
WIDE = 256
ROT = (4, 8, 36, 40)
VMEM = pl.BlockSpec(memory_space=pltpu.VMEM)
HBM = pl.BlockSpec(memory_space=pltpu.HBM)
SMEM = pl.BlockSpec(memory_space=pltpu.SMEM)
P_VMEM = 49 * 1024 * 1024
Q_VMEM = 49 * 1024 * 1024
SMALL = pltpu.CompilerParams(vmem_limit_bytes=8 * 1024 * 1024)


def lanes(shape):
    return lax.broadcasted_iota(jnp.int32, shape, len(shape) - 1)


def prepack(raw, out):
    lane = lanes((TAU, 128))
    for low in range(4):
        a = raw[:, 256 * low : 256 * low + 128]
        b = raw[:, 256 * low + 128 : 256 * low + 256]
        first = jnp.where(
            lane < 32, a, jnp.where(lane < 64, pltpu.roll(b, 32, 1), jnp.where(lane < 96, pltpu.roll(a, 32, 1), pltpu.roll(b, 64, 1)))
        )
        second = jnp.where(
            lane < 32, pltpu.roll(a, 64, 1), jnp.where(lane < 64, pltpu.roll(b, 96, 1), jnp.where(lane < 96, pltpu.roll(a, 96, 1), b))
        )
        for high in range(2):
            out[4 * high + low, :, 512:640] = first
            out[4 * high + low, :, 640:768] = second
            out[4 * high + low, :, 0:512] = raw[:, 512 * high : 512 * high + 512]


def pairs(got, high, pair, at):
    low = lanes((TAU, 128)) < 64
    a = got[4 * high + 2 * pair, :, at : at + 128]
    b = got[4 * high + 2 * pair + 1, :, at : at + 128]
    return jnp.where(low, a, pltpu.roll(b, 64, 1)), jnp.where(low, pltpu.roll(a, 64, 1), b)


def repack_p(got, out, rest):
    for high in range(2):
        for pair in range(2):
            for v in range(4):
                out[2 * v, pair, high], out[2 * v + 1, pair, high] = pairs(got, high, pair, 128 * v)
    rest[...] = got[:, :, 512:768]


def repack_q(me, got, out):
    for high in range(2):
        for pair in range(2):
            for v in range(2):
                for n, block in enumerate(pairs(got, high, pair, 128 * v)):
                    out[lax.rem(2 * v + n + 4 - me[0], 4), pair, high] = block


def split(x):
    hi = x.astype(jnp.bfloat16)
    return hi, (x - hi.astype(jnp.float32)).astype(jnp.bfloat16)


def normalize(rec, mag):
    row = lax.broadcasted_iota(jnp.int32, (128, 256), 0)
    col = lanes((128, 256))
    band = jnp.where((col >= row) & (col <= row + 2 * HALF), 1.0, 0.0).astype(jnp.bfloat16)
    zero = jnp.zeros((HALF, 256), jnp.bfloat16)
    mag[0:HALF, :] = zero
    mag[HALF + SAMPLES : 2 * HALF + SAMPLES, :] = zero
    for pair in range(2):
        mean = jnp.sum(rec[pair], axis=0, keepdims=True) * (1.0 / SAMPLES)
        for i in range(12):
            d = rec[pair, 128 * i : 128 * i + 128, :] - mean
            rec[pair, 128 * i : 128 * i + 128, :] = d
            hi, lo = split(jnp.abs(d))
            mag[HALF + 128 * i : HALF + 128 * i + 128, 0:128] = hi
            mag[HALF + 128 * i : HALF + 128 * i + 128, 128:256] = lo
        for i in range(12):
            both = jnp.dot(band, mag[128 * i : 128 * i + 256, :], preferred_element_type=jnp.float32)
            t = lax.broadcasted_iota(jnp.int32, (128, 128), 0) + 128 * i
            count = (jnp.minimum(t, HALF) + jnp.minimum(SAMPLES - 1 - t, HALF) + 1).astype(jnp.float32)
            running = (both[:, 0:128] + both[:, 128:256]) / count
            rec[pair, 128 * i : 128 * i + 128, :] = rec[pair, 128 * i : 128 * i + 128, :] / (running + epsilon)


def place(me, d, high, z):
    return pl.multiple_of(((high * 8 + z) * 4) * TAU + lax.rem(me[0] + 4 - d, 4) * TAU, 8)


def clear(seq):
    seq[0:64, :] = jnp.zeros((64, 128), jnp.float32)
    at = QFRONT + SAMPLES - 16
    seq[at : at + 80, :] = jnp.zeros((80, 128), jnp.float32)
    at = QFRONT + ROW + SAMPLES - 16
    seq[at:SEQ, :] = jnp.zeros((SEQ - at, 128), jnp.float32)


def moves(from_, to, sems, pair, start):
    copy = pltpu.make_async_copy(from_.at[pair], to.at[pair], sems.at[pair])
    if start:
        copy.start()
    else:
        copy.wait()


def p_side(me, p0, p1, p2, p3, out, rec, mag, seq, turned, lhs, sems):
    for d, ref in enumerate((p0, p1, p2, p3)):
        for high in range(2):
            for z in range(8):
                for pair in range(2):
                    rec[pair, pl.ds(place(me, d, high, z), TAU), :] = ref[z, pair, high]
    normalize(rec, mag)
    for pair in range(2):
        clear(seq)
        for i in range(12):
            x = rec[pair, 128 * i : 128 * i + 128, :]
            r = pltpu.roll(x, 64, 1)
            at = FRONT + 128 * i
            seq[at : at + 128, 0:64] = x[:, 0:64]
            seq[at - 16 : at + 112, 64:128] = r[:, 64:128]
            at += ROW
            seq[at : at + 128, 0:64] = r[:, 0:64]
            seq[at - 16 : at + 112, 64:128] = x[:, 64:128]
        for i in range(SEQ // 128):
            turned[:, 128 * i : 128 * i + 128] = seq[128 * i : 128 * i + 128, :].T
        for at in range(0, K, WIDE):
            for m in range(8):
                wide = turned[16 * m : 16 * m + 16, at : at + WIDE + 128]
                for r, rot in enumerate(ROT):
                    hi, lo = split(pltpu.roll(wide, WIDE + 128 - rot, 1)[:, 0:WIDE])
                    lhs[pair, 0, 128 * r + 16 * m : 128 * r + 16 * m + 16, at : at + WIDE] = hi
                    lhs[pair, 1, 128 * r + 16 * m : 128 * r + 16 * m + 16, at : at + WIDE] = lo
        moves(lhs, out, sems, pair, True)
    for pair in range(2):
        moves(lhs, out, sems, pair, False)


def correlate(me, q_in, p_in, keep, send, rec, mag, seq, lhs, rhs_hi, rhs_lo, acc, sems):
    for pair in range(2):
        moves(p_in, lhs, sems, pair, True)
    for d in range(4):
        for high in range(2):
            for z in range(8):
                for pair in range(2):
                    rec[pair, pl.ds(place(me, d, high, z), TAU), :] = q_in[z, d, pair, high]
    normalize(rec, mag)
    for pair in range(2):
        clear(seq.at[pair])
        for i in range(12):
            x = rec[pair, 128 * i : 128 * i + 128, :]
            r32, r64, r96 = (pltpu.roll(x, n, 1) for n in (32, 64, 96))
            at = QFRONT + 128 * i
            for e, parts in enumerate(((x, r32, r32, r64), (r64, r96, r96, x))):
                for n, part in enumerate(parts):
                    to = at + e * ROW - 8 * (n % 2)
                    seq[pair, to : to + 128, 32 * n : 32 * n + 32] = part[:, 32 * n : 32 * n + 32]
        moves(p_in, lhs, sems, pair, False)
        start = 0
        for n, width in enumerate(CHUNKS):
            for s in range(4):
                for m in range(width // 128):
                    at = start + 128 * m
                    hi, lo = split(seq[pair, at + s : at + s + 128, :])
                    rhs_hi[pair, at : at + 128, 128 * s : 128 * s + 128] = hi
                    rhs_lo[pair, at : at + 128, 128 * s : 128 * s + 128] = lo
            span = slice(start, start + width)
            part = jnp.dot(lhs[pair, 0, :, span], rhs_hi[pair, span, :], preferred_element_type=jnp.float32)
            part += jnp.dot(lhs[pair, 0, :, span], rhs_lo[pair, span, :], preferred_element_type=jnp.float32)
            part += jnp.dot(lhs[pair, 1, :, span], rhs_hi[pair, span, :], preferred_element_type=jnp.float32)
            if n or pair:
                acc[...] += part
            else:
                acc[...] = part
            start += width
    low = lanes((16, 128)) < 64
    first = me[1] == 0
    for g in range(8):
        for x in range(4):
            at = 64 * g + 16 * x
            for s2 in range(2):
                a = acc[at : at + 16, 256 * s2 : 256 * s2 + 128]
                b = acc[at : at + 16, 256 * s2 + 128 : 256 * s2 + 256]
                one = jnp.where(low, a, pltpu.roll(b, 64, 1))
                two = jnp.where(low, pltpu.roll(a, 64, 1), b)
                keep[x, g, s2] = jnp.where(first, one, two)
                send[x, g, s2] = jnp.where(first, two, one)


def final_kernel(got, out):
    lane = lanes((16, 128))
    for g in range(8):
        r, j = g // 2, g % 2
        r0, r1 = r % 2, r // 2
        for s2 in range(2):
            parts = [got[x, g, s2] for x in range(4)]
            for sb in range(2):
                for i in range(2):
                    mu = 2 * s2 + sb + 4 * (1 - r0) + 8 * i + 16 * (1 - j) + 32 * (1 - r1)
                    if mu == 0:
                        continue
                    n = 2 * sb + i
                    moved = [pltpu.roll(parts[x], (32 * (x - n)) % 128, 1) if x != n else parts[x] for x in range(4)]
                    value = jnp.where(lane < 32, moved[0], jnp.where(lane < 64, moved[1], jnp.where(lane < 96, moved[2], moved[3])))
                    out[mu - 1] = value * (1.0 / SAMPLES)


def sds(*shape, dtype=jnp.float32):
    return jax.ShapeDtypeStruct(shape, dtype)


def around(v, d):
    return lax.ppermute(v, "x", [(i, (i + d) % 4) for i in range(4)])


def copies(v):
    return jnp.broadcast_to(v[None], (8,) + v.shape)


def to_all(v):
    return lax.all_to_all(v, "z", 0, 0, tiled=True)


def local(raw):
    x = lax.axis_index("x")
    me = jnp.stack([x, lax.axis_index("core")]).astype(jnp.int32)
    sent = pl.pallas_call(prepack, out_shape=sds(8, TAU, 768), in_specs=[VMEM], out_specs=VMEM, compiler_params=SMALL, name="prepack")(raw[0])
    got = lax.all_to_all(sent, ("yh", "yl"), 0, 0, tiled=True)
    p_send, rest = pl.pallas_call(
        repack_p,
        out_shape=(sds(8, 2, 2, TAU, 128), sds(8, TAU, 256)),
        in_specs=[VMEM],
        out_specs=(VMEM, VMEM),
        compiler_params=SMALL,
        name="repack_p",
    )(got)
    p_mine = to_all(p_send)
    q_send = pl.pallas_call(
        repack_q,
        out_shape=sds(4, 2, 2, TAU, 128),
        in_specs=[SMEM, VMEM],
        out_specs=VMEM,
        compiler_params=SMALL,
        cost_estimate=pl.CostEstimate(flops=0, bytes_accessed=6 * 10**7, transcendentals=0),
        name="repack_q",
    )(me, rest)
    q_mine = [q_send[0]] + [around(q_send[d], d) for d in (1, 2, 3)]
    p_mine, *q_mine = lax.optimization_barrier((p_mine, *q_mine))
    q_all = to_all(copies(jnp.stack(q_mine)))
    p_all = [p_mine] + [around(p_mine, d) for d in (1, 2, 3)]
    shifted = pl.pallas_call(
        p_side,
        out_shape=sds(2, 2, 512, K, dtype=jnp.bfloat16),
        in_specs=[SMEM] + [VMEM] * 4,
        out_specs=HBM,
        scratch_shapes=[
            pltpu.VMEM((2, SAMPLES, 128), jnp.float32),
            pltpu.VMEM((SAMPLES + 2 * HALF, 256), jnp.bfloat16),
            pltpu.VMEM((SEQ, 128), jnp.float32),
            pltpu.VMEM((128, SEQ), jnp.float32),
            pltpu.VMEM((2, 2, 512, K), jnp.bfloat16),
            pltpu.SemaphoreType.DMA((2,)),
        ],
        compiler_params=pltpu.CompilerParams(vmem_limit_bytes=P_VMEM),
        cost_estimate=pl.CostEstimate(flops=10**9, bytes_accessed=20 * 10**6, transcendentals=0),
        name="p_side",
    )(me, *p_all)
    keep, send = pl.pallas_call(
        correlate,
        out_shape=(sds(4, 8, 2, 16, 128),) * 2,
        in_specs=[SMEM, VMEM, HBM],
        out_specs=(VMEM, VMEM),
        scratch_shapes=[
            pltpu.VMEM((2, SAMPLES, 128), jnp.float32),
            pltpu.VMEM((SAMPLES + 2 * HALF, 256), jnp.bfloat16),
            pltpu.VMEM((2, SEQ, 128), jnp.float32),
            pltpu.VMEM((2, 2, 512, K), jnp.bfloat16),
            pltpu.VMEM((2, K, 512), jnp.bfloat16),
            pltpu.VMEM((2, K, 512), jnp.bfloat16),
            pltpu.VMEM((512, 512), jnp.float32),
            pltpu.SemaphoreType.DMA((2,)),
        ],
        compiler_params=pltpu.CompilerParams(vmem_limit_bytes=Q_VMEM),
        cost_estimate=pl.CostEstimate(flops=10**10, bytes_accessed=20 * 10**6, transcendentals=0),
        name="correlate",
    )(me, q_all, shifted)
    summed = keep + lax.ppermute(send, "core", [(0, 1), (1, 0)])
    mine = lax.all_to_all(summed, "x", 0, 0, tiled=True)
    out = pl.pallas_call(final_kernel, out_shape=sds(LAGS, 16, 128), in_specs=[VMEM], out_specs=VMEM, compiler_params=SMALL, name="finish")(mine)
    return jnp.transpose(out, (1, 0, 2))


def solution(mesh):
    grid = Mesh(mesh.devices.reshape(2, 8, 4, 4, 2), ("yh", "z", "x", "yl", "core"))
    in_specs = (P(("yl", "core"), ("yh", "z", "x"), None),)
    out_specs = P(("yh", "z", "x"), None, ("yl", "core"))
    return jax.shard_map(local, mesh=grid, in_specs=in_specs, out_specs=out_specs, check_vma=False)
```

time: 147 us -> 132 us (0.90)
  Pallas kernels: 39.2 us -> 30.3 us
  blocking collectives: 43.4 us -> 34.8 us
  local copies, waits for them, and re-layouts: 6.23 us -> 2.22 us
  starting transfers between devices: 36.8 us -> 40.8 us
  waiting for transfers between devices: 20 us -> 23.4 us
    all_to_all x1 -> x0, blocking collectives: 9.14 us -> none  [local(): both = lax.all_to_all(part, 'core', 0, 0, tiled=True)]
    pallas_call x4 -> x5, Pallas kernels: 37.3 us -> 30.1 us  [the longest x1 16.1 us: local(): pl.pallas_call(correlate, out_shape=(sds(4, 8, 2, 16, 128),) * 2, in_spec...]
    ppermute x0 -> x1, starting transfers between devices: none -> 5.74 us  [local(): summed = keep + lax.ppermute(send, 'core', [(0, 1), (1, 0)])]
    pallas_call x1 -> x0, local copies, waits for them, and re-layouts: 2.13 us -> none  [local(): pl.pallas_call(final_kernel, out_shape=sds(16, LAGS, 128), in_specs=[VMEM...]
    all_to_all x2, waiting for transfers between devices: 2.1 us -> 3.91 us  [to_all(): return lax.all_to_all(v, 'z', 0, 0, tiled=True)]
    all_to_all x2, starting transfers between devices: 19.6 us -> 17.9 us  [to_all(): return lax.all_to_all(v, 'z', 0, 0, tiled=True)]
    pallas_call x1, Pallas kernels: 1.86 us -> 0.14 us  [local(): pl.pallas_call(prepack, out_shape=sds(8, TAU, 768), in_specs=[VMEM], out_...]
    ppermute x0 -> x1, waiting for transfers between devices: none -> 1.51 us  [local(): summed = keep + lax.ppermute(send, 'core', [(0, 1), (1, 0)])]
  transfers between devices with their start and end apart: 8 -> 9, of which waited for: 6 -> 7; matrix products, arithmetic and copies ran while one was open for 1% -> 0% of each run, Pallas kernels for 8% -> 9%
where the time goes in v5:
time: 132 us
  starting transfers between devices  40.8 us (31%)
  blocking collectives  34.8 us (26%)
  Pallas kernels  30.3 us (23%)
  waiting for transfers between devices  23.4 us (18%)
  local copies, waits for them, and re-layouts  2.22 us (2%)
    all_to_all x1, blocking collectives, local(): got = lax.all_to_all(sent, ('yh', 'yl'), 0, 0, tiled=True)  23.4 us
    ppermute x6, waiting for transfers between devices, around(): return lax.ppermute(v, 'x', [(i, (i + d) % 4) for i in range(4)])  17.9 us
    all_to_all x2, starting transfers between devices, to_all(): return lax.all_to_all(v, 'z', 0, 0, tiled=True)  17.9 us
    ppermute x6, starting transfers between devices, around(): return lax.ppermute(v, 'x', [(i, (i + d) % 4) for i in range(4)])  17.1 us
    pallas_call x1, Pallas kernels, local(): pl.pallas_call(correlate, out_shape=(sds(4, 8, 2, 16, 128),) * 2, in_spec...  16.1 us
    all_to_all x1, blocking collectives, local(): mine = lax.all_to_all(summed, 'x', 0, 0, tiled=True)  11.4 us
    pallas_call x1, Pallas kernels, local(): pl.pallas_call(p_side, out_shape=sds(2, 2, 512, K, dtype=jnp.bfloat16), i...  11.2 us
    ppermute x1, starting transfers between devices, local(): summed = keep + lax.ppermute(send, 'core', [(0, 1), (1, 0)])  5.74 us
  transfers between devices with their start and end apart: 9, of which 7 were waited for; matrix products, arithmetic and copies ran while one was open for 0% of the time, Pallas kernels for 9%

profile of v5, /device:TPU:1, one launch (start us, length us, event | category | flops | bytes accessed | tf_op | source)
XLA Modules:
  0.0 131.7 jit_solution(10613294218280205949)
XLA Ops:
  0.0 0.0 copy-start
  0.0 0.9 copy-done
  0.9 0.1 prepack.1
  1.0 23.4 %all_to_all.20.got = f32[8,24,768]{2,1,0:T(8,128)S(1)} all-to-all(f32[8,24,768]{2,1,0:T(8,128)S(1)} %prepack.1), channel_id=1, replica_groups=mesh['yh'=2,'z'=8,'x'=4,'yl'=4,'core'=2] {'yh','yl'}, dimensions={0} | all-to-all | bytes 1179648 | tf_op jit(solution)/shard_map/all_to_all | solution.py:245
  24.4 0.9 repack_p.1
  25.3 11.6 %all-to-all-start.1 = ((f32[8,2,2,24,128]{4,3,2,1,0:T(8,128)}), f32[8,2,2,24,128]{4,3,2,1,0:T(8,128)S(1)}, u32[]{:S(2)}, u32[]{:S(2)}) async-start(f32[8,2,2,24,128]{4,3,2,1,0:T(8,128)} %get-tuple-element.14), calls=%async_computation.1 | async-start | bytes 786432 | tf_op jit(solution)/shard_map/all_to_all | solution.py:238
  36.9 0.1 pad_add_fusion.me
  37.0 0.7 repack_q.1
  37.6 4.4 %collective-permute-start.2 = (f32[2,2,24,128]{3,2,1,0:T(8,128)S(1)}, f32[2,2,24,128]{3,2,1,0:T(8,128)S(1)}, u32[]{:S(2)}, u32[]{:S(2)}) collective-permute-start(f32[2,2,24,128]{3,2,1,0:T(8,128)S(1)} %get-tuple-element.23), channel_id=1, source_target_pairs={{0,24},{8,0},{16,8},{24,16},{1,25},{9,1},{17,9},{25,17},{2,26},{10... | collective-permute-start | bytes 147464 | tf_op jit(solution)/shard_map/ppermute | solution.py:230
  42.0 2.4 %collective-permute-start.1 = (f32[2,2,24,128]{3,2,1,0:T(8,128)S(1)}, f32[2,2,24,128]{3,2,1,0:T(8,128)S(1)}, u32[]{:S(2)}, u32[]{:S(2)}) collective-permute-start(f32[2,2,24,128]{3,2,1,0:T(8,128)S(1)} %get-tuple-element.24), channel_id=1, source_target_pairs={{0,16},{8,24},{16,0},{24,8},{1,17},{9,25},{17,1},{25,9},{2,18},{10... | collective-permute-start | bytes 147464 | tf_op jit(solution)/shard_map/ppermute | solution.py:230
  44.5 2.5 %collective-permute-start = (f32[2,2,24,128]{3,2,1,0:T(8,128)S(1)}, f32[2,2,24,128]{3,2,1,0:T(8,128)S(1)}, u32[]{:S(2)}, u32[]{:S(2)}) collective-permute-start(f32[2,2,24,128]{3,2,1,0:T(8,128)S(1)} %get-tuple-element.25), channel_id=1, source_target_pairs={{0,8},{8,16},{16,24},{24,0},{1,9},{9,17},{17,25},{25,1},{2,10},{10... | collective-permute-start | bytes 147464 | tf_op jit(solution)/shard_map/ppermute | solution.py:230
  47.0 0.0 collective-permute-done.2
  47.0 1.5 %collective-permute-done.1 = f32[2,2,24,128]{3,2,1,0:T(8,128)S(1)} collective-permute-done((f32[2,2,24,128]{3,2,1,0:T(8,128)S(1)}, f32[2,2,24,128]{3,2,1,0:T(8,128)S(1)}, u32[]{:S(2)}, u32[]{:S(2)}) %collective-permute-start.1) | collective-permute-done | bytes 49184 | tf_op jit(solution)/shard_map/ppermute | solution.py:230
  48.5 2.4 %collective-permute-done = f32[2,2,24,128]{3,2,1,0:T(8,128)S(1)} collective-permute-done((f32[2,2,24,128]{3,2,1,0:T(8,128)S(1)}, f32[2,2,24,128]{3,2,1,0:T(8,128)S(1)}, u32[]{:S(2)}, u32[]{:S(2)}) %collective-permute-start) | collective-permute-done | bytes 49184 | tf_op jit(solution)/shard_map/ppermute | solution.py:230
  50.8 0.0 all-to-all-done.1.p0
  50.8 1.3 broadcast_in_dim.2
  52.1 6.4 %all-to-all-start.2 = ((f32[8,4,2,2,24,128]{5,4,3,2,1,0:T(8,128)}), f32[8,4,2,2,24,128]{5,4,3,2,1,0:T(8,128)S(1)}, u32[]{:S(2)}, u32[]{:S(2)}) async-start(f32[8,4,2,2,24,128]{5,4,3,2,1,0:T(8,128)} %broadcast_in_dim.2), calls=%async_computation.2 | async-start | bytes 3145728 | tf_op jit(solution)/shard_map/all_to_all | solution.py:238
  58.5 2.0 %collective-permute-start.5 = (f32[8,2,2,24,128]{4,3,2,1,0:T(8,128)S(1)}, f32[8,2,2,24,128]{4,3,2,1,0:T(8,128)S(1)}, u32[]{:S(2)}, u32[]{:S(2)}) collective-permute-start(f32[8,2,2,24,128]{4,3,2,1,0:T(8,128)S(1)} %all-to-all-done.1.p0), channel_id=1, source_target_pairs={{0,24},{8,0},{16,8},{24,16},{1,25},{9,1},{17,9},{25,17},{2,26},{10... | collective-permute-start | bytes 1179656 | tf_op jit(solution)/shard_map/ppermute | solution.py:230
  60.5 3.1 %collective-permute-start.4 = (f32[8,2,2,24,128]{4,3,2,1,0:T(8,128)S(1)}, f32[8,2,2,24,128]{4,3,2,1,0:T(8,128)S(1)}, u32[]{:S(2)}, u32[]{:S(2)}) collective-permute-start(f32[8,2,2,24,128]{4,3,2,1,0:T(8,128)S(1)} %all-to-all-done.1.p0), channel_id=1, source_target_pairs={{0,16},{8,24},{16,0},{24,8},{1,17},{9,25},{17,1},{25,9},{2,18},{10... | collective-permute-start | bytes 1179656 | tf_op jit(solution)/shard_map/ppermute | solution.py:230
  63.6 2.8 %collective-permute-start.3 = (f32[8,2,2,24,128]{4,3,2,1,0:T(8,128)S(1)}, f32[8,2,2,24,128]{4,3,2,1,0:T(8,128)S(1)}, u32[]{:S(2)}, u32[]{:S(2)}) collective-permute-start(f32[8,2,2,24,128]{4,3,2,1,0:T(8,128)S(1)} %all-to-all-done.1.p0), channel_id=1, source_target_pairs={{0,8},{8,16},{16,24},{24,0},{1,9},{9,17},{17,25},{25,1},{2,10},{10... | collective-permute-start | bytes 1179656 | tf_op jit(solution)/shard_map/ppermute | solution.py:230
  66.3 1.0 collective-permute-done.5.p3
  67.3 3.5 %collective-permute-done.4.p2 = f32[8,2,2,24,128]{4,3,2,1,0:T(8,128)S(1)} collective-permute-done((f32[8,2,2,24,128]{4,3,2,1,0:T(8,128)S(1)}, f32[8,2,2,24,128]{4,3,2,1,0:T(8,128)S(1)}, u32[]{:S(2)}, u32[]{:S(2)}) %collective-permute-start.4) | collective-permute-done | bytes 393248 | tf_op jit(solution)/shard_map/ppermute | solution.py:230
  70.8 9.7 %collective-permute-done.3.p1 = f32[8,2,2,24,128]{4,3,2,1,0:T(8,128)S(1)} collective-permute-done((f32[8,2,2,24,128]{4,3,2,1,0:T(8,128)S(1)}, f32[8,2,2,24,128]{4,3,2,1,0:T(8,128)S(1)}, u32[]{:S(2)}, u32[]{:S(2)}) %collective-permute-start.3) | collective-permute-done | bytes 393248 | tf_op jit(solution)/shard_map/ppermute | solution.py:230
  80.5 11.2 %p_side.1.p_in = bf16[2,2,512,3328]{3,2,1,0:T(8,128)(2,1)} custom-call(s32[2]{0:T(128)S(1)} %pad_add_fusion.me, f32[8,2,2,24,128]{4,3,2,1,0:T(8,128)S(1)} %all-to-all-done.1.p0, f32[8,2,2,24,128]{4,3,2,1,0:T(8,128)S(1)} %collective-permute-done.3.p1, f32[8,2,2,24,128]{4,3,2,1,0:T(8,128)S(1)} %collective-permute-done.4.p2, ...), custom_call_target="tpu_custom_call" | custom-call | flops 1000000000 | bytes 20000000 | tf_op jit(solution)/shard_map/p_side/pallas_call | solution.py:268
  91.7 3.9 %all-to-all-done.2.q_in = f32[8,4,2,2,24,128]{5,4,3,2,1,0:T(8,128)S(1)} async-done(((f32[8,4,2,2,24,128]{5,4,3,2,1,0:T(8,128)}), f32[8,4,2,2,24,128]{5,4,3,2,1,0:T(8,128)S(1)}, u32[]{:S(2)}, u32[]{:S(2)}) %all-to-all-start.2) | async-done | bytes 1572896 | tf_op jit(solution)/shard_map/all_to_all | solution.py:238
  95.6 16.1 %correlate.1 = (f32[4,8,2,16,128]{4,3,2,1,0:T(8,128)S(1)}, f32[4,8,2,16,128]{4,3,2,1,0:T(8,128)S(1)}) custom-call(s32[2]{0:T(128)S(1)} %pad_add_fusion.me, f32[8,4,2,2,24,128]{5,4,3,2,1,0:T(8,128)S(1)} %all-to-all-done.2.q_in, bf16[2,2,512,3328]{3,2,1,0:T(8,128)(2,1)} %p_side.1.p_in), custom_call_target="tpu_custom_call" | custom-call | flops 10000000000 | bytes 20000000 | tf_op jit(solution)/shard_map/correlate/pallas_call | solution.py:285
  111.7 5.7 %collective-permute-start.6 = (f32[4,8,2,16,128]{4,3,2,1,0:T(8,128)S(1)}, f32[4,8,2,16,128]{4,3,2,1,0:T(8,128)S(1)}, u32[]{:S(2)}, u32[]{:S(2)}) collective-permute-start(f32[4,8,2,16,128]{4,3,2,1,0:T(8,128)S(1)} %get-tuple-element.22), channel_id=1, source_target_pairs={{0,1},{1,0},{2,3},{3,2},{4,5},{5,4},{6,7},{7,6},{8,9},{9,8},{10,11... | collective-permute-start | bytes 1572872 | tf_op jit(solution)/shard_map/ppermute | solution.py:304
  117.5 1.5 %collective-permute-done.6 = f32[4,8,2,16,128]{4,3,2,1,0:T(8,128)S(1)} collective-permute-done((f32[4,8,2,16,128]{4,3,2,1,0:T(8,128)S(1)}, f32[4,8,2,16,128]{4,3,2,1,0:T(8,128)S(1)}, u32[]{:S(2)}, u32[]{:S(2)}) %collective-permute-start.6) | collective-permute-done | bytes 524320 | tf_op jit(solution)/shard_map/ppermute | solution.py:304
  119.0 0.1 add.3
  119.1 11.4 %all_to_all.21.got = f32[4,8,2,16,128]{4,3,2,1,0:T(8,128)S(1)} all-to-all(f32[4,8,2,16,128]{4,3,2,1,0:T(8,128)S(1)} %add.3), channel_id=1, replica_groups=mesh['yh'=2,'z'=8,'x'=4,'yl'=4,'core'=2] {'x'}, dimensions={0} | all-to-all | bytes 1048576 | tf_op jit(solution)/shard_map/all_to_all | solution.py:305
  130.5 1.3 finish.1
  (2 shorter events, 0.0 us)
Async XLA Ops:
  0.0 0.9 copy-start
  25.3 25.5 %all-to-all-start.1 = ((f32[8,2,2,24,128]{4,3,2,1,0:T(8,128)}), f32[8,2,2,24,128]{4,3,2,1,0:T(8,128)S(1)}, u32[]{:S(2)}, u32[]{:S(2)}) async-start(f32[8,2,2,24,128]{4,3,2,1,0:T(8,128)} %get-tuple-element.14), calls=%async_computation.1 | async-start | bytes 786432 | tf_op jit(solution)/shard_map/all_to_all | solution.py:238
  37.6 9.4 %collective-permute-start.2 = (f32[2,2,24,128]{3,2,1,0:T(8,128)S(1)}, f32[2,2,24,128]{3,2,1,0:T(8,128)S(1)}, u32[]{:S(2)}, u32[]{:S(2)}) collective-permute-start(f32[2,2,24,128]{3,2,1,0:T(8,128)S(1)} %get-tuple-element.23), channel_id=1, source_target_pairs={{0,24},{8,0},{16,8},{24,16},{1,25},{9,1},{17,9},{25,17},{2,26},{10... | collective-permute-start | bytes 147464 | tf_op jit(solution)/shard_map/ppermute | solution.py:230
  42.0 6.4 %collective-permute-start.1 = (f32[2,2,24,128]{3,2,1,0:T(8,128)S(1)}, f32[2,2,24,128]{3,2,1,0:T(8,128)S(1)}, u32[]{:S(2)}, u32[]{:S(2)}) collective-permute-start(f32[2,2,24,128]{3,2,1,0:T(8,128)S(1)} %get-tuple-element.24), channel_id=1, source_target_pairs={{0,16},{8,24},{16,0},{24,8},{1,17},{9,25},{17,1},{25,9},{2,18},{10... | collective-permute-start | bytes 147464 | tf_op jit(solution)/shard_map/ppermute | solution.py:230
  44.5 6.3 %collective-permute-start = (f32[2,2,24,128]{3,2,1,0:T(8,128)S(1)}, f32[2,2,24,128]{3,2,1,0:T(8,128)S(1)}, u32[]{:S(2)}, u32[]{:S(2)}) collective-permute-start(f32[2,2,24,128]{3,2,1,0:T(8,128)S(1)} %get-tuple-element.25), channel_id=1, source_target_pairs={{0,8},{8,16},{16,24},{24,0},{1,9},{9,17},{17,25},{25,1},{2,10},{10... | collective-permute-start | bytes 147464 | tf_op jit(solution)/shard_map/ppermute | solution.py:230
  52.1 43.5 %all-to-all-start.2 = ((f32[8,4,2,2,24,128]{5,4,3,2,1,0:T(8,128)}), f32[8,4,2,2,24,128]{5,4,3,2,1,0:T(8,128)S(1)}, u32[]{:S(2)}, u32[]{:S(2)}) async-start(f32[8,4,2,2,24,128]{5,4,3,2,1,0:T(8,128)} %broadcast_in_dim.2), calls=%async_computation.2 | async-start | bytes 3145728 | tf_op jit(solution)/shard_map/all_to_all | solution.py:238
  58.5 8.8 %collective-permute-start.5 = (f32[8,2,2,24,128]{4,3,2,1,0:T(8,128)S(1)}, f32[8,2,2,24,128]{4,3,2,1,0:T(8,128)S(1)}, u32[]{:S(2)}, u32[]{:S(2)}) collective-permute-start(f32[8,2,2,24,128]{4,3,2,1,0:T(8,128)S(1)} %all-to-all-done.1.p0), channel_id=1, source_target_pairs={{0,24},{8,0},{16,8},{24,16},{1,25},{9,1},{17,9},{25,17},{2,26},{10... | collective-permute-start | bytes 1179656 | tf_op jit(solution)/shard_map/ppermute | solution.py:230
  60.5 10.3 %collective-permute-start.4 = (f32[8,2,2,24,128]{4,3,2,1,0:T(8,128)S(1)}, f32[8,2,2,24,128]{4,3,2,1,0:T(8,128)S(1)}, u32[]{:S(2)}, u32[]{:S(2)}) collective-permute-start(f32[8,2,2,24,128]{4,3,2,1,0:T(8,128)S(1)} %all-to-all-done.1.p0), channel_id=1, source_target_pairs={{0,16},{8,24},{16,0},{24,8},{1,17},{9,25},{17,1},{25,9},{2,18},{10... | collective-permute-start | bytes 1179656 | tf_op jit(solution)/shard_map/ppermute | solution.py:230
  63.6 16.9 %collective-permute-start.3 = (f32[8,2,2,24,128]{4,3,2,1,0:T(8,128)S(1)}, f32[8,2,2,24,128]{4,3,2,1,0:T(8,128)S(1)}, u32[]{:S(2)}, u32[]{:S(2)}) collective-permute-start(f32[8,2,2,24,128]{4,3,2,1,0:T(8,128)S(1)} %all-to-all-done.1.p0), channel_id=1, source_target_pairs={{0,8},{8,16},{16,24},{24,0},{1,9},{9,17},{17,25},{25,1},{2,10},{10... | collective-permute-start | bytes 1179656 | tf_op jit(solution)/shard_map/ppermute | solution.py:230
  111.7 7.3 %collective-permute-start.6 = (f32[4,8,2,16,128]{4,3,2,1,0:T(8,128)S(1)}, f32[4,8,2,16,128]{4,3,2,1,0:T(8,128)S(1)}, u32[]{:S(2)}, u32[]{:S(2)}) collective-permute-start(f32[4,8,2,16,128]{4,3,2,1,0:T(8,128)S(1)} %get-tuple-element.22), channel_id=1, source_target_pairs={{0,1},{1,0},{2,3},{3,2},{4,5},{5,4},{6,7},{7,6},{8,9},{9,8},{10,11... | collective-permute-start | bytes 1572872 | tf_op jit(solution)/shard_map/ppermute | solution.py:304

commit v6 on v5

--- a/solution.py
+++ b/solution.py
@@ -19,7 +19,6 @@
 QFRONT = FRONT - 24
 SEQ = K + 128
 CHUNKS = (768, 768, 768, 1024)
-WIDE = 256
 ROT = (4, 8, 36, 40)
 VMEM = pl.BlockSpec(memory_space=pltpu.VMEM)
 HBM = pl.BlockSpec(memory_space=pltpu.HBM)
@@ -114,14 +113,14 @@
 
 
 def moves(from_, to, sems, pair, start):
-    copy = pltpu.make_async_copy(from_.at[pair], to.at[pair], sems.at[pair])
+    copy = pltpu.make_async_copy(from_, to, sems.at[pair])
     if start:
         copy.start()
     else:
         copy.wait()
 
 
-def p_side(me, p0, p1, p2, p3, out, rec, mag, seq, turned, lhs, sems):
+def p_side(me, p0, p1, p2, p3, out, rec, mag, seq, turned, sems):
     for d, ref in enumerate((p0, p1, p2, p3)):
         for high in range(2):
             for z in range(8):
@@ -129,33 +128,26 @@
                     rec[pair, pl.ds(place(me, d, high, z), TAU), :] = ref[z, pair, high]
     normalize(rec, mag)
     for pair in range(2):
-        clear(seq)
+        clear(seq.at[pair])
         for i in range(12):
             x = rec[pair, 128 * i : 128 * i + 128, :]
             r = pltpu.roll(x, 64, 1)
             at = FRONT + 128 * i
-            seq[at : at + 128, 0:64] = x[:, 0:64]
-            seq[at - 16 : at + 112, 64:128] = r[:, 64:128]
+            seq[pair, at : at + 128, 0:64] = x[:, 0:64]
+            seq[pair, at - 16 : at + 112, 64:128] = r[:, 64:128]
             at += ROW
-            seq[at : at + 128, 0:64] = r[:, 0:64]
-            seq[at - 16 : at + 112, 64:128] = x[:, 64:128]
+            seq[pair, at : at + 128, 0:64] = r[:, 0:64]
+            seq[pair, at - 16 : at + 112, 64:128] = x[:, 64:128]
         for i in range(SEQ // 128):
-            turned[:, 128 * i : 128 * i + 128] = seq[128 * i : 128 * i + 128, :].T
-        for at in range(0, K, WIDE):
-            for m in range(8):
-                wide = turned[16 * m : 16 * m + 16, at : at + WIDE + 128]
-                for r, rot in enumerate(ROT):
-                    hi, lo = split(pltpu.roll(wide, WIDE + 128 - rot, 1)[:, 0:WIDE])
-                    lhs[pair, 0, 128 * r + 16 * m : 128 * r + 16 * m + 16, at : at + WIDE] = hi
-                    lhs[pair, 1, 128 * r + 16 * m : 128 * r + 16 * m + 16, at : at + WIDE] = lo
-        moves(lhs, out, sems, pair, True)
-    for pair in range(2):
-        moves(lhs, out, sems, pair, False)
-
-
-def correlate(me, q_in, p_in, keep, send, rec, mag, seq, lhs, rhs_hi, rhs_lo, acc, sems):
-    for pair in range(2):
-        moves(p_in, lhs, sems, pair, True)
+            turned[pair, :, 128 * i : 128 * i + 128] = seq[pair, 128 * i : 128 * i + 128, :].T
+        moves(turned.at[pair], out.at[pair, 0], sems, pair, True)
+    for pair in range(2):
+        moves(turned.at[pair], out.at[pair, 0], sems, pair, False)
+
+
+def correlate(me, q_in, p_in, keep, send, rec, mag, seq, turned, lhs_hi, lhs_lo, rhs_hi, rhs_lo, acc, sems):
+    for pair in range(2):
+        moves(p_in.at[pair, 0], turned.at[pair], sems, pair, True)
     for d in range(4):
         for high in range(2):
             for z in range(8):
@@ -172,9 +164,15 @@
                 for n, part in enumerate(parts):
                     to = at + e * ROW - 8 * (n % 2)
                     seq[pair, to : to + 128, 32 * n : 32 * n + 32] = part[:, 32 * n : 32 * n + 32]
-        moves(p_in, lhs, sems, pair, False)
+        moves(p_in.at[pair, 0], turned.at[pair], sems, pair, False)
         start = 0
         for n, width in enumerate(CHUNKS):
+            for m in range(8):
+                wide = turned[pair, 16 * m : 16 * m + 16, start : start + width + 128]
+                for r, rot in enumerate(ROT):
+                    hi, lo = split(pltpu.roll(wide, width + 128 - rot, 1)[:, 0:width])
+                    lhs_hi[pair, 128 * r + 16 * m : 128 * r + 16 * m + 16, start : start + width] = hi
+                    lhs_lo[pair, 128 * r + 16 * m : 128 * r + 16 * m + 16, start : start + width] = lo
             for s in range(4):
                 for m in range(width // 128):
                     at = start + 128 * m
@@ -182,9 +180,9 @@
                     rhs_hi[pair, at : at + 128, 128 * s : 128 * s + 128] = hi
                     rhs_lo[pair, at : at + 128, 128 * s : 128 * s + 128] = lo
             span = slice(start, start + width)
-            part = jnp.dot(lhs[pair, 0, :, span], rhs_hi[pair, span, :], preferred_element_type=jnp.float32)
-            part += jnp.dot(lhs[pair, 0, :, span], rhs_lo[pair, span, :], preferred_element_type=jnp.float32)
-            part += jnp.dot(lhs[pair, 1, :, span], rhs_hi[pair, span, :], preferred_element_type=jnp.float32)
+            part = jnp.dot(lhs_hi[pair, :, span], rhs_hi[pair, span, :], preferred_element_type=jnp.float32)
+            part += jnp.dot(lhs_hi[pair, :, span], rhs_lo[pair, span, :], preferred_element_type=jnp.float32)
+            part += jnp.dot(lhs_lo[pair, :, span], rhs_hi[pair, span, :], preferred_element_type=jnp.float32)
             if n or pair:
                 acc[...] += part
             else:
@@ -265,17 +263,16 @@
     p_mine, *q_mine = lax.optimization_barrier((p_mine, *q_mine))
     q_all = to_all(copies(jnp.stack(q_mine)))
     p_all = [p_mine] + [around(p_mine, d) for d in (1, 2, 3)]
-    shifted = pl.pallas_call(
+    p_done = pl.pallas_call(
         p_side,
-        out_shape=sds(2, 2, 512, K, dtype=jnp.bfloat16),
+        out_shape=sds(2, 4, 128, SEQ),
         in_specs=[SMEM] + [VMEM] * 4,
         out_specs=HBM,
         scratch_shapes=[
             pltpu.VMEM((2, SAMPLES, 128), jnp.float32),
             pltpu.VMEM((SAMPLES + 2 * HALF, 256), jnp.bfloat16),
-            pltpu.VMEM((SEQ, 128), jnp.float32),
-            pltpu.VMEM((128, SEQ), jnp.float32),
-            pltpu.VMEM((2, 2, 512, K), jnp.bfloat16),
+            pltpu.VMEM((2, SEQ, 128), jnp.float32),
+            pltpu.VMEM((2, 128, SEQ), jnp.float32),
             pltpu.SemaphoreType.DMA((2,)),
         ],
         compiler_params=pltpu.CompilerParams(vmem_limit_bytes=P_VMEM),
@@ -291,7 +288,9 @@
             pltpu.VMEM((2, SAMPLES, 128), jnp.float32),
             pltpu.VMEM((SAMPLES + 2 * HALF, 256), jnp.bfloat16),
             pltpu.VMEM((2, SEQ, 128), jnp.float32),
-            pltpu.VMEM((2, 2, 512, K), jnp.bfloat16),
+            pltpu.VMEM((2, 128, SEQ), jnp.float32),
+            pltpu.VMEM((2, 512, K), jnp.bfloat16),
+            pltpu.VMEM((2, 512, K), jnp.bfloat16),
             pltpu.VMEM((2, K, 512), jnp.bfloat16),
             pltpu.VMEM((2, K, 512), jnp.bfloat16),
             pltpu.VMEM((512, 512), jnp.float32),
@@ -300,7 +299,7 @@
         compiler_params=pltpu.CompilerParams(vmem_limit_bytes=Q_VMEM),
         cost_estimate=pl.CostEstimate(flops=10**10, bytes_accessed=20 * 10**6, transcendentals=0),
         name="correlate",
-    )(me, q_all, shifted)
+    )(me, q_all, p_done)
     summed = keep + lax.ppermute(send, "core", [(0, 1), (1, 0)])
     mine = lax.all_to_all(summed, "x", 0, 0, tiled=True)
     out = pl.pallas_call(final_kernel, out_shape=sds(LAGS, 16, 128), in_specs=[VMEM], out_specs=VMEM, compiler_params=SMALL, name="finish")(mine)

time: 132 us -> 131 us (level)
  Pallas kernels: 30.3 us -> 22.7 us
  waiting for transfers between devices: 23.4 us -> 29.9 us
    all_to_all x2, waiting for transfers between devices: 3.91 us -> 10.5 us  [to_all(): return lax.all_to_all(v, 'z', 0, 0, tiled=True)]
    pallas_call x1, Pallas kernels: 11.2 us -> 4.71 us  [local(): pl.pallas_call(p_side, out_shape=sds(2, 4, 128, SEQ), in_specs=[SMEM] + [...]
  transfers between devices with their start and end apart: 9 -> 9, of which waited for: 7 -> 7; matrix products, arithmetic and copies ran while one was open for 0% -> 0% of each run, Pallas kernels for 9% -> 4%
where the time goes in v6:
time: 131 us
  starting transfers between devices  40.8 us (31%)
  blocking collectives  34.8 us (27%)
  waiting for transfers between devices  29.9 us (23%)
  Pallas kernels  22.7 us (17%)
  local copies, waits for them, and re-layouts  2.23 us (2%)
    all_to_all x1, blocking collectives, local(): got = lax.all_to_all(sent, ('yh', 'yl'), 0, 0, tiled=True)  23.4 us
    ppermute x6, waiting for transfers between devices, around(): return lax.ppermute(v, 'x', [(i, (i + d) % 4) for i in range(4)])  17.9 us
    all_to_all x2, starting transfers between devices, to_all(): return lax.all_to_all(v, 'z', 0, 0, tiled=True)  17.9 us
    ppermute x6, starting transfers between devices, around(): return lax.ppermute(v, 'x', [(i, (i + d) % 4) for i in range(4)])  17.1 us
    pallas_call x1, Pallas kernels, local(): pl.pallas_call(correlate, out_shape=(sds(4, 8, 2, 16, 128),) * 2, in_spec...  15 us
    all_to_all x1, blocking collectives, local(): mine = lax.all_to_all(summed, 'x', 0, 0, tiled=True)  11.4 us
    all_to_all x2, waiting for transfers between devices, to_all(): return lax.all_to_all(v, 'z', 0, 0, tiled=True)  10.5 us
    ppermute x1, starting transfers between devices, local(): summed = keep + lax.ppermute(send, 'core', [(0, 1), (1, 0)])  5.74 us
  transfers between devices with their start and end apart: 9, of which 7 were waited for; matrix products, arithmetic and copies ran while one was open for 0% of the time, Pallas kernels for 4%

profile of v6, /device:TPU:1, one launch (start us, length us, event | category | flops | bytes accessed | tf_op | source)
XLA Modules:
  0.0 130.7 jit_solution(12542772997762897337)
XLA Ops:
  0.0 0.0 copy-start
  0.0 0.9 copy-done
  0.9 0.1 prepack.1
  1.0 23.4 %all_to_all.20.got = f32[8,24,768]{2,1,0:T(8,128)S(1)} all-to-all(f32[8,24,768]{2,1,0:T(8,128)S(1)} %prepack.1), channel_id=1, replica_groups=mesh['yh'=2,'z'=8,'x'=4,'yl'=4,'core'=2] {'yh','yl'}, dimensions={0} | all-to-all | bytes 1179648 | tf_op jit(solution)/shard_map/all_to_all | solution.py:243
  24.4 0.9 repack_p.1
  25.3 11.6 %all-to-all-start.1 = ((f32[8,2,2,24,128]{4,3,2,1,0:T(8,128)}), f32[8,2,2,24,128]{4,3,2,1,0:T(8,128)S(1)}, u32[]{:S(2)}, u32[]{:S(2)}) async-start(f32[8,2,2,24,128]{4,3,2,1,0:T(8,128)} %get-tuple-element.14), calls=%async_computation.1 | async-start | bytes 786432 | tf_op jit(solution)/shard_map/all_to_all | solution.py:236
  36.9 0.1 pad_add_fusion.me
  37.0 0.7 repack_q.1
  37.6 4.4 %collective-permute-start.2 = (f32[2,2,24,128]{3,2,1,0:T(8,128)S(1)}, f32[2,2,24,128]{3,2,1,0:T(8,128)S(1)}, u32[]{:S(2)}, u32[]{:S(2)}) collective-permute-start(f32[2,2,24,128]{3,2,1,0:T(8,128)S(1)} %get-tuple-element.23), channel_id=1, source_target_pairs={{0,24},{8,0},{16,8},{24,16},{1,25},{9,1},{17,9},{25,17},{2,26},{10... | collective-permute-start | bytes 147464 | tf_op jit(solution)/shard_map/ppermute | solution.py:228
  42.0 2.4 %collective-permute-start.1 = (f32[2,2,24,128]{3,2,1,0:T(8,128)S(1)}, f32[2,2,24,128]{3,2,1,0:T(8,128)S(1)}, u32[]{:S(2)}, u32[]{:S(2)}) collective-permute-start(f32[2,2,24,128]{3,2,1,0:T(8,128)S(1)} %get-tuple-element.24), channel_id=1, source_target_pairs={{0,16},{8,24},{16,0},{24,8},{1,17},{9,25},{17,1},{25,9},{2,18},{10... | collective-permute-start | bytes 147464 | tf_op jit(solution)/shard_map/ppermute | solution.py:228
  44.5 2.5 %collective-permute-start = (f32[2,2,24,128]{3,2,1,0:T(8,128)S(1)}, f32[2,2,24,128]{3,2,1,0:T(8,128)S(1)}, u32[]{:S(2)}, u32[]{:S(2)}) collective-permute-start(f32[2,2,24,128]{3,2,1,0:T(8,128)S(1)} %get-tuple-element.25), channel_id=1, source_target_pairs={{0,8},{8,16},{16,24},{24,0},{1,9},{9,17},{17,25},{25,1},{2,10},{10... | collective-permute-start | bytes 147464 | tf_op jit(solution)/shard_map/ppermute | solution.py:228
  47.0 0.0 collective-permute-done.2
  47.0 1.5 %collective-permute-done.1 = f32[2,2,24,128]{3,2,1,0:T(8,128)S(1)} collective-permute-done((f32[2,2,24,128]{3,2,1,0:T(8,128)S(1)}, f32[2,2,24,128]{3,2,1,0:T(8,128)S(1)}, u32[]{:S(2)}, u32[]{:S(2)}) %collective-permute-start.1) | collective-permute-done | bytes 49184 | tf_op jit(solution)/shard_map/ppermute | solution.py:228
  48.5 2.4 %collective-permute-done = f32[2,2,24,128]{3,2,1,0:T(8,128)S(1)} collective-permute-done((f32[2,2,24,128]{3,2,1,0:T(8,128)S(1)}, f32[2,2,24,128]{3,2,1,0:T(8,128)S(1)}, u32[]{:S(2)}, u32[]{:S(2)}) %collective-permute-start) | collective-permute-done | bytes 49184 | tf_op jit(solution)/shard_map/ppermute | solution.py:228
  50.8 0.0 all-to-all-done.1.p0
  50.8 1.3 %broadcast_in_dim.2 = f32[8,4,2,2,24,128]{5,4,3,2,1,0:T(8,128)} broadcast(f32[4,2,2,24,128]{4,3,2,1,0:T(8,128)S(1)} %pad_maximum_fusion), dimensions={1,2,3,4,5} | broadcast | bytes 1769472 | tf_op jit(solution)/shard_map/broadcast_in_dim | solution.py:232
  52.2 6.4 %all-to-all-start.2 = ((f32[8,4,2,2,24,128]{5,4,3,2,1,0:T(8,128)}), f32[8,4,2,2,24,128]{5,4,3,2,1,0:T(8,128)S(1)}, u32[]{:S(2)}, u32[]{:S(2)}) async-start(f32[8,4,2,2,24,128]{5,4,3,2,1,0:T(8,128)} %broadcast_in_dim.2), calls=%async_computation.2 | async-start | bytes 3145728 | tf_op jit(solution)/shard_map/all_to_all | solution.py:236
  58.5 2.0 %collective-permute-start.5 = (f32[8,2,2,24,128]{4,3,2,1,0:T(8,128)S(1)}, f32[8,2,2,24,128]{4,3,2,1,0:T(8,128)S(1)}, u32[]{:S(2)}, u32[]{:S(2)}) collective-permute-start(f32[8,2,2,24,128]{4,3,2,1,0:T(8,128)S(1)} %all-to-all-done.1.p0), channel_id=1, source_target_pairs={{0,24},{8,0},{16,8},{24,16},{1,25},{9,1},{17,9},{25,17},{2,26},{10... | collective-permute-start | bytes 1179656 | tf_op jit(solution)/shard_map/ppermute | solution.py:228
  60.5 3.1 %collective-permute-start.4 = (f32[8,2,2,24,128]{4,3,2,1,0:T(8,128)S(1)}, f32[8,2,2,24,128]{4,3,2,1,0:T(8,128)S(1)}, u32[]{:S(2)}, u32[]{:S(2)}) collective-permute-start(f32[8,2,2,24,128]{4,3,2,1,0:T(8,128)S(1)} %all-to-all-done.1.p0), channel_id=1, source_target_pairs={{0,16},{8,24},{16,0},{24,8},{1,17},{9,25},{17,1},{25,9},{2,18},{10... | collective-permute-start | bytes 1179656 | tf_op jit(solution)/shard_map/ppermute | solution.py:228
  63.6 2.8 %collective-permute-start.3 = (f32[8,2,2,24,128]{4,3,2,1,0:T(8,128)S(1)}, f32[8,2,2,24,128]{4,3,2,1,0:T(8,128)S(1)}, u32[]{:S(2)}, u32[]{:S(2)}) collective-permute-start(f32[8,2,2,24,128]{4,3,2,1,0:T(8,128)S(1)} %all-to-all-done.1.p0), channel_id=1, source_target_pairs={{0,8},{8,16},{16,24},{24,0},{1,9},{9,17},{17,25},{25,1},{2,10},{10... | collective-permute-start | bytes 1179656 | tf_op jit(solution)/shard_map/ppermute | solution.py:228
  66.3 1.0 collective-permute-done.5.p3
  67.3 3.5 %collective-permute-done.4.p2 = f32[8,2,2,24,128]{4,3,2,1,0:T(8,128)S(1)} collective-permute-done((f32[8,2,2,24,128]{4,3,2,1,0:T(8,128)S(1)}, f32[8,2,2,24,128]{4,3,2,1,0:T(8,128)S(1)}, u32[]{:S(2)}, u32[]{:S(2)}) %collective-permute-start.4) | collective-permute-done | bytes 393248 | tf_op jit(solution)/shard_map/ppermute | solution.py:228
  70.8 9.7 %collective-permute-done.3.p1 = f32[8,2,2,24,128]{4,3,2,1,0:T(8,128)S(1)} collective-permute-done((f32[8,2,2,24,128]{4,3,2,1,0:T(8,128)S(1)}, f32[8,2,2,24,128]{4,3,2,1,0:T(8,128)S(1)}, u32[]{:S(2)}, u32[]{:S(2)}) %collective-permute-start.3) | collective-permute-done | bytes 393248 | tf_op jit(solution)/shard_map/ppermute | solution.py:228
  80.5 4.7 %p_side.1.p_in = f32[2,4,128,3456]{3,2,1,0:T(8,128)} custom-call(s32[2]{0:T(128)S(1)} %pad_add_fusion.me, f32[8,2,2,24,128]{4,3,2,1,0:T(8,128)S(1)} %all-to-all-done.1.p0, f32[8,2,2,24,128]{4,3,2,1,0:T(8,128)S(1)} %collective-permute-done.3.p1, f32[8,2,2,24,128]{4,3,2,1,0:T(8,128)S(1)} %collective-permute-done.4.p2, ...), custom_call_target="tpu_custom_call" | custom-call | flops 1000000000 | bytes 20000000 | tf_op jit(solution)/shard_map/p_side/pallas_call | solution.py:266
  85.2 10.4 %all-to-all-done.2.q_in = f32[8,4,2,2,24,128]{5,4,3,2,1,0:T(8,128)S(1)} async-done(((f32[8,4,2,2,24,128]{5,4,3,2,1,0:T(8,128)}), f32[8,4,2,2,24,128]{5,4,3,2,1,0:T(8,128)S(1)}, u32[]{:S(2)}, u32[]{:S(2)}) %all-to-all-start.2) | async-done | bytes 1572896 | tf_op jit(solution)/shard_map/all_to_all | solution.py:236
  95.6 15.0 %correlate.1 = (f32[4,8,2,16,128]{4,3,2,1,0:T(8,128)S(1)}, f32[4,8,2,16,128]{4,3,2,1,0:T(8,128)S(1)}) custom-call(s32[2]{0:T(128)S(1)} %pad_add_fusion.me, f32[8,4,2,2,24,128]{5,4,3,2,1,0:T(8,128)S(1)} %all-to-all-done.2.q_in, f32[2,4,128,3456]{3,2,1,0:T(8,128)} %p_side.1.p_in), custom_call_target="tpu_custom_call" | custom-call | flops 10000000000 | bytes 20000000 | tf_op jit(solution)/shard_map/correlate/pallas_call | solution.py:282
  110.7 5.7 %collective-permute-start.6 = (f32[4,8,2,16,128]{4,3,2,1,0:T(8,128)S(1)}, f32[4,8,2,16,128]{4,3,2,1,0:T(8,128)S(1)}, u32[]{:S(2)}, u32[]{:S(2)}) collective-permute-start(f32[4,8,2,16,128]{4,3,2,1,0:T(8,128)S(1)} %get-tuple-element.22), channel_id=1, source_target_pairs={{0,1},{1,0},{2,3},{3,2},{4,5},{5,4},{6,7},{7,6},{8,9},{9,8},{10,11... | collective-permute-start | bytes 1572872 | tf_op jit(solution)/shard_map/ppermute | solution.py:303
  116.4 1.5 %collective-permute-done.6 = f32[4,8,2,16,128]{4,3,2,1,0:T(8,128)S(1)} collective-permute-done((f32[4,8,2,16,128]{4,3,2,1,0:T(8,128)S(1)}, f32[4,8,2,16,128]{4,3,2,1,0:T(8,128)S(1)}, u32[]{:S(2)}, u32[]{:S(2)}) %collective-permute-start.6) | collective-permute-done | bytes 524320 | tf_op jit(solution)/shard_map/ppermute | solution.py:303
  117.9 0.1 add.3
  118.0 11.4 %all_to_all.21.got = f32[4,8,2,16,128]{4,3,2,1,0:T(8,128)S(1)} all-to-all(f32[4,8,2,16,128]{4,3,2,1,0:T(8,128)S(1)} %add.3), channel_id=1, replica_groups=mesh['yh'=2,'z'=8,'x'=4,'yl'=4,'core'=2] {'x'}, dimensions={0} | all-to-all | bytes 1048576 | tf_op jit(solution)/shard_map/all_to_all | solution.py:304
  129.4 1.3 finish.1
  (2 shorter events, 0.0 us)
Async XLA Ops:
  0.0 0.9 copy-start
  25.3 25.5 %all-to-all-start.1 = ((f32[8,2,2,24,128]{4,3,2,1,0:T(8,128)}), f32[8,2,2,24,128]{4,3,2,1,0:T(8,128)S(1)}, u32[]{:S(2)}, u32[]{:S(2)}) async-start(f32[8,2,2,24,128]{4,3,2,1,0:T(8,128)} %get-tuple-element.14), calls=%async_computation.1 | async-start | bytes 786432 | tf_op jit(solution)/shard_map/all_to_all | solution.py:236
  37.6 9.4 %collective-permute-start.2 = (f32[2,2,24,128]{3,2,1,0:T(8,128)S(1)}, f32[2,2,24,128]{3,2,1,0:T(8,128)S(1)}, u32[]{:S(2)}, u32[]{:S(2)}) collective-permute-start(f32[2,2,24,128]{3,2,1,0:T(8,128)S(1)} %get-tuple-element.23), channel_id=1, source_target_pairs={{0,24},{8,0},{16,8},{24,16},{1,25},{9,1},{17,9},{25,17},{2,26},{10... | collective-permute-start | bytes 147464 | tf_op jit(solution)/shard_map/ppermute | solution.py:228
  42.0 6.4 %collective-permute-start.1 = (f32[2,2,24,128]{3,2,1,0:T(8,128)S(1)}, f32[2,2,24,128]{3,2,1,0:T(8,128)S(1)}, u32[]{:S(2)}, u32[]{:S(2)}) collective-permute-start(f32[2,2,24,128]{3,2,1,0:T(8,128)S(1)} %get-tuple-element.24), channel_id=1, source_target_pairs={{0,16},{8,24},{16,0},{24,8},{1,17},{9,25},{17,1},{25,9},{2,18},{10... | collective-permute-start | bytes 147464 | tf_op jit(solution)/shard_map/ppermute | solution.py:228
  44.5 6.3 %collective-permute-start = (f32[2,2,24,128]{3,2,1,0:T(8,128)S(1)}, f32[2,2,24,128]{3,2,1,0:T(8,128)S(1)}, u32[]{:S(2)}, u32[]{:S(2)}) collective-permute-start(f32[2,2,24,128]{3,2,1,0:T(8,128)S(1)} %get-tuple-element.25), channel_id=1, source_target_pairs={{0,8},{8,16},{16,24},{24,0},{1,9},{9,17},{17,25},{25,1},{2,10},{10... | collective-permute-start | bytes 147464 | tf_op jit(solution)/shard_map/ppermute | solution.py:228
  52.2 43.5 %all-to-all-start.2 = ((f32[8,4,2,2,24,128]{5,4,3,2,1,0:T(8,128)}), f32[8,4,2,2,24,128]{5,4,3,2,1,0:T(8,128)S(1)}, u32[]{:S(2)}, u32[]{:S(2)}) async-start(f32[8,4,2,2,24,128]{5,4,3,2,1,0:T(8,128)} %broadcast_in_dim.2), calls=%async_computation.2 | async-start | bytes 3145728 | tf_op jit(solution)/shard_map/all_to_all | solution.py:236
  58.5 8.8 %collective-permute-start.5 = (f32[8,2,2,24,128]{4,3,2,1,0:T(8,128)S(1)}, f32[8,2,2,24,128]{4,3,2,1,0:T(8,128)S(1)}, u32[]{:S(2)}, u32[]{:S(2)}) collective-permute-start(f32[8,2,2,24,128]{4,3,2,1,0:T(8,128)S(1)} %all-to-all-done.1.p0), channel_id=1, source_target_pairs={{0,24},{8,0},{16,8},{24,16},{1,25},{9,1},{17,9},{25,17},{2,26},{10... | collective-permute-start | bytes 1179656 | tf_op jit(solution)/shard_map/ppermute | solution.py:228
  60.5 10.3 %collective-permute-start.4 = (f32[8,2,2,24,128]{4,3,2,1,0:T(8,128)S(1)}, f32[8,2,2,24,128]{4,3,2,1,0:T(8,128)S(1)}, u32[]{:S(2)}, u32[]{:S(2)}) collective-permute-start(f32[8,2,2,24,128]{4,3,2,1,0:T(8,128)S(1)} %all-to-all-done.1.p0), channel_id=1, source_target_pairs={{0,16},{8,24},{16,0},{24,8},{1,17},{9,25},{17,1},{25,9},{2,18},{10... | collective-permute-start | bytes 1179656 | tf_op jit(solution)/shard_map/ppermute | solution.py:228
  63.6 16.9 %collective-permute-start.3 = (f32[8,2,2,24,128]{4,3,2,1,0:T(8,128)S(1)}, f32[8,2,2,24,128]{4,3,2,1,0:T(8,128)S(1)}, u32[]{:S(2)}, u32[]{:S(2)}) collective-permute-start(f32[8,2,2,24,128]{4,3,2,1,0:T(8,128)S(1)} %all-to-all-done.1.p0), channel_id=1, source_target_pairs={{0,8},{8,16},{16,24},{24,0},{1,9},{9,17},{17,25},{25,1},{2,10},{10... | collective-permute-start | bytes 1179656 | tf_op jit(solution)/shard_map/ppermute | solution.py:228
  110.7 7.3 %collective-permute-start.6 = (f32[4,8,2,16,128]{4,3,2,1,0:T(8,128)S(1)}, f32[4,8,2,16,128]{4,3,2,1,0:T(8,128)S(1)}, u32[]{:S(2)}, u32[]{:S(2)}) collective-permute-start(f32[4,8,2,16,128]{4,3,2,1,0:T(8,128)S(1)} %get-tuple-element.22), channel_id=1, source_target_pairs={{0,1},{1,0},{2,3},{3,2},{4,5},{5,4},{6,7},{7,6},{8,9},{9,8},{10,11... | collective-permute-start | bytes 1572872 | tf_op jit(solution)/shard_map/ppermute | solution.py:303

commit v7 on v6

--- a/solution.py
+++ b/solution.py
@@ -14,11 +14,11 @@
 
 TAU = 24
 ROW = SAMPLES + 32
-K = 3328
+K = 3200
 FRONT = 40
 QFRONT = FRONT - 24
 SEQ = K + 128
-CHUNKS = (768, 768, 768, 1024)
+CHUNKS = (1024, 1024, 1152)
 ROT = (4, 8, 36, 40)
 VMEM = pl.BlockSpec(memory_space=pltpu.VMEM)
 HBM = pl.BlockSpec(memory_space=pltpu.HBM)
@@ -56,20 +56,14 @@
     return jnp.where(low, a, pltpu.roll(b, 64, 1)), jnp.where(low, pltpu.roll(a, 64, 1), b)
 
 
-def repack_p(got, out, rest):
+def repack(me, got, p_out, q_out):
     for high in range(2):
         for pair in range(2):
             for v in range(4):
-                out[2 * v, pair, high], out[2 * v + 1, pair, high] = pairs(got, high, pair, 128 * v)
-    rest[...] = got[:, :, 512:768]
-
-
-def repack_q(me, got, out):
-    for high in range(2):
-        for pair in range(2):
+                p_out[2 * v, pair, high], p_out[2 * v + 1, pair, high] = pairs(got, high, pair, 128 * v)
             for v in range(2):
-                for n, block in enumerate(pairs(got, high, pair, 128 * v)):
-                    out[lax.rem(2 * v + n + 4 - me[0], 4), pair, high] = block
+                for n, block in enumerate(pairs(got, high, pair, 512 + 128 * v)):
+                    q_out[lax.rem(2 * v + n + 4 - me[0], 4), pair, high] = block
 
 
 def split(x):
@@ -241,24 +235,15 @@
     me = jnp.stack([x, lax.axis_index("core")]).astype(jnp.int32)
     sent = pl.pallas_call(prepack, out_shape=sds(8, TAU, 768), in_specs=[VMEM], out_specs=VMEM, compiler_params=SMALL, name="prepack")(raw[0])
     got = lax.all_to_all(sent, ("yh", "yl"), 0, 0, tiled=True)
-    p_send, rest = pl.pallas_call(
-        repack_p,
-        out_shape=(sds(8, 2, 2, TAU, 128), sds(8, TAU, 256)),
-        in_specs=[VMEM],
+    p_send, q_send = pl.pallas_call(
+        repack,
+        out_shape=(sds(8, 2, 2, TAU, 128), sds(4, 2, 2, TAU, 128)),
+        in_specs=[SMEM, VMEM],
         out_specs=(VMEM, VMEM),
         compiler_params=SMALL,
-        name="repack_p",
-    )(got)
+        name="repack",
+    )(me, got)
     p_mine = to_all(p_send)
-    q_send = pl.pallas_call(
-        repack_q,
-        out_shape=sds(4, 2, 2, TAU, 128),
-        in_specs=[SMEM, VMEM],
-        out_specs=VMEM,
-        compiler_params=SMALL,
-        cost_estimate=pl.CostEstimate(flops=0, bytes_accessed=6 * 10**7, transcendentals=0),
-        name="repack_q",
-    )(me, rest)
     q_mine = [q_send[0]] + [around(q_send[d], d) for d in (1, 2, 3)]
     p_mine, *q_mine = lax.optimization_barrier((p_mine, *q_mine))
     q_all = to_all(copies(jnp.stack(q_mine)))

time: 131 us -> 134 us (1.023)
  blocking collectives: 34.8 us -> 11.1 us
  waiting for transfers between devices: 29.9 us -> 51.3 us
  starting transfers between devices: 40.8 us -> 45.2 us
    all_to_all x1 -> x0, blocking collectives: 23.4 us -> none  [local(): got = lax.all_to_all(sent, ('yh', 'yl'), 0, 0, tiled=True)]
    all_to_all x0 -> x1, waiting for transfers between devices: none -> 16.4 us  [local(): got = lax.all_to_all(sent, ('yh', 'yl'), 0, 0, tiled=True)]
    all_to_all x0 -> x1, starting transfers between devices: none -> 7.65 us  [local(): got = lax.all_to_all(sent, ('yh', 'yl'), 0, 0, tiled=True)]
    ppermute x6, waiting for transfers between devices: 17.9 us -> 21.8 us  [around(): return lax.ppermute(v, 'x', [(i, (i + d) % 4) for i in range(4)])]
    ppermute x1, starting transfers between devices: 5.74 us -> 2.39 us  [local(): summed = keep + lax.ppermute(send, 'core', [(0, 1), (1, 0)])]
  transfers between devices with their start and end apart: 9 -> 10, of which waited for: 7 -> 9; matrix products, arithmetic and copies ran while one was open for 0% -> 0% of each run, Pallas kernels for 4% -> 3%
where the time goes in v7:
time: 134 us
  waiting for transfers between devices  51.3 us (38%)
  starting transfers between devices  45.2 us (34%)
  Pallas kernels  23.5 us (18%)
  blocking collectives  11.1 us (8%)
  local copies, waits for them, and re-layouts  2.25 us (2%)
    ppermute x6, waiting for transfers between devices, around(): return lax.ppermute(v, 'x', [(i, (i + d) % 4) for i in range(4)])  21.8 us
    all_to_all x2, starting transfers between devices, to_all(): return lax.all_to_all(v, 'z', 0, 0, tiled=True)  17.7 us
    ppermute x6, starting transfers between devices, around(): return lax.ppermute(v, 'x', [(i, (i + d) % 4) for i in range(4)])  17.4 us
    all_to_all x1, waiting for transfers between devices, local(): got = lax.all_to_all(sent, ('yh', 'yl'), 0, 0, tiled=True)  16.4 us
    pallas_call x1, Pallas kernels, local(): pl.pallas_call(correlate, out_shape=(sds(4, 8, 2, 16, 128),) * 2, in_spec...  15.2 us
    all_to_all x2, waiting for transfers between devices, to_all(): return lax.all_to_all(v, 'z', 0, 0, tiled=True)  11.6 us
    all_to_all x1, blocking collectives, local(): mine = lax.all_to_all(summed, 'x', 0, 0, tiled=True)  11.1 us
    all_to_all x1, starting transfers between devices, local(): got = lax.all_to_all(sent, ('yh', 'yl'), 0, 0, tiled=True)  7.65 us
  transfers between devices with their start and end apart: 10, of which 9 were waited for; matrix products, arithmetic and copies ran while one was open for 0% of the time, Pallas kernels for 3%

profile of v7, /device:TPU:1, one launch (start us, length us, event | category | flops | bytes accessed | tf_op | source)
XLA Modules:
  0.0 133.6 jit_solution(10538691679596267428)
XLA Ops:
  0.0 0.0 copy-start
  0.0 0.9 copy-done
  0.9 1.0 prepack.1
  1.9 7.7 %all-to-all-start = ((f32[8,24,768]{2,1,0:T(8,128)}), f32[8,24,768]{2,1,0:T(8,128)S(1)}, u32[]{:S(2)}, u32[]{:S(2)}) async-start(f32[8,24,768]{2,1,0:T(8,128)} %prepack.1), calls=%async_computation | async-start | bytes 1179648 | tf_op jit(solution)/shard_map/all_to_all | solution.py:237
  9.5 0.1 pad_add_fusion.me
  9.6 16.4 %all-to-all-done.got = f32[8,24,768]{2,1,0:T(8,128)S(1)} async-done(((f32[8,24,768]{2,1,0:T(8,128)}), f32[8,24,768]{2,1,0:T(8,128)S(1)}, u32[]{:S(2)}, u32[]{:S(2)}) %all-to-all-start) | async-done | bytes 589856 | tf_op jit(solution)/shard_map/all_to_all | solution.py:237
  26.0 1.5 %repack.1 = (f32[8,2,2,24,128]{4,3,2,1,0:T(8,128)}, f32[4,2,2,24,128]{4,3,2,1,0:T(8,128)S(1)}) custom-call(s32[2]{0:T(128)S(1)} %pad_add_fusion.me, f32[8,24,768]{2,1,0:T(8,128)S(1)} %all-to-all-done.got), custom_call_target="tpu_custom_call" | custom-call | tf_op jit(solution)/shard_map/repack/pallas_call | solution.py:238
  27.5 12.9 %all-to-all-start.1 = ((f32[8,2,2,24,128]{4,3,2,1,0:T(8,128)}), f32[8,2,2,24,128]{4,3,2,1,0:T(8,128)S(1)}, u32[]{:S(2)}, u32[]{:S(2)}) async-start(f32[8,2,2,24,128]{4,3,2,1,0:T(8,128)} %get-tuple-element.14), calls=%async_computation.1 | async-start | bytes 786432 | tf_op jit(solution)/shard_map/all_to_all | solution.py:230
  40.4 4.4 %collective-permute-start.2 = (f32[2,2,24,128]{3,2,1,0:T(8,128)S(1)}, f32[2,2,24,128]{3,2,1,0:T(8,128)S(1)}, u32[]{:S(2)}, u32[]{:S(2)}) collective-permute-start(f32[2,2,24,128]{3,2,1,0:T(8,128)S(1)} %get-tuple-element.23), channel_id=1, source_target_pairs={{0,24},{8,0},{16,8},{24,16},{1,25},{9,1},{17,9},{25,17},{2,26},{10... | collective-permute-start | bytes 147464 | tf_op jit(solution)/shard_map/ppermute | solution.py:222
  44.8 2.4 %collective-permute-start.1 = (f32[2,2,24,128]{3,2,1,0:T(8,128)S(1)}, f32[2,2,24,128]{3,2,1,0:T(8,128)S(1)}, u32[]{:S(2)}, u32[]{:S(2)}) collective-permute-start(f32[2,2,24,128]{3,2,1,0:T(8,128)S(1)} %get-tuple-element.24), channel_id=1, source_target_pairs={{0,16},{8,24},{16,0},{24,8},{1,17},{9,25},{17,1},{25,9},{2,18},{10... | collective-permute-start | bytes 147464 | tf_op jit(solution)/shard_map/ppermute | solution.py:222
  47.3 2.5 %collective-permute-start = (f32[2,2,24,128]{3,2,1,0:T(8,128)S(1)}, f32[2,2,24,128]{3,2,1,0:T(8,128)S(1)}, u32[]{:S(2)}, u32[]{:S(2)}) collective-permute-start(f32[2,2,24,128]{3,2,1,0:T(8,128)S(1)} %get-tuple-element.25), channel_id=1, source_target_pairs={{0,8},{8,16},{16,24},{24,0},{1,9},{9,17},{17,25},{25,1},{2,10},{10... | collective-permute-start | bytes 147464 | tf_op jit(solution)/shard_map/ppermute | solution.py:222
  49.8 0.0 collective-permute-done.2
  49.8 1.7 %collective-permute-done.1 = f32[2,2,24,128]{3,2,1,0:T(8,128)S(1)} collective-permute-done((f32[2,2,24,128]{3,2,1,0:T(8,128)S(1)}, f32[2,2,24,128]{3,2,1,0:T(8,128)S(1)}, u32[]{:S(2)}, u32[]{:S(2)}) %collective-permute-start.1) | collective-permute-done | bytes 49184 | tf_op jit(solution)/shard_map/ppermute | solution.py:222
  51.5 2.2 %collective-permute-done = f32[2,2,24,128]{3,2,1,0:T(8,128)S(1)} collective-permute-done((f32[2,2,24,128]{3,2,1,0:T(8,128)S(1)}, f32[2,2,24,128]{3,2,1,0:T(8,128)S(1)}, u32[]{:S(2)}, u32[]{:S(2)}) %collective-permute-start) | collective-permute-done | bytes 49184 | tf_op jit(solution)/shard_map/ppermute | solution.py:222
  53.6 1.8 %all-to-all-done.1.p0 = f32[8,2,2,24,128]{4,3,2,1,0:T(8,128)S(1)} async-done(((f32[8,2,2,24,128]{4,3,2,1,0:T(8,128)}), f32[8,2,2,24,128]{4,3,2,1,0:T(8,128)S(1)}, u32[]{:S(2)}, u32[]{:S(2)}) %all-to-all-start.1) | async-done | bytes 393248 | tf_op jit(solution)/shard_map/all_to_all | solution.py:230
  55.5 1.3 %broadcast_in_dim.2 = f32[8,4,2,2,24,128]{5,4,3,2,1,0:T(8,128)} broadcast(f32[4,2,2,24,128]{4,3,2,1,0:T(8,128)S(1)} %pad_maximum_fusion), dimensions={1,2,3,4,5} | broadcast | bytes 1769472 | tf_op jit(solution)/shard_map/broadcast_in_dim | solution.py:226
  56.9 4.8 %all-to-all-start.2 = ((f32[8,4,2,2,24,128]{5,4,3,2,1,0:T(8,128)}), f32[8,4,2,2,24,128]{5,4,3,2,1,0:T(8,128)S(1)}, u32[]{:S(2)}, u32[]{:S(2)}) async-start(f32[8,4,2,2,24,128]{5,4,3,2,1,0:T(8,128)} %broadcast_in_dim.2), calls=%async_computation.2 | async-start | bytes 3145728 | tf_op jit(solution)/shard_map/all_to_all | solution.py:230
  61.7 3.2 %collective-permute-start.5 = (f32[8,2,2,24,128]{4,3,2,1,0:T(8,128)S(1)}, f32[8,2,2,24,128]{4,3,2,1,0:T(8,128)S(1)}, u32[]{:S(2)}, u32[]{:S(2)}) collective-permute-start(f32[8,2,2,24,128]{4,3,2,1,0:T(8,128)S(1)} %all-to-all-done.1.p0), channel_id=1, source_target_pairs={{0,24},{8,0},{16,8},{24,16},{1,25},{9,1},{17,9},{25,17},{2,26},{10... | collective-permute-start | bytes 1179656 | tf_op jit(solution)/shard_map/ppermute | solution.py:222
  64.8 2.4 %collective-permute-start.4 = (f32[8,2,2,24,128]{4,3,2,1,0:T(8,128)S(1)}, f32[8,2,2,24,128]{4,3,2,1,0:T(8,128)S(1)}, u32[]{:S(2)}, u32[]{:S(2)}) collective-permute-start(f32[8,2,2,24,128]{4,3,2,1,0:T(8,128)S(1)} %all-to-all-done.1.p0), channel_id=1, source_target_pairs={{0,16},{8,24},{16,0},{24,8},{1,17},{9,25},{17,1},{25,9},{2,18},{10... | collective-permute-start | bytes 1179656 | tf_op jit(solution)/shard_map/ppermute | solution.py:222
  67.3 2.5 %collective-permute-start.3 = (f32[8,2,2,24,128]{4,3,2,1,0:T(8,128)S(1)}, f32[8,2,2,24,128]{4,3,2,1,0:T(8,128)S(1)}, u32[]{:S(2)}, u32[]{:S(2)}) collective-permute-start(f32[8,2,2,24,128]{4,3,2,1,0:T(8,128)S(1)} %all-to-all-done.1.p0), channel_id=1, source_target_pairs={{0,8},{8,16},{16,24},{24,0},{1,9},{9,17},{17,25},{25,1},{2,10},{10... | collective-permute-start | bytes 1179656 | tf_op jit(solution)/shard_map/ppermute | solution.py:222
  69.8 3.3 %collective-permute-done.5.p3 = f32[8,2,2,24,128]{4,3,2,1,0:T(8,128)S(1)} collective-permute-done((f32[8,2,2,24,128]{4,3,2,1,0:T(8,128)S(1)}, f32[8,2,2,24,128]{4,3,2,1,0:T(8,128)S(1)}, u32[]{:S(2)}, u32[]{:S(2)}) %collective-permute-start.5) | collective-permute-done | bytes 393248 | tf_op jit(solution)/shard_map/ppermute | solution.py:222
  73.1 4.3 %collective-permute-done.4.p2 = f32[8,2,2,24,128]{4,3,2,1,0:T(8,128)S(1)} collective-permute-done((f32[8,2,2,24,128]{4,3,2,1,0:T(8,128)S(1)}, f32[8,2,2,24,128]{4,3,2,1,0:T(8,128)S(1)}, u32[]{:S(2)}, u32[]{:S(2)}) %collective-permute-start.4) | collective-permute-done | bytes 393248 | tf_op jit(solution)/shard_map/ppermute | solution.py:222
  77.4 10.3 %collective-permute-done.3.p1 = f32[8,2,2,24,128]{4,3,2,1,0:T(8,128)S(1)} collective-permute-done((f32[8,2,2,24,128]{4,3,2,1,0:T(8,128)S(1)}, f32[8,2,2,24,128]{4,3,2,1,0:T(8,128)S(1)}, u32[]{:S(2)}, u32[]{:S(2)}) %collective-permute-start.3) | collective-permute-done | bytes 393248 | tf_op jit(solution)/shard_map/ppermute | solution.py:222
  87.7 4.6 %p_side.1.p_in = f32[2,4,128,3328]{3,2,1,0:T(8,128)} custom-call(s32[2]{0:T(128)S(1)} %pad_add_fusion.me, f32[8,2,2,24,128]{4,3,2,1,0:T(8,128)S(1)} %all-to-all-done.1.p0, f32[8,2,2,24,128]{4,3,2,1,0:T(8,128)S(1)} %collective-permute-done.3.p1, f32[8,2,2,24,128]{4,3,2,1,0:T(8,128)S(1)} %collective-permute-done.4.p2, ...), custom_call_target="tpu_custom_call" | custom-call | flops 1000000000 | bytes 20000000 | tf_op jit(solution)/shard_map/p_side/pallas_call | solution.py:251
  92.3 9.8 %all-to-all-done.2.q_in = f32[8,4,2,2,24,128]{5,4,3,2,1,0:T(8,128)S(1)} async-done(((f32[8,4,2,2,24,128]{5,4,3,2,1,0:T(8,128)}), f32[8,4,2,2,24,128]{5,4,3,2,1,0:T(8,128)S(1)}, u32[]{:S(2)}, u32[]{:S(2)}) %all-to-all-start.2) | async-done | bytes 1572896 | tf_op jit(solution)/shard_map/all_to_all | solution.py:230
  102.1 15.2 %correlate.1 = (f32[4,8,2,16,128]{4,3,2,1,0:T(8,128)S(1)}, f32[4,8,2,16,128]{4,3,2,1,0:T(8,128)S(1)}) custom-call(s32[2]{0:T(128)S(1)} %pad_add_fusion.me, f32[8,4,2,2,24,128]{5,4,3,2,1,0:T(8,128)S(1)} %all-to-all-done.2.q_in, f32[2,4,128,3328]{3,2,1,0:T(8,128)} %p_side.1.p_in), custom_call_target="tpu_custom_call" | custom-call | flops 10000000000 | bytes 20000000 | tf_op jit(solution)/shard_map/correlate/pallas_call | solution.py:267
  117.2 2.4 %collective-permute-start.6 = (f32[4,8,2,16,128]{4,3,2,1,0:T(8,128)S(1)}, f32[4,8,2,16,128]{4,3,2,1,0:T(8,128)S(1)}, u32[]{:S(2)}, u32[]{:S(2)}) collective-permute-start(f32[4,8,2,16,128]{4,3,2,1,0:T(8,128)S(1)} %get-tuple-element.22), channel_id=1, source_target_pairs={{0,1},{1,0},{2,3},{3,2},{4,5},{5,4},{6,7},{7,6},{8,9},{9,8},{10,11... | collective-permute-start | bytes 1572872 | tf_op jit(solution)/shard_map/ppermute | solution.py:288
  119.6 1.5 %collective-permute-done.6 = f32[4,8,2,16,128]{4,3,2,1,0:T(8,128)S(1)} collective-permute-done((f32[4,8,2,16,128]{4,3,2,1,0:T(8,128)S(1)}, f32[4,8,2,16,128]{4,3,2,1,0:T(8,128)S(1)}, u32[]{:S(2)}, u32[]{:S(2)}) %collective-permute-start.6) | collective-permute-done | bytes 524320 | tf_op jit(solution)/shard_map/ppermute | solution.py:288
  121.2 0.1 add.3
  121.2 11.1 %all_to_all.20.got = f32[4,8,2,16,128]{4,3,2,1,0:T(8,128)S(1)} all-to-all(f32[4,8,2,16,128]{4,3,2,1,0:T(8,128)S(1)} %add.3), channel_id=1, replica_groups=mesh['yh'=2,'z'=8,'x'=4,'yl'=4,'core'=2] {'x'}, dimensions={0} | all-to-all | bytes 1048576 | tf_op jit(solution)/shard_map/all_to_all | solution.py:289
  132.4 1.3 finish.1
  (2 shorter events, 0.0 us)
Async XLA Ops:
  0.0 0.9 copy-start
  1.9 24.1 %all-to-all-start = ((f32[8,24,768]{2,1,0:T(8,128)}), f32[8,24,768]{2,1,0:T(8,128)S(1)}, u32[]{:S(2)}, u32[]{:S(2)}) async-start(f32[8,24,768]{2,1,0:T(8,128)} %prepack.1), calls=%async_computation | async-start | bytes 1179648 | tf_op jit(solution)/shard_map/all_to_all | solution.py:237
  27.5 28.0 %all-to-all-start.1 = ((f32[8,2,2,24,128]{4,3,2,1,0:T(8,128)}), f32[8,2,2,24,128]{4,3,2,1,0:T(8,128)S(1)}, u32[]{:S(2)}, u32[]{:S(2)}) async-start(f32[8,2,2,24,128]{4,3,2,1,0:T(8,128)} %get-tuple-element.14), calls=%async_computation.1 | async-start | bytes 786432 | tf_op jit(solution)/shard_map/all_to_all | solution.py:230
  40.4 9.4 %collective-permute-start.2 = (f32[2,2,24,128]{3,2,1,0:T(8,128)S(1)}, f32[2,2,24,128]{3,2,1,0:T(8,128)S(1)}, u32[]{:S(2)}, u32[]{:S(2)}) collective-permute-start(f32[2,2,24,128]{3,2,1,0:T(8,128)S(1)} %get-tuple-element.23), channel_id=1, source_target_pairs={{0,24},{8,0},{16,8},{24,16},{1,25},{9,1},{17,9},{25,17},{2,26},{10... | collective-permute-start | bytes 147464 | tf_op jit(solution)/shard_map/ppermute | solution.py:222
  44.8 6.6 %collective-permute-start.1 = (f32[2,2,24,128]{3,2,1,0:T(8,128)S(1)}, f32[2,2,24,128]{3,2,1,0:T(8,128)S(1)}, u32[]{:S(2)}, u32[]{:S(2)}) collective-permute-start(f32[2,2,24,128]{3,2,1,0:T(8,128)S(1)} %get-tuple-element.24), channel_id=1, source_target_pairs={{0,16},{8,24},{16,0},{24,8},{1,17},{9,25},{17,1},{25,9},{2,18},{10... | collective-permute-start | bytes 147464 | tf_op jit(solution)/shard_map/ppermute | solution.py:222
  47.3 6.4 %collective-permute-start = (f32[2,2,24,128]{3,2,1,0:T(8,128)S(1)}, f32[2,2,24,128]{3,2,1,0:T(8,128)S(1)}, u32[]{:S(2)}, u32[]{:S(2)}) collective-permute-start(f32[2,2,24,128]{3,2,1,0:T(8,128)S(1)} %get-tuple-element.25), channel_id=1, source_target_pairs={{0,8},{8,16},{16,24},{24,0},{1,9},{9,17},{17,25},{25,1},{2,10},{10... | collective-permute-start | bytes 147464 | tf_op jit(solution)/shard_map/ppermute | solution.py:222
  56.9 45.2 %all-to-all-start.2 = ((f32[8,4,2,2,24,128]{5,4,3,2,1,0:T(8,128)}), f32[8,4,2,2,24,128]{5,4,3,2,1,0:T(8,128)S(1)}, u32[]{:S(2)}, u32[]{:S(2)}) async-start(f32[8,4,2,2,24,128]{5,4,3,2,1,0:T(8,128)} %broadcast_in_dim.2), calls=%async_computation.2 | async-start | bytes 3145728 | tf_op jit(solution)/shard_map/all_to_all | solution.py:230
  61.7 11.4 %collective-permute-start.5 = (f32[8,2,2,24,128]{4,3,2,1,0:T(8,128)S(1)}, f32[8,2,2,24,128]{4,3,2,1,0:T(8,128)S(1)}, u32[]{:S(2)}, u32[]{:S(2)}) collective-permute-start(f32[8,2,2,24,128]{4,3,2,1,0:T(8,128)S(1)} %all-to-all-done.1.p0), channel_id=1, source_target_pairs={{0,24},{8,0},{16,8},{24,16},{1,25},{9,1},{17,9},{25,17},{2,26},{10... | collective-permute-start | bytes 1179656 | tf_op jit(solution)/shard_map/ppermute | solution.py:222
  64.8 12.5 %collective-permute-start.4 = (f32[8,2,2,24,128]{4,3,2,1,0:T(8,128)S(1)}, f32[8,2,2,24,128]{4,3,2,1,0:T(8,128)S(1)}, u32[]{:S(2)}, u32[]{:S(2)}) collective-permute-start(f32[8,2,2,24,128]{4,3,2,1,0:T(8,128)S(1)} %all-to-all-done.1.p0), channel_id=1, source_target_pairs={{0,16},{8,24},{16,0},{24,8},{1,17},{9,25},{17,1},{25,9},{2,18},{10... | collective-permute-start | bytes 1179656 | tf_op jit(solution)/shard_map/ppermute | solution.py:222
  67.3 20.4 %collective-permute-start.3 = (f32[8,2,2,24,128]{4,3,2,1,0:T(8,128)S(1)}, f32[8,2,2,24,128]{4,3,2,1,0:T(8,128)S(1)}, u32[]{:S(2)}, u32[]{:S(2)}) collective-permute-start(f32[8,2,2,24,128]{4,3,2,1,0:T(8,128)S(1)} %all-to-all-done.1.p0), channel_id=1, source_target_pairs={{0,8},{8,16},{16,24},{24,0},{1,9},{9,17},{17,25},{25,1},{2,10},{10... | collective-permute-start | bytes 1179656 | tf_op jit(solution)/shard_map/ppermute | solution.py:222
  117.2 3.9 %collective-permute-start.6 = (f32[4,8,2,16,128]{4,3,2,1,0:T(8,128)S(1)}, f32[4,8,2,16,128]{4,3,2,1,0:T(8,128)S(1)}, u32[]{:S(2)}, u32[]{:S(2)}) collective-permute-start(f32[4,8,2,16,128]{4,3,2,1,0:T(8,128)S(1)} %get-tuple-element.22), channel_id=1, source_target_pairs={{0,1},{1,0},{2,3},{3,2},{4,5},{5,4},{6,7},{7,6},{8,9},{9,8},{10,11... | collective-permute-start | bytes 1572872 | tf_op jit(solution)/shard_map/ppermute | solution.py:288

commit v8 on v6

--- a/solution.py
+++ b/solution.py
@@ -193,16 +193,19 @@
     for g in range(8):
         for x in range(4):
             at = 64 * g + 16 * x
+            ahead = lax.rem(x + 4 - me[0], 4)
             for s2 in range(2):
                 a = acc[at : at + 16, 256 * s2 : 256 * s2 + 128]
                 b = acc[at : at + 16, 256 * s2 + 128 : 256 * s2 + 256]
                 one = jnp.where(low, a, pltpu.roll(b, 64, 1))
                 two = jnp.where(low, pltpu.roll(a, 64, 1), b)
-                keep[x, g, s2] = jnp.where(first, one, two)
-                send[x, g, s2] = jnp.where(first, two, one)
-
-
-def final_kernel(got, out):
+                keep[ahead, g, s2] = jnp.where(first, one, two)
+                send[ahead, g, s2] = jnp.where(first, two, one)
+
+
+def final_kernel(me, p0, p1, p2, p3, out, got):
+    for d, ref in enumerate((p0, p1, p2, p3)):
+        got[lax.rem(me[0] + 4 - d, 4)] = ref[...]
     lane = lanes((16, 128))
     for g in range(8):
         r, j = g // 2, g % 2
@@ -301,8 +304,16 @@
         name="correlate",
     )(me, q_all, p_done)
     summed = keep + lax.ppermute(send, "core", [(0, 1), (1, 0)])
-    mine = lax.all_to_all(summed, "x", 0, 0, tiled=True)
-    out = pl.pallas_call(final_kernel, out_shape=sds(LAGS, 16, 128), in_specs=[VMEM], out_specs=VMEM, compiler_params=SMALL, name="finish")(mine)
+    parts = [summed[0]] + [around(summed[d], d) for d in (1, 2, 3)]
+    out = pl.pallas_call(
+        final_kernel,
+        out_shape=sds(LAGS, 16, 128),
+        in_specs=[SMEM] + [VMEM] * 4,
+        out_specs=VMEM,
+        scratch_shapes=[pltpu.VMEM((4, 8, 2, 16, 128), jnp.float32)],
+        compiler_params=SMALL,
+        name="finish",
+    )(me, *parts)
     return jnp.transpose(out, (1, 0, 2))
 
 

time: 131 us -> 133 us (1.015)
  blocking collectives: 34.8 us -> 23.4 us
  starting transfers between devices: 40.8 us -> 48.6 us
  waiting for transfers between devices: 29.9 us -> 34.4 us
    all_to_all x1 -> x0, blocking collectives: 11.4 us -> none  [local(): mine = lax.all_to_all(summed, 'x', 0, 0, tiled=True)]
    ppermute x6 -> x9, starting transfers between devices: 17.1 us -> 25 us  [around(): return lax.ppermute(v, 'x', [(i, (i + d) % 4) for i in range(4)])]
    ppermute x6 -> x9, waiting for transfers between devices: 17.9 us -> 22.4 us  [around(): return lax.ppermute(v, 'x', [(i, (i + d) % 4) for i in range(4)])]
  transfers between devices with their start and end apart: 9 -> 12, of which waited for: 7 -> 9; matrix products, arithmetic and copies ran while one was open for 0% -> 0% of each run, Pallas kernels for 4% -> 4%
where the time goes in v8:
time: 133 us; the launch traced here: 132 us
  starting transfers between devices  48.6 us (37%)
  waiting for transfers between devices  34.4 us (26%)
  blocking collectives  23.4 us (18%)
  Pallas kernels  23.2 us (17%)
  local copies, waits for them, and re-layouts  2.28 us (2%)
    ppermute x9, starting transfers between devices, around(): return lax.ppermute(v, 'x', [(i, (i + d) % 4) for i in range(4)])  25 us
    all_to_all x1, blocking collectives, local(): got = lax.all_to_all(sent, ('yh', 'yl'), 0, 0, tiled=True)  23.4 us
    ppermute x9, waiting for transfers between devices, around(): return lax.ppermute(v, 'x', [(i, (i + d) % 4) for i in range(4)])  22.4 us
    all_to_all x2, starting transfers between devices, to_all(): return lax.all_to_all(v, 'z', 0, 0, tiled=True)  17.9 us
    pallas_call x1, Pallas kernels, local(): pl.pallas_call(correlate, out_shape=(sds(4, 8, 2, 16, 128),) * 2, in_spec...  15 us
    all_to_all x2, waiting for transfers between devices, to_all(): return lax.all_to_all(v, 'z', 0, 0, tiled=True)  10.5 us
    ppermute x1, starting transfers between devices, local(): summed = keep + lax.ppermute(send, 'core', [(0, 1), (1, 0)])  5.76 us
    pallas_call x1, Pallas kernels, local(): pl.pallas_call(p_side, out_shape=sds(2, 4, 128, SEQ), in_specs=[SMEM] + [...  4.69 us
  transfers between devices with their start and end apart: 12, of which 9 were waited for; matrix products, arithmetic and copies ran while one was open for 0% of the time, Pallas kernels for 4%

profile of v8, /device:TPU:1, one launch (start us, length us, event | category | flops | bytes accessed | tf_op | source)
XLA Modules:
  0.0 132.2 jit_solution(1193777924309414600)
XLA Ops:
  0.0 0.0 copy-start
  0.0 0.9 copy-done
  0.9 0.1 prepack.1
  1.0 23.4 %all_to_all.15.got = f32[8,24,768]{2,1,0:T(8,128)S(1)} all-to-all(f32[8,24,768]{2,1,0:T(8,128)S(1)} %prepack.1), channel_id=1, replica_groups=mesh['yh'=2,'z'=8,'x'=4,'yl'=4,'core'=2] {'yh','yl'}, dimensions={0} | all-to-all | bytes 1179648 | tf_op jit(solution)/shard_map/all_to_all | solution.py:246
  24.4 0.9 repack_p.1
  25.3 11.6 %all-to-all-start.1 = ((f32[8,2,2,24,128]{4,3,2,1,0:T(8,128)}), f32[8,2,2,24,128]{4,3,2,1,0:T(8,128)S(1)}, u32[]{:S(2)}, u32[]{:S(2)}) async-start(f32[8,2,2,24,128]{4,3,2,1,0:T(8,128)} %get-tuple-element.14), calls=%async_computation.1 | async-start | bytes 786432 | tf_op jit(solution)/shard_map/all_to_all | solution.py:239
  36.9 0.1 pad_add_fusion.me
  37.0 0.7 repack_q.1
  37.6 4.4 %collective-permute-start.2 = (f32[2,2,24,128]{3,2,1,0:T(8,128)S(1)}, f32[2,2,24,128]{3,2,1,0:T(8,128)S(1)}, u32[]{:S(2)}, u32[]{:S(2)}) collective-permute-start(f32[2,2,24,128]{3,2,1,0:T(8,128)S(1)} %get-tuple-element.27), channel_id=1, source_target_pairs={{0,24},{8,0},{16,8},{24,16},{1,25},{9,1},{17,9},{25,17},{2,26},{10... | collective-permute-start | bytes 147464 | tf_op jit(solution)/shard_map/ppermute | solution.py:231
  42.0 2.4 %collective-permute-start.1 = (f32[2,2,24,128]{3,2,1,0:T(8,128)S(1)}, f32[2,2,24,128]{3,2,1,0:T(8,128)S(1)}, u32[]{:S(2)}, u32[]{:S(2)}) collective-permute-start(f32[2,2,24,128]{3,2,1,0:T(8,128)S(1)} %get-tuple-element.28), channel_id=1, source_target_pairs={{0,16},{8,24},{16,0},{24,8},{1,17},{9,25},{17,1},{25,9},{2,18},{10... | collective-permute-start | bytes 147464 | tf_op jit(solution)/shard_map/ppermute | solution.py:231
  44.5 2.5 %collective-permute-start = (f32[2,2,24,128]{3,2,1,0:T(8,128)S(1)}, f32[2,2,24,128]{3,2,1,0:T(8,128)S(1)}, u32[]{:S(2)}, u32[]{:S(2)}) collective-permute-start(f32[2,2,24,128]{3,2,1,0:T(8,128)S(1)} %get-tuple-element.29), channel_id=1, source_target_pairs={{0,8},{8,16},{16,24},{24,0},{1,9},{9,17},{17,25},{25,1},{2,10},{10... | collective-permute-start | bytes 147464 | tf_op jit(solution)/shard_map/ppermute | solution.py:231
  47.0 0.0 collective-permute-done.2
  47.0 1.5 %collective-permute-done.1 = f32[2,2,24,128]{3,2,1,0:T(8,128)S(1)} collective-permute-done((f32[2,2,24,128]{3,2,1,0:T(8,128)S(1)}, f32[2,2,24,128]{3,2,1,0:T(8,128)S(1)}, u32[]{:S(2)}, u32[]{:S(2)}) %collective-permute-start.1) | collective-permute-done | bytes 49184 | tf_op jit(solution)/shard_map/ppermute | solution.py:231
  48.5 2.4 %collective-permute-done = f32[2,2,24,128]{3,2,1,0:T(8,128)S(1)} collective-permute-done((f32[2,2,24,128]{3,2,1,0:T(8,128)S(1)}, f32[2,2,24,128]{3,2,1,0:T(8,128)S(1)}, u32[]{:S(2)}, u32[]{:S(2)}) %collective-permute-start) | collective-permute-done | bytes 49184 | tf_op jit(solution)/shard_map/ppermute | solution.py:231
  50.8 0.0 all-to-all-done.1.p0
  50.8 1.3 %broadcast_in_dim.2 = f32[8,4,2,2,24,128]{5,4,3,2,1,0:T(8,128)} broadcast(f32[4,2,2,24,128]{4,3,2,1,0:T(8,128)S(1)} %pad_maximum_fusion), dimensions={1,2,3,4,5} | broadcast | bytes 1769472 | tf_op jit(solution)/shard_map/broadcast_in_dim | solution.py:235
  52.2 6.4 %all-to-all-start.2 = ((f32[8,4,2,2,24,128]{5,4,3,2,1,0:T(8,128)}), f32[8,4,2,2,24,128]{5,4,3,2,1,0:T(8,128)S(1)}, u32[]{:S(2)}, u32[]{:S(2)}) async-start(f32[8,4,2,2,24,128]{5,4,3,2,1,0:T(8,128)} %broadcast_in_dim.2), calls=%async_computation.2 | async-start | bytes 3145728 | tf_op jit(solution)/shard_map/all_to_all | solution.py:239
  58.5 2.0 %collective-permute-start.5 = (f32[8,2,2,24,128]{4,3,2,1,0:T(8,128)S(1)}, f32[8,2,2,24,128]{4,3,2,1,0:T(8,128)S(1)}, u32[]{:S(2)}, u32[]{:S(2)}) collective-permute-start(f32[8,2,2,24,128]{4,3,2,1,0:T(8,128)S(1)} %all-to-all-done.1.p0), channel_id=1, source_target_pairs={{0,24},{8,0},{16,8},{24,16},{1,25},{9,1},{17,9},{25,17},{2,26},{10... | collective-permute-start | bytes 1179656 | tf_op jit(solution)/shard_map/ppermute | solution.py:231
  60.5 3.1 %collective-permute-start.4 = (f32[8,2,2,24,128]{4,3,2,1,0:T(8,128)S(1)}, f32[8,2,2,24,128]{4,3,2,1,0:T(8,128)S(1)}, u32[]{:S(2)}, u32[]{:S(2)}) collective-permute-start(f32[8,2,2,24,128]{4,3,2,1,0:T(8,128)S(1)} %all-to-all-done.1.p0), channel_id=1, source_target_pairs={{0,16},{8,24},{16,0},{24,8},{1,17},{9,25},{17,1},{25,9},{2,18},{10... | collective-permute-start | bytes 1179656 | tf_op jit(solution)/shard_map/ppermute | solution.py:231
  63.6 2.8 %collective-permute-start.3 = (f32[8,2,2,24,128]{4,3,2,1,0:T(8,128)S(1)}, f32[8,2,2,24,128]{4,3,2,1,0:T(8,128)S(1)}, u32[]{:S(2)}, u32[]{:S(2)}) collective-permute-start(f32[8,2,2,24,128]{4,3,2,1,0:T(8,128)S(1)} %all-to-all-done.1.p0), channel_id=1, source_target_pairs={{0,8},{8,16},{16,24},{24,0},{1,9},{9,17},{17,25},{25,1},{2,10},{10... | collective-permute-start | bytes 1179656 | tf_op jit(solution)/shard_map/ppermute | solution.py:231
  66.4 1.0 collective-permute-done.5.p3
  67.3 3.5 %collective-permute-done.4.p2 = f32[8,2,2,24,128]{4,3,2,1,0:T(8,128)S(1)} collective-permute-done((f32[8,2,2,24,128]{4,3,2,1,0:T(8,128)S(1)}, f32[8,2,2,24,128]{4,3,2,1,0:T(8,128)S(1)}, u32[]{:S(2)}, u32[]{:S(2)}) %collective-permute-start.4) | collective-permute-done | bytes 393248 | tf_op jit(solution)/shard_map/ppermute | solution.py:231
  70.8 9.7 %collective-permute-done.3.p1 = f32[8,2,2,24,128]{4,3,2,1,0:T(8,128)S(1)} collective-permute-done((f32[8,2,2,24,128]{4,3,2,1,0:T(8,128)S(1)}, f32[8,2,2,24,128]{4,3,2,1,0:T(8,128)S(1)}, u32[]{:S(2)}, u32[]{:S(2)}) %collective-permute-start.3) | collective-permute-done | bytes 393248 | tf_op jit(solution)/shard_map/ppermute | solution.py:231
  80.5 4.7 %p_side.1.p_in = f32[2,4,128,3456]{3,2,1,0:T(8,128)} custom-call(s32[2]{0:T(128)S(1)} %pad_add_fusion.me, f32[8,2,2,24,128]{4,3,2,1,0:T(8,128)S(1)} %all-to-all-done.1.p0, f32[8,2,2,24,128]{4,3,2,1,0:T(8,128)S(1)} %collective-permute-done.3.p1, f32[8,2,2,24,128]{4,3,2,1,0:T(8,128)S(1)} %collective-permute-done.4.p2, ...), custom_call_target="tpu_custom_call" | custom-call | flops 1000000000 | bytes 20000000 | tf_op jit(solution)/shard_map/p_side/pallas_call | solution.py:269
  85.2 10.5 %all-to-all-done.2.q_in = f32[8,4,2,2,24,128]{5,4,3,2,1,0:T(8,128)S(1)} async-done(((f32[8,4,2,2,24,128]{5,4,3,2,1,0:T(8,128)}), f32[8,4,2,2,24,128]{5,4,3,2,1,0:T(8,128)S(1)}, u32[]{:S(2)}, u32[]{:S(2)}) %all-to-all-start.2) | async-done | bytes 1572896 | tf_op jit(solution)/shard_map/all_to_all | solution.py:239
  95.7 15.0 %correlate.1 = (f32[4,8,2,16,128]{4,3,2,1,0:T(8,128)S(1)}, f32[4,8,2,16,128]{4,3,2,1,0:T(8,128)S(1)}) custom-call(s32[2]{0:T(128)S(1)} %pad_add_fusion.me, f32[8,4,2,2,24,128]{5,4,3,2,1,0:T(8,128)S(1)} %all-to-all-done.2.q_in, f32[2,4,128,3456]{3,2,1,0:T(8,128)} %p_side.1.p_in), custom_call_target="tpu_custom_call" | custom-call | flops 10000000000 | bytes 20000000 | tf_op jit(solution)/shard_map/correlate/pallas_call | solution.py:285
  110.7 5.8 %collective-permute-start.6 = (f32[4,8,2,16,128]{4,3,2,1,0:T(8,128)S(1)}, f32[4,8,2,16,128]{4,3,2,1,0:T(8,128)S(1)}, u32[]{:S(2)}, u32[]{:S(2)}) collective-permute-start(f32[4,8,2,16,128]{4,3,2,1,0:T(8,128)S(1)} %get-tuple-element.22), channel_id=1, source_target_pairs={{0,1},{1,0},{2,3},{3,2},{4,5},{5,4},{6,7},{7,6},{8,9},{9,8},{10,11... | collective-permute-start | bytes 1572872 | tf_op jit(solution)/shard_map/ppermute | solution.py:306
  116.4 1.5 %collective-permute-done.6 = f32[4,8,2,16,128]{4,3,2,1,0:T(8,128)S(1)} collective-permute-done((f32[4,8,2,16,128]{4,3,2,1,0:T(8,128)S(1)}, f32[4,8,2,16,128]{4,3,2,1,0:T(8,128)S(1)}, u32[]{:S(2)}, u32[]{:S(2)}) %collective-permute-start.6) | collective-permute-done | bytes 524320 | tf_op jit(solution)/shard_map/ppermute | solution.py:306
  118.0 0.1 add.3
  118.1 1.9 %collective-permute-start.9 = (f32[8,2,16,128]{3,2,1,0:T(8,128)S(1)}, f32[8,2,16,128]{3,2,1,0:T(8,128)S(1)}, u32[]{:S(2)}, u32[]{:S(2)}) collective-permute-start(f32[8,2,16,128]{3,2,1,0:T(8,128)S(1)} %get-tuple-element.23), channel_id=1, source_target_pairs={{0,24},{8,0},{16,8},{24,16},{1,25},{9,1},{17,9},{25,17},{2,26},{10... | collective-permute-start | bytes 393224 | tf_op jit(solution)/shard_map/ppermute | solution.py:231
  120.0 3.1 %collective-permute-start.8 = (f32[8,2,16,128]{3,2,1,0:T(8,128)S(1)}, f32[8,2,16,128]{3,2,1,0:T(8,128)S(1)}, u32[]{:S(2)}, u32[]{:S(2)}) collective-permute-start(f32[8,2,16,128]{3,2,1,0:T(8,128)S(1)} %get-tuple-element.24), channel_id=1, source_target_pairs={{0,16},{8,24},{16,0},{24,8},{1,17},{9,25},{17,1},{25,9},{2,18},{10... | collective-permute-start | bytes 393224 | tf_op jit(solution)/shard_map/ppermute | solution.py:231
  123.2 2.8 %collective-permute-start.7 = (f32[8,2,16,128]{3,2,1,0:T(8,128)S(1)}, f32[8,2,16,128]{3,2,1,0:T(8,128)S(1)}, u32[]{:S(2)}, u32[]{:S(2)}) collective-permute-start(f32[8,2,16,128]{3,2,1,0:T(8,128)S(1)} %get-tuple-element.25), channel_id=1, source_target_pairs={{0,8},{8,16},{16,24},{24,0},{1,9},{9,17},{17,25},{25,1},{2,10},{10... | collective-permute-start | bytes 393224 | tf_op jit(solution)/shard_map/ppermute | solution.py:231
  125.9 0.0 collective-permute-done.9.p3
  125.9 1.9 %collective-permute-done.8.p2 = f32[8,2,16,128]{3,2,1,0:T(8,128)S(1)} collective-permute-done((f32[8,2,16,128]{3,2,1,0:T(8,128)S(1)}, f32[8,2,16,128]{3,2,1,0:T(8,128)S(1)}, u32[]{:S(2)}, u32[]{:S(2)}) %collective-permute-start.8) | collective-permute-done | bytes 131104 | tf_op jit(solution)/shard_map/ppermute | solution.py:231
  127.8 2.6 %collective-permute-done.7.p1 = f32[8,2,16,128]{3,2,1,0:T(8,128)S(1)} collective-permute-done((f32[8,2,16,128]{3,2,1,0:T(8,128)S(1)}, f32[8,2,16,128]{3,2,1,0:T(8,128)S(1)}, u32[]{:S(2)}, u32[]{:S(2)}) %collective-permute-start.7) | collective-permute-done | bytes 131104 | tf_op jit(solution)/shard_map/ppermute | solution.py:231
  130.4 1.8 %finish.1 = f32[63,16,128]{2,1,0:T(8,128)} custom-call(s32[2]{0:T(128)S(1)} %pad_add_fusion.me, f32[8,2,16,128]{3,2,1,0:T(8,128)S(1)} %get-tuple-element.26.p0, f32[8,2,16,128]{3,2,1,0:T(8,128)S(1)} %collective-permute-done.7.p1, f32[8,2,16,128]{3,2,1,0:T(8,128)S(1)} %collective-permute-done.8.p2, f32[8,2,16,128]{3,2,1,0:T(8,128)S(1)} %collective-permute-done.9.p3), custom_call_target="tpu_custom_call" | custom-call | tf_op jit(solution)/shard_map/finish/pallas_call | solution.py:308
  (3 shorter events, 0.1 us)
Async XLA Ops:
  0.0 0.9 copy-start
  25.3 25.5 %all-to-all-start.1 = ((f32[8,2,2,24,128]{4,3,2,1,0:T(8,128)}), f32[8,2,2,24,128]{4,3,2,1,0:T(8,128)S(1)}, u32[]{:S(2)}, u32[]{:S(2)}) async-start(f32[8,2,2,24,128]{4,3,2,1,0:T(8,128)} %get-tuple-element.14), calls=%async_computation.1 | async-start | bytes 786432 | tf_op jit(solution)/shard_map/all_to_all | solution.py:239
  37.6 9.4 %collective-permute-start.2 = (f32[2,2,24,128]{3,2,1,0:T(8,128)S(1)}, f32[2,2,24,128]{3,2,1,0:T(8,128)S(1)}, u32[]{:S(2)}, u32[]{:S(2)}) collective-permute-start(f32[2,2,24,128]{3,2,1,0:T(8,128)S(1)} %get-tuple-element.27), channel_id=1, source_target_pairs={{0,24},{8,0},{16,8},{24,16},{1,25},{9,1},{17,9},{25,17},{2,26},{10... | collective-permute-start | bytes 147464 | tf_op jit(solution)/shard_map/ppermute | solution.py:231
  42.0 6.4 %collective-permute-start.1 = (f32[2,2,24,128]{3,2,1,0:T(8,128)S(1)}, f32[2,2,24,128]{3,2,1,0:T(8,128)S(1)}, u32[]{:S(2)}, u32[]{:S(2)}) collective-permute-start(f32[2,2,24,128]{3,2,1,0:T(8,128)S(1)} %get-tuple-element.28), channel_id=1, source_target_pairs={{0,16},{8,24},{16,0},{24,8},{1,17},{9,25},{17,1},{25,9},{2,18},{10... | collective-permute-start | bytes 147464 | tf_op jit(solution)/shard_map/ppermute | solution.py:231
  44.5 6.3 %collective-permute-start = (f32[2,2,24,128]{3,2,1,0:T(8,128)S(1)}, f32[2,2,24,128]{3,2,1,0:T(8,128)S(1)}, u32[]{:S(2)}, u32[]{:S(2)}) collective-permute-start(f32[2,2,24,128]{3,2,1,0:T(8,128)S(1)} %get-tuple-element.29), channel_id=1, source_target_pairs={{0,8},{8,16},{16,24},{24,0},{1,9},{9,17},{17,25},{25,1},{2,10},{10... | collective-permute-start | bytes 147464 | tf_op jit(solution)/shard_map/ppermute | solution.py:231
  52.2 43.5 %all-to-all-start.2 = ((f32[8,4,2,2,24,128]{5,4,3,2,1,0:T(8,128)}), f32[8,4,2,2,24,128]{5,4,3,2,1,0:T(8,128)S(1)}, u32[]{:S(2)}, u32[]{:S(2)}) async-start(f32[8,4,2,2,24,128]{5,4,3,2,1,0:T(8,128)} %broadcast_in_dim.2), calls=%async_computation.2 | async-start | bytes 3145728 | tf_op jit(solution)/shard_map/all_to_all | solution.py:239
  58.5 8.8 %collective-permute-start.5 = (f32[8,2,2,24,128]{4,3,2,1,0:T(8,128)S(1)}, f32[8,2,2,24,128]{4,3,2,1,0:T(8,128)S(1)}, u32[]{:S(2)}, u32[]{:S(2)}) collective-permute-start(f32[8,2,2,24,128]{4,3,2,1,0:T(8,128)S(1)} %all-to-all-done.1.p0), channel_id=1, source_target_pairs={{0,24},{8,0},{16,8},{24,16},{1,25},{9,1},{17,9},{25,17},{2,26},{10... | collective-permute-start | bytes 1179656 | tf_op jit(solution)/shard_map/ppermute | solution.py:231
  60.5 10.3 %collective-permute-start.4 = (f32[8,2,2,24,128]{4,3,2,1,0:T(8,128)S(1)}, f32[8,2,2,24,128]{4,3,2,1,0:T(8,128)S(1)}, u32[]{:S(2)}, u32[]{:S(2)}) collective-permute-start(f32[8,2,2,24,128]{4,3,2,1,0:T(8,128)S(1)} %all-to-all-done.1.p0), channel_id=1, source_target_pairs={{0,16},{8,24},{16,0},{24,8},{1,17},{9,25},{17,1},{25,9},{2,18},{10... | collective-permute-start | bytes 1179656 | tf_op jit(solution)/shard_map/ppermute | solution.py:231
  63.6 16.9 %collective-permute-start.3 = (f32[8,2,2,24,128]{4,3,2,1,0:T(8,128)S(1)}, f32[8,2,2,24,128]{4,3,2,1,0:T(8,128)S(1)}, u32[]{:S(2)}, u32[]{:S(2)}) collective-permute-start(f32[8,2,2,24,128]{4,3,2,1,0:T(8,128)S(1)} %all-to-all-done.1.p0), channel_id=1, source_target_pairs={{0,8},{8,16},{16,24},{24,0},{1,9},{9,17},{17,25},{25,1},{2,10},{10... | collective-permute-start | bytes 1179656 | tf_op jit(solution)/shard_map/ppermute | solution.py:231
  110.7 7.3 %collective-permute-start.6 = (f32[4,8,2,16,128]{4,3,2,1,0:T(8,128)S(1)}, f32[4,8,2,16,128]{4,3,2,1,0:T(8,128)S(1)}, u32[]{:S(2)}, u32[]{:S(2)}) collective-permute-start(f32[4,8,2,16,128]{4,3,2,1,0:T(8,128)S(1)} %get-tuple-element.22), channel_id=1, source_target_pairs={{0,1},{1,0},{2,3},{3,2},{4,5},{5,4},{6,7},{7,6},{8,9},{9,8},{10,11... | collective-permute-start | bytes 1572872 | tf_op jit(solution)/shard_map/ppermute | solution.py:306
  118.1 7.8 %collective-permute-start.9 = (f32[8,2,16,128]{3,2,1,0:T(8,128)S(1)}, f32[8,2,16,128]{3,2,1,0:T(8,128)S(1)}, u32[]{:S(2)}, u32[]{:S(2)}) collective-permute-start(f32[8,2,16,128]{3,2,1,0:T(8,128)S(1)} %get-tuple-element.23), channel_id=1, source_target_pairs={{0,24},{8,0},{16,8},{24,16},{1,25},{9,1},{17,9},{25,17},{2,26},{10... | collective-permute-start | bytes 393224 | tf_op jit(solution)/shard_map/ppermute | solution.py:231
  120.0 7.8 %collective-permute-start.8 = (f32[8,2,16,128]{3,2,1,0:T(8,128)S(1)}, f32[8,2,16,128]{3,2,1,0:T(8,128)S(1)}, u32[]{:S(2)}, u32[]{:S(2)}) collective-permute-start(f32[8,2,16,128]{3,2,1,0:T(8,128)S(1)} %get-tuple-element.24), channel_id=1, source_target_pairs={{0,16},{8,24},{16,0},{24,8},{1,17},{9,25},{17,1},{25,9},{2,18},{10... | collective-permute-start | bytes 393224 | tf_op jit(solution)/shard_map/ppermute | solution.py:231
  123.2 7.3 %collective-permute-start.7 = (f32[8,2,16,128]{3,2,1,0:T(8,128)S(1)}, f32[8,2,16,128]{3,2,1,0:T(8,128)S(1)}, u32[]{:S(2)}, u32[]{:S(2)}) collective-permute-start(f32[8,2,16,128]{3,2,1,0:T(8,128)S(1)} %get-tuple-element.25), channel_id=1, source_target_pairs={{0,8},{8,16},{16,24},{24,0},{1,9},{9,17},{17,25},{25,1},{2,10},{10... | collective-permute-start | bytes 393224 | tf_op jit(solution)/shard_map/ppermute | solution.py:231

commit v9 on v7

--- a/solution.py
+++ b/solution.py
@@ -14,11 +14,11 @@
 
 TAU = 24
 ROW = SAMPLES + 32
-K = 3200
+K = 3328
 FRONT = 40
 QFRONT = FRONT - 24
 SEQ = K + 128
-CHUNKS = (1024, 1024, 1152)
+CHUNKS = (768, 768, 768, 1024)
 ROT = (4, 8, 36, 40)
 VMEM = pl.BlockSpec(memory_space=pltpu.VMEM)
 HBM = pl.BlockSpec(memory_space=pltpu.HBM)
@@ -56,14 +56,15 @@
     return jnp.where(low, a, pltpu.roll(b, 64, 1)), jnp.where(low, pltpu.roll(a, 64, 1), b)
 
 
-def repack(me, got, p_out, q_out):
+def repack(got, p_out, q_out):
+    me = lax.axis_index("x")
     for high in range(2):
         for pair in range(2):
             for v in range(4):
                 p_out[2 * v, pair, high], p_out[2 * v + 1, pair, high] = pairs(got, high, pair, 128 * v)
             for v in range(2):
                 for n, block in enumerate(pairs(got, high, pair, 512 + 128 * v)):
-                    q_out[lax.rem(2 * v + n + 4 - me[0], 4), pair, high] = block
+                    q_out[lax.rem(2 * v + n + 4 - me, 4), pair, high] = block
 
 
 def split(x):
@@ -238,11 +239,11 @@
     p_send, q_send = pl.pallas_call(
         repack,
         out_shape=(sds(8, 2, 2, TAU, 128), sds(4, 2, 2, TAU, 128)),
-        in_specs=[SMEM, VMEM],
+        in_specs=[VMEM],
         out_specs=(VMEM, VMEM),
         compiler_params=SMALL,
         name="repack",
-    )(me, got)
+    )(got)
     p_mine = to_all(p_send)
     q_mine = [q_send[0]] + [around(q_send[d], d) for d in (1, 2, 3)]
     p_mine, *q_mine = lax.optimization_barrier((p_mine, *q_mine))

time: 134 us -> 130 us (0.970)
  blocking collectives: 11.1 us -> 34.7 us
  waiting for transfers between devices: 51.3 us -> 29.5 us
  starting transfers between devices: 45.2 us -> 41.1 us
  Pallas kernels: 23.5 us -> 22.1 us
    all_to_all x0 -> x1, blocking collectives: none -> 23.4 us  [local(): got = lax.all_to_all(sent, ('yh', 'yl'), 0, 0, tiled=True)]
    all_to_all x1 -> x0, waiting for transfers between devices: 16.4 us -> none  [local(): got = lax.all_to_all(sent, ('yh', 'yl'), 0, 0, tiled=True)]
    all_to_all x1 -> x0, starting transfers between devices: 7.65 us -> none  [local(): got = lax.all_to_all(sent, ('yh', 'yl'), 0, 0, tiled=True)]
    ppermute x6, waiting for transfers between devices: 21.8 us -> 17.6 us  [around(): return lax.ppermute(v, 'x', [(i, (i + d) % 4) for i in range(4)])]
    ppermute x1, starting transfers between devices: 2.39 us -> 5.74 us  [local(): summed = keep + lax.ppermute(send, 'core', [(0, 1), (1, 0)])]
  transfers between devices with their start and end apart: 10 -> 9, of which waited for: 9 -> 7; matrix products, arithmetic and copies ran while one was open for 0% -> 0% of each run, Pallas kernels for 3% -> 4%
where the time goes in v9:
time: 130 us
  starting transfers between devices  41.1 us (32%)
  blocking collectives  34.7 us (27%)
  waiting for transfers between devices  29.5 us (23%)
  Pallas kernels  22.1 us (17%)
  local copies, waits for them, and re-layouts  2.23 us (2%)
    all_to_all x1, blocking collectives, local(): got = lax.all_to_all(sent, ('yh', 'yl'), 0, 0, tiled=True)  23.4 us
    all_to_all x2, starting transfers between devices, to_all(): return lax.all_to_all(v, 'z', 0, 0, tiled=True)  18.2 us
    ppermute x6, waiting for transfers between devices, around(): return lax.ppermute(v, 'x', [(i, (i + d) % 4) for i in range(4)])  17.6 us
    ppermute x6, starting transfers between devices, around(): return lax.ppermute(v, 'x', [(i, (i + d) % 4) for i in range(4)])  17.1 us
    pallas_call x1, Pallas kernels, local(): pl.pallas_call(correlate, out_shape=(sds(4, 8, 2, 16, 128),) * 2, in_spec...  15 us
    all_to_all x1, blocking collectives, local(): mine = lax.all_to_all(summed, 'x', 0, 0, tiled=True)  11.4 us
    all_to_all x2, waiting for transfers between devices, to_all(): return lax.all_to_all(v, 'z', 0, 0, tiled=True)  10.5 us
    ppermute x1, starting transfers between devices, local(): summed = keep + lax.ppermute(send, 'core', [(0, 1), (1, 0)])  5.74 us
  transfers between devices with their start and end apart: 9, of which 7 were waited for; matrix products, arithmetic and copies ran while one was open for 0% of the time, Pallas kernels for 4%

profile of v9, /device:TPU:1, one launch (start us, length us, event | category | flops | bytes accessed | tf_op | source)
XLA Modules:
  0.0 130.0 jit_solution(6052880122364086933)
XLA Ops:
  0.0 0.0 copy-start
  0.0 0.9 copy-done
  0.9 0.1 prepack.1
  1.0 23.4 %all_to_all.20.got = f32[8,24,768]{2,1,0:T(8,128)S(1)} all-to-all(f32[8,24,768]{2,1,0:T(8,128)S(1)} %prepack.1), channel_id=1, replica_groups=mesh['yh'=2,'z'=8,'x'=4,'yl'=4,'core'=2] {'yh','yl'}, dimensions={0} | all-to-all | bytes 1179648 | tf_op jit(solution)/shard_map/all_to_all | solution.py:238
  24.4 1.0 repack.1
  25.4 11.6 %all-to-all-start.1 = ((f32[8,2,2,24,128]{4,3,2,1,0:T(8,128)}), f32[8,2,2,24,128]{4,3,2,1,0:T(8,128)S(1)}, u32[]{:S(2)}, u32[]{:S(2)}) async-start(f32[8,2,2,24,128]{4,3,2,1,0:T(8,128)} %get-tuple-element.14), calls=%async_computation.1 | async-start | bytes 786432 | tf_op jit(solution)/shard_map/all_to_all | solution.py:231
  36.9 4.4 %collective-permute-start.2 = (f32[2,2,24,128]{3,2,1,0:T(8,128)S(1)}, f32[2,2,24,128]{3,2,1,0:T(8,128)S(1)}, u32[]{:S(2)}, u32[]{:S(2)}) collective-permute-start(f32[2,2,24,128]{3,2,1,0:T(8,128)S(1)} %get-tuple-element.23), channel_id=1, source_target_pairs={{0,24},{8,0},{16,8},{24,16},{1,25},{9,1},{17,9},{25,17},{2,26},{10... | collective-permute-start | bytes 147464 | tf_op jit(solution)/shard_map/ppermute | solution.py:223
  41.3 2.4 %collective-permute-start.1 = (f32[2,2,24,128]{3,2,1,0:T(8,128)S(1)}, f32[2,2,24,128]{3,2,1,0:T(8,128)S(1)}, u32[]{:S(2)}, u32[]{:S(2)}) collective-permute-start(f32[2,2,24,128]{3,2,1,0:T(8,128)S(1)} %get-tuple-element.24), channel_id=1, source_target_pairs={{0,16},{8,24},{16,0},{24,8},{1,17},{9,25},{17,1},{25,9},{2,18},{10... | collective-permute-start | bytes 147464 | tf_op jit(solution)/shard_map/ppermute | solution.py:223
  43.8 2.5 %collective-permute-start = (f32[2,2,24,128]{3,2,1,0:T(8,128)S(1)}, f32[2,2,24,128]{3,2,1,0:T(8,128)S(1)}, u32[]{:S(2)}, u32[]{:S(2)}) collective-permute-start(f32[2,2,24,128]{3,2,1,0:T(8,128)S(1)} %get-tuple-element.25), channel_id=1, source_target_pairs={{0,8},{8,16},{16,24},{24,0},{1,9},{9,17},{17,25},{25,1},{2,10},{10... | collective-permute-start | bytes 147464 | tf_op jit(solution)/shard_map/ppermute | solution.py:223
  46.3 0.0 collective-permute-done.2
  46.3 1.7 %collective-permute-done.1 = f32[2,2,24,128]{3,2,1,0:T(8,128)S(1)} collective-permute-done((f32[2,2,24,128]{3,2,1,0:T(8,128)S(1)}, f32[2,2,24,128]{3,2,1,0:T(8,128)S(1)}, u32[]{:S(2)}, u32[]{:S(2)}) %collective-permute-start.1) | collective-permute-done | bytes 49184 | tf_op jit(solution)/shard_map/ppermute | solution.py:223
  48.0 1.8 %collective-permute-done = f32[2,2,24,128]{3,2,1,0:T(8,128)S(1)} collective-permute-done((f32[2,2,24,128]{3,2,1,0:T(8,128)S(1)}, f32[2,2,24,128]{3,2,1,0:T(8,128)S(1)}, u32[]{:S(2)}, u32[]{:S(2)}) %collective-permute-start) | collective-permute-done | bytes 49184 | tf_op jit(solution)/shard_map/ppermute | solution.py:223
  49.8 0.0 all-to-all-done.1.p0
  49.8 1.3 %broadcast_in_dim.2 = f32[8,4,2,2,24,128]{5,4,3,2,1,0:T(8,128)} broadcast(f32[4,2,2,24,128]{4,3,2,1,0:T(8,128)S(1)} %pad_maximum_fusion), dimensions={1,2,3,4,5} | broadcast | bytes 1769472 | tf_op jit(solution)/shard_map/broadcast_in_dim | solution.py:227
  51.2 6.6 %all-to-all-start.2 = ((f32[8,4,2,2,24,128]{5,4,3,2,1,0:T(8,128)}), f32[8,4,2,2,24,128]{5,4,3,2,1,0:T(8,128)S(1)}, u32[]{:S(2)}, u32[]{:S(2)}) async-start(f32[8,4,2,2,24,128]{5,4,3,2,1,0:T(8,128)} %broadcast_in_dim.2), calls=%async_computation.2 | async-start | bytes 3145728 | tf_op jit(solution)/shard_map/all_to_all | solution.py:231
  57.8 2.0 %collective-permute-start.5 = (f32[8,2,2,24,128]{4,3,2,1,0:T(8,128)S(1)}, f32[8,2,2,24,128]{4,3,2,1,0:T(8,128)S(1)}, u32[]{:S(2)}, u32[]{:S(2)}) collective-permute-start(f32[8,2,2,24,128]{4,3,2,1,0:T(8,128)S(1)} %all-to-all-done.1.p0), channel_id=1, source_target_pairs={{0,24},{8,0},{16,8},{24,16},{1,25},{9,1},{17,9},{25,17},{2,26},{10... | collective-permute-start | bytes 1179656 | tf_op jit(solution)/shard_map/ppermute | solution.py:223
  59.8 3.1 %collective-permute-start.4 = (f32[8,2,2,24,128]{4,3,2,1,0:T(8,128)S(1)}, f32[8,2,2,24,128]{4,3,2,1,0:T(8,128)S(1)}, u32[]{:S(2)}, u32[]{:S(2)}) collective-permute-start(f32[8,2,2,24,128]{4,3,2,1,0:T(8,128)S(1)} %all-to-all-done.1.p0), channel_id=1, source_target_pairs={{0,16},{8,24},{16,0},{24,8},{1,17},{9,25},{17,1},{25,9},{2,18},{10... | collective-permute-start | bytes 1179656 | tf_op jit(solution)/shard_map/ppermute | solution.py:223
  62.9 2.8 %collective-permute-start.3 = (f32[8,2,2,24,128]{4,3,2,1,0:T(8,128)S(1)}, f32[8,2,2,24,128]{4,3,2,1,0:T(8,128)S(1)}, u32[]{:S(2)}, u32[]{:S(2)}) collective-permute-start(f32[8,2,2,24,128]{4,3,2,1,0:T(8,128)S(1)} %all-to-all-done.1.p0), channel_id=1, source_target_pairs={{0,8},{8,16},{16,24},{24,0},{1,9},{9,17},{17,25},{25,1},{2,10},{10... | collective-permute-start | bytes 1179656 | tf_op jit(solution)/shard_map/ppermute | solution.py:223
  65.7 0.1 pad_add_fusion.me
  65.7 0.9 collective-permute-done.5.p3
  66.6 3.5 %collective-permute-done.4.p2 = f32[8,2,2,24,128]{4,3,2,1,0:T(8,128)S(1)} collective-permute-done((f32[8,2,2,24,128]{4,3,2,1,0:T(8,128)S(1)}, f32[8,2,2,24,128]{4,3,2,1,0:T(8,128)S(1)}, u32[]{:S(2)}, u32[]{:S(2)}) %collective-permute-start.4) | collective-permute-done | bytes 393248 | tf_op jit(solution)/shard_map/ppermute | solution.py:223
  70.1 9.7 %collective-permute-done.3.p1 = f32[8,2,2,24,128]{4,3,2,1,0:T(8,128)S(1)} collective-permute-done((f32[8,2,2,24,128]{4,3,2,1,0:T(8,128)S(1)}, f32[8,2,2,24,128]{4,3,2,1,0:T(8,128)S(1)}, u32[]{:S(2)}, u32[]{:S(2)}) %collective-permute-start.3) | collective-permute-done | bytes 393248 | tf_op jit(solution)/shard_map/ppermute | solution.py:223
  79.8 4.7 %p_side.1.p_in = f32[2,4,128,3456]{3,2,1,0:T(8,128)} custom-call(s32[2]{0:T(128)S(1)} %pad_add_fusion.me, f32[8,2,2,24,128]{4,3,2,1,0:T(8,128)S(1)} %all-to-all-done.1.p0, f32[8,2,2,24,128]{4,3,2,1,0:T(8,128)S(1)} %collective-permute-done.3.p1, f32[8,2,2,24,128]{4,3,2,1,0:T(8,128)S(1)} %collective-permute-done.4.p2, ...), custom_call_target="tpu_custom_call" | custom-call | flops 1000000000 | bytes 20000000 | tf_op jit(solution)/shard_map/p_side/pallas_call | solution.py:252
  84.5 10.4 %all-to-all-done.2.q_in = f32[8,4,2,2,24,128]{5,4,3,2,1,0:T(8,128)S(1)} async-done(((f32[8,4,2,2,24,128]{5,4,3,2,1,0:T(8,128)}), f32[8,4,2,2,24,128]{5,4,3,2,1,0:T(8,128)S(1)}, u32[]{:S(2)}, u32[]{:S(2)}) %all-to-all-start.2) | async-done | bytes 1572896 | tf_op jit(solution)/shard_map/all_to_all | solution.py:231
  94.9 15.0 %correlate.1 = (f32[4,8,2,16,128]{4,3,2,1,0:T(8,128)S(1)}, f32[4,8,2,16,128]{4,3,2,1,0:T(8,128)S(1)}) custom-call(s32[2]{0:T(128)S(1)} %pad_add_fusion.me, f32[8,4,2,2,24,128]{5,4,3,2,1,0:T(8,128)S(1)} %all-to-all-done.2.q_in, f32[2,4,128,3456]{3,2,1,0:T(8,128)} %p_side.1.p_in), custom_call_target="tpu_custom_call" | custom-call | flops 10000000000 | bytes 20000000 | tf_op jit(solution)/shard_map/correlate/pallas_call | solution.py:268
  110.0 5.7 %collective-permute-start.6 = (f32[4,8,2,16,128]{4,3,2,1,0:T(8,128)S(1)}, f32[4,8,2,16,128]{4,3,2,1,0:T(8,128)S(1)}, u32[]{:S(2)}, u32[]{:S(2)}) collective-permute-start(f32[4,8,2,16,128]{4,3,2,1,0:T(8,128)S(1)} %get-tuple-element.22), channel_id=1, source_target_pairs={{0,1},{1,0},{2,3},{3,2},{4,5},{5,4},{6,7},{7,6},{8,9},{9,8},{10,11... | collective-permute-start | bytes 1572872 | tf_op jit(solution)/shard_map/ppermute | solution.py:289
  115.7 1.5 %collective-permute-done.6 = f32[4,8,2,16,128]{4,3,2,1,0:T(8,128)S(1)} collective-permute-done((f32[4,8,2,16,128]{4,3,2,1,0:T(8,128)S(1)}, f32[4,8,2,16,128]{4,3,2,1,0:T(8,128)S(1)}, u32[]{:S(2)}, u32[]{:S(2)}) %collective-permute-start.6) | collective-permute-done | bytes 524320 | tf_op jit(solution)/shard_map/ppermute | solution.py:289
  117.2 0.1 add.3
  117.3 11.4 %all_to_all.21.got = f32[4,8,2,16,128]{4,3,2,1,0:T(8,128)S(1)} all-to-all(f32[4,8,2,16,128]{4,3,2,1,0:T(8,128)S(1)} %add.3), channel_id=1, replica_groups=mesh['yh'=2,'z'=8,'x'=4,'yl'=4,'core'=2] {'x'}, dimensions={0} | all-to-all | bytes 1048576 | tf_op jit(solution)/shard_map/all_to_all | solution.py:290
  128.7 1.3 finish.1
  (2 shorter events, 0.0 us)
Async XLA Ops:
  0.0 0.9 copy-start
  25.4 24.5 %all-to-all-start.1 = ((f32[8,2,2,24,128]{4,3,2,1,0:T(8,128)}), f32[8,2,2,24,128]{4,3,2,1,0:T(8,128)S(1)}, u32[]{:S(2)}, u32[]{:S(2)}) async-start(f32[8,2,2,24,128]{4,3,2,1,0:T(8,128)} %get-tuple-element.14), calls=%async_computation.1 | async-start | bytes 786432 | tf_op jit(solution)/shard_map/all_to_all | solution.py:231
  36.9 9.4 %collective-permute-start.2 = (f32[2,2,24,128]{3,2,1,0:T(8,128)S(1)}, f32[2,2,24,128]{3,2,1,0:T(8,128)S(1)}, u32[]{:S(2)}, u32[]{:S(2)}) collective-permute-start(f32[2,2,24,128]{3,2,1,0:T(8,128)S(1)} %get-tuple-element.23), channel_id=1, source_target_pairs={{0,24},{8,0},{16,8},{24,16},{1,25},{9,1},{17,9},{25,17},{2,26},{10... | collective-permute-start | bytes 147464 | tf_op jit(solution)/shard_map/ppermute | solution.py:223
  41.3 6.6 %collective-permute-start.1 = (f32[2,2,24,128]{3,2,1,0:T(8,128)S(1)}, f32[2,2,24,128]{3,2,1,0:T(8,128)S(1)}, u32[]{:S(2)}, u32[]{:S(2)}) collective-permute-start(f32[2,2,24,128]{3,2,1,0:T(8,128)S(1)} %get-tuple-element.24), channel_id=1, source_target_pairs={{0,16},{8,24},{16,0},{24,8},{1,17},{9,25},{17,1},{25,9},{2,18},{10... | collective-permute-start | bytes 147464 | tf_op jit(solution)/shard_map/ppermute | solution.py:223
  43.8 6.0 %collective-permute-start = (f32[2,2,24,128]{3,2,1,0:T(8,128)S(1)}, f32[2,2,24,128]{3,2,1,0:T(8,128)S(1)}, u32[]{:S(2)}, u32[]{:S(2)}) collective-permute-start(f32[2,2,24,128]{3,2,1,0:T(8,128)S(1)} %get-tuple-element.25), channel_id=1, source_target_pairs={{0,8},{8,16},{16,24},{24,0},{1,9},{9,17},{17,25},{25,1},{2,10},{10... | collective-permute-start | bytes 147464 | tf_op jit(solution)/shard_map/ppermute | solution.py:223
  51.2 43.8 %all-to-all-start.2 = ((f32[8,4,2,2,24,128]{5,4,3,2,1,0:T(8,128)}), f32[8,4,2,2,24,128]{5,4,3,2,1,0:T(8,128)S(1)}, u32[]{:S(2)}, u32[]{:S(2)}) async-start(f32[8,4,2,2,24,128]{5,4,3,2,1,0:T(8,128)} %broadcast_in_dim.2), calls=%async_computation.2 | async-start | bytes 3145728 | tf_op jit(solution)/shard_map/all_to_all | solution.py:231
  57.8 8.8 %collective-permute-start.5 = (f32[8,2,2,24,128]{4,3,2,1,0:T(8,128)S(1)}, f32[8,2,2,24,128]{4,3,2,1,0:T(8,128)S(1)}, u32[]{:S(2)}, u32[]{:S(2)}) collective-permute-start(f32[8,2,2,24,128]{4,3,2,1,0:T(8,128)S(1)} %all-to-all-done.1.p0), channel_id=1, source_target_pairs={{0,24},{8,0},{16,8},{24,16},{1,25},{9,1},{17,9},{25,17},{2,26},{10... | collective-permute-start | bytes 1179656 | tf_op jit(solution)/shard_map/ppermute | solution.py:223
  59.8 10.3 %collective-permute-start.4 = (f32[8,2,2,24,128]{4,3,2,1,0:T(8,128)S(1)}, f32[8,2,2,24,128]{4,3,2,1,0:T(8,128)S(1)}, u32[]{:S(2)}, u32[]{:S(2)}) collective-permute-start(f32[8,2,2,24,128]{4,3,2,1,0:T(8,128)S(1)} %all-to-all-done.1.p0), channel_id=1, source_target_pairs={{0,16},{8,24},{16,0},{24,8},{1,17},{9,25},{17,1},{25,9},{2,18},{10... | collective-permute-start | bytes 1179656 | tf_op jit(solution)/shard_map/ppermute | solution.py:223
  62.9 16.9 %collective-permute-start.3 = (f32[8,2,2,24,128]{4,3,2,1,0:T(8,128)S(1)}, f32[8,2,2,24,128]{4,3,2,1,0:T(8,128)S(1)}, u32[]{:S(2)}, u32[]{:S(2)}) collective-permute-start(f32[8,2,2,24,128]{4,3,2,1,0:T(8,128)S(1)} %all-to-all-done.1.p0), channel_id=1, source_target_pairs={{0,8},{8,16},{16,24},{24,0},{1,9},{9,17},{17,25},{25,1},{2,10},{10... | collective-permute-start | bytes 1179656 | tf_op jit(solution)/shard_map/ppermute | solution.py:223
  110.0 7.3 %collective-permute-start.6 = (f32[4,8,2,16,128]{4,3,2,1,0:T(8,128)S(1)}, f32[4,8,2,16,128]{4,3,2,1,0:T(8,128)S(1)}, u32[]{:S(2)}, u32[]{:S(2)}) collective-permute-start(f32[4,8,2,16,128]{4,3,2,1,0:T(8,128)S(1)} %get-tuple-element.22), channel_id=1, source_target_pairs={{0,1},{1,0},{2,3},{3,2},{4,5},{5,4},{6,7},{7,6},{8,9},{9,8},{10,11... | collective-permute-start | bytes 1572872 | tf_op jit(solution)/shard_map/ppermute | solution.py:289
